TPU v7x, 32 devices: a whole 2x2x4 slice. The times are simulated.
32 devices in a mesh: group: 4 (over y, x), expert: 8 (over z, core).
Axes of the slice: x: 2, y: 2, z: 4, core: 2. Of those that a mesh axis runs over, the one named last changes fastest.
Arguments:
- tokens: bfloat16 [32768, 768], P(('group', 'expert')), may hold values from -6 to 6
- cotangent: bfloat16 [32768, 768], P(('group', 'expert')), may hold values from -6 to 6
- norm_attn: bfloat16 [768], P('expert'), may hold values from 0.5 to 1.5
- w_query: bfloat16 [768, 768], P('expert'), may hold values from -0.21875 to 0.21875
- w_key: bfloat16 [768, 768], P('expert'), may hold values from -0.21875 to 0.21875
- w_value: bfloat16 [768, 768], P('expert'), may hold values from -0.21875 to 0.21875
- w_out: bfloat16 [768, 768], P('expert'), may hold values from -0.875 to 0.875
- rel_bias: bfloat16 [384], P('expert'), may hold values from -4 to 4
- norm_expert: bfloat16 [768], P('expert'), may hold values from 0.5 to 1.5
- w_router: bfloat16 [768, 8], P('expert'), may hold values from -0.14941406 to 0.14941406
- expert_in: bfloat16 [8, 768, 3072], P('expert'), may hold values from -0.21875 to 0.21875
- expert_out: bfloat16 [8, 3072, 768], P('expert'), may hold values from -0.109375 to 0.109375
- expert_ids: int32 [32768, 2], P(('group', 'expert')), may hold values from 0 to 7, all different within a row; in each aligned block of 512 rows (0 to 511, 512 to 1023, ...) at most 192 rows name the same one
- span_starts: int32 [64], P(('group', 'expert')), may hold values from 0 to 256
Outputs:
- mixed: bfloat16 [32768, 768], P(('group', 'expert'))
- grad_tokens: bfloat16 [32768, 768], P(('group', 'expert'))
- grad_norm_attn: float32 [768], P('expert')
- grad_w_query: float32 [768, 768], P('expert')
- grad_w_key: float32 [768, 768], P('expert')
- grad_w_value: float32 [768, 768], P('expert')
- grad_w_out: float32 [768, 768], P('expert')
- grad_rel_bias: float32 [384], P('expert')
- grad_norm_expert: float32 [768], P('expert')
- grad_w_router: float32 [768, 8], P('expert')
- grad_expert_in: float32 [8, 768, 3072], P('expert')
- grad_expert_out: float32 [8, 3072, 768], P('expert')
Inputs may be any that keep to these rules, and one draw needn't show every extreme that they name: `expert_ids`: in each aligned block of 512 rows no expert is named by more than 192 rows, a bound that some block reaches; the 2 experts of a row differ.
All inputs are finite; a program needn't handle non-finite values.
Results may differ from a plain program's by a relative error of at most 0.015.
Values may be sent and summed in bfloat16 or wider, within the bound.
No kernel may reach another device: no remote copies, remote signals or barrier semaphores. Data moves between devices by JAX's collectives and lax.ppermute only.
A program may use at most 256 MiB of HBM per device.

v0:
```python
import jax
import jax.numpy as jnp
from jax import lax
from jax.sharding import PartitionSpec as P

D = 768
HEADS = 12
HEAD_DIM = 64
FF = 3072
TOP = 2
BUCKETS = 32
SEQ_LEN = 512
PIC = 256
MICRO = 2
SEQ_MB = 1
TOK_MB = 512


epsilon = 1e-06
bucket_edges = (1, 2, 3, 4, 5, 6, 7, 8, 12, 16, 23, 32, 45, 64, 91)


def bucket_index(offset):
    magnitude = jnp.zeros(offset.shape, jnp.int32)
    for edge in bucket_edges:
        magnitude = magnitude + (jnp.abs(offset) >= edge).astype(jnp.int32)
    return magnitude + 16 * (offset > 0).astype(jnp.int32)


def allowed_mask(start):
    places = jnp.arange(SEQ_LEN, dtype=jnp.int32)
    causal = places[None, :] <= places[:, None]
    inside = (places >= start) & (places < start + PIC)
    return causal | inside[:, None] & inside[None, :]


def gelu_tanh(inner):
    return jax.nn.gelu(inner, approximate=True)


def norm_forward(values):
    scaler = lax.rsqrt(jnp.mean(values * values, axis=-1, keepdims=True) + epsilon)
    return (values * scaler, scaler)


def norm_backward(grad_normed, normal, scaler, gain):
    grad_scaled = grad_normed * gain
    grad_values = scaler * (
        grad_scaled - normal * jnp.mean(grad_scaled * normal, axis=-1, keepdims=True)
    )
    return (grad_values, jnp.sum(grad_normed * normal, axis=0))


def matmul_tn(left, right):
    return jnp.einsum("td,te->de", left, right, preferred_element_type=jnp.float32)


def matmul_nt(left, right):
    return jnp.einsum("te,de->td", left, right, preferred_element_type=jnp.float32)


def plain_dot(left, right):
    return jnp.dot(left, right, preferred_element_type=jnp.float32)


def add_trees(first, second):
    return jax.tree.map(jnp.add, first, second)


def shards(
    tokens,
    cotangent,
    norm_attn,
    w_query,
    w_key,
    w_value,
    w_out,
    rel_bias,
    norm_expert,
    w_router,
    expert_in,
    expert_out,
    expert_ids,
    span_starts,
):
    experts = w_router.shape[1]
    capacity = 3 * TOK_MB * TOP // (2 * experts)
    local_experts = expert_in.shape[0]
    senders = experts // local_experts
    scale_head = HEAD_DIM ** (-0.5)
    places = jnp.arange(SEQ_LEN, dtype=jnp.int32)
    bucket_flat = bucket_index(places[None, :] - places[:, None]).reshape(1, -1)
    bucket_hot = (bucket_flat == jnp.arange(BUCKETS, dtype=jnp.int32)[:, None]).astype(jnp.bfloat16)
    slot_iota = jnp.arange(experts * capacity, dtype=jnp.int32)
    expert_iota = jnp.arange(experts, dtype=jnp.int32)
    grad_inner_sum = jnp.zeros(expert_in.shape, jnp.float32)
    grad_outer_sum = jnp.zeros(expert_out.shape, jnp.float32)
    dense_total = None
    mixed_parts = []
    grad_parts = []
    for micro_step in range(MICRO):
        weights = (
            lax.all_gather(norm_attn, "expert", axis=0, tiled=True),
            lax.all_gather(w_query, "expert", axis=0, tiled=True),
            lax.all_gather(w_key, "expert", axis=0, tiled=True),
            lax.all_gather(w_value, "expert", axis=0, tiled=True),
            lax.all_gather(w_out, "expert", axis=0, tiled=True),
            lax.all_gather(rel_bias, "expert", axis=0, tiled=True),
            lax.all_gather(norm_expert, "expert", axis=0, tiled=True),
            lax.all_gather(w_router, "expert", axis=0, tiled=True),
        )
        gain_attn, query_w, key_w, value_w, out_w, bias_w, gain_expert, router_w = weights
        gain_one = gain_attn.astype(jnp.float32)
        gain_two = gain_expert.astype(jnp.float32)
        first_row = micro_step * TOK_MB
        inputs = tokens[first_row : first_row + TOK_MB].astype(jnp.float32)
        upstream = cotangent[first_row : first_row + TOK_MB].astype(jnp.float32)
        routes = expert_ids[first_row : first_row + TOK_MB]
        starts = span_starts[micro_step * SEQ_MB : (micro_step + 1) * SEQ_MB]
        normal_one, scale_one = norm_forward(inputs)
        attn_in = (normal_one * gain_one).astype(jnp.bfloat16)
        query = plain_dot(attn_in, query_w).astype(jnp.bfloat16)
        keys = plain_dot(attn_in, key_w).astype(jnp.bfloat16)
        values = plain_dot(attn_in, value_w).astype(jnp.bfloat16)
        bias_full = plain_dot(bias_w.reshape(HEADS, BUCKETS), bucket_hot).reshape(
            HEADS, SEQ_LEN, SEQ_LEN
        )

        def heads(matrix):
            return matrix.reshape(SEQ_MB, SEQ_LEN, HEADS, HEAD_DIM)

        def scores_of(query_seq, key_seq, start):
            logits = (
                jnp.einsum("qhd,khd->hqk", query_seq, key_seq, preferred_element_type=jnp.float32)
                * scale_head
                + bias_full
            )
            return jnp.where(allowed_mask(start)[None], logits, -1e30)

        def forward_seq(element):
            query_seq, key_seq, value_seq, start = element
            masked = scores_of(query_seq, key_seq, start)
            largest = jnp.max(masked, axis=-1, keepdims=True)
            expo = jnp.exp(masked - largest)
            total = jnp.sum(expo, axis=-1, keepdims=True)
            probs = (expo / total).astype(jnp.bfloat16)
            mixed_seq = jnp.einsum(
                "hqk,khd->qhd", probs, value_seq, preferred_element_type=jnp.float32
            )
            return (
                mixed_seq.astype(jnp.bfloat16).reshape(SEQ_LEN, D),
                largest[..., 0] + jnp.log(total[..., 0]),
            )

        attended, log_total = lax.map(
            forward_seq, (heads(query), heads(keys), heads(values), starts)
        )
        attended = attended.reshape(TOK_MB, D)
        hidden = inputs + plain_dot(attended, out_w)
        normal_two, scale_two = norm_forward(hidden)
        expert_rows = (normal_two * gain_two).astype(jnp.bfloat16)
        router = plain_dot(expert_rows, router_w)
        picks = (routes[:, :, None] == expert_iota[None, None, :]).astype(jnp.float32)
        chosen = jnp.sum(router[:, None, :] * picks, axis=-1)
        gates = jax.nn.softmax(chosen, axis=-1)
        flat_routes = routes.reshape(-1)
        pair_hot = (flat_routes[:, None] == expert_iota[None, :]).astype(jnp.int32)
        position = jnp.sum((jnp.cumsum(pair_hot, axis=0) - pair_hot) * pair_hot, axis=-1)
        slots = flat_routes * capacity + position
        spread = (slot_iota[:, None] == slots[None, :]).astype(jnp.bfloat16)
        dispatch = jnp.sum(spread.reshape(experts * capacity, TOK_MB, TOP), axis=-1)
        outgoing = (
            plain_dot(dispatch, expert_rows).astype(jnp.bfloat16).reshape(experts, capacity, D)
        )
        incoming = lax.all_to_all(outgoing, "expert", split_axis=0, concat_axis=0, tiled=True)
        count = incoming.shape[1]
        grouped = incoming.reshape(senders, local_experts, count, D)
        inner = jnp.einsum("sjcd,jdf->sjcf", grouped, expert_in, preferred_element_type=jnp.float32)
        active = gelu_tanh(inner).astype(jnp.bfloat16)
        result = jnp.einsum(
            "sjcf,jfd->sjcd", active, expert_out, preferred_element_type=jnp.float32
        ).astype(jnp.bfloat16)
        returned_rows = lax.all_to_all(
            result.reshape(senders * local_experts, count, D),
            "expert",
            split_axis=0,
            concat_axis=0,
            tiled=True,
        )
        inner_kept = inner.reshape(senders * local_experts, count, FF)
        picked = (
            jnp.take(returned_rows.reshape(experts * capacity, D), slots, axis=0)
            .astype(jnp.float32)
            .reshape(TOK_MB, TOP, D)
        )
        output = hidden + jnp.sum(gates[:, :, None] * picked, axis=1)
        mixed_parts.append(output.astype(jnp.bfloat16))
        gate_grad = jnp.sum(upstream[:, None, :] * picked, axis=-1)
        choice_grad = gates * (gate_grad - jnp.sum(gates * gate_grad, axis=-1, keepdims=True))
        logit_grad = jnp.sum(picks * choice_grad[:, :, None], axis=1).astype(jnp.bfloat16)
        grad_router_w = matmul_tn(expert_rows, logit_grad)
        rows_grad = matmul_nt(logit_grad, router_w)
        pick_grad = (
            (gates[:, :, None] * upstream[:, None, :]).astype(jnp.bfloat16).reshape(TOK_MB * TOP, D)
        )
        slot_grad = plain_dot(spread, pick_grad).astype(jnp.bfloat16).reshape(experts, capacity, D)
        arriving = lax.all_to_all(slot_grad, "expert", split_axis=0, concat_axis=0, tiled=True)
        grouped_grad = arriving.reshape(senders, local_experts, capacity, D)
        grouped_in = incoming.reshape(senders, local_experts, capacity, D)
        grouped_inner = inner_kept.reshape(senders, local_experts, capacity, FF)
        active_full, gelu_pull = jax.vjp(gelu_tanh, grouped_inner)
        active_low = active_full.astype(jnp.bfloat16)
        grad_outer_sum = grad_outer_sum + jnp.einsum(
            "sjcf,sjcd->jfd", active_low, grouped_grad, preferred_element_type=jnp.float32
        )
        active_grad = jnp.einsum(
            "sjcd,jfd->sjcf", grouped_grad, expert_out, preferred_element_type=jnp.float32
        )
        inner_grad = gelu_pull(active_grad)[0].astype(jnp.bfloat16)
        grad_inner_sum = grad_inner_sum + jnp.einsum(
            "sjcd,sjcf->jdf", grouped_in, inner_grad, preferred_element_type=jnp.float32
        )
        row_grad = jnp.einsum(
            "sjcf,jdf->sjcd", inner_grad, expert_in, preferred_element_type=jnp.float32
        ).astype(jnp.bfloat16)
        going_back = lax.all_to_all(
            row_grad.reshape(senders * local_experts, capacity, D),
            "expert",
            split_axis=0,
            concat_axis=0,
            tiled=True,
        )
        gathered_grad = (
            jnp.take(going_back.reshape(experts * capacity, D), slots, axis=0)
            .astype(jnp.float32)
            .reshape(TOK_MB, TOP, D)
        )
        rows_grad = rows_grad + jnp.sum(gathered_grad, axis=1)
        hidden_norm_grad, grad_gain_two = norm_backward(rows_grad, normal_two, scale_two, gain_two)
        hidden_grad = upstream + hidden_norm_grad
        branch_grad = hidden_grad.astype(jnp.bfloat16)
        grad_out_w = matmul_tn(attended, branch_grad)
        attended_grad = matmul_nt(branch_grad, out_w).astype(jnp.bfloat16)

        def backward_seq(element):
            query_seq, key_seq, value_seq, grad_seq, start, log_seq = element
            masked = scores_of(query_seq, key_seq, start)
            probs = jnp.exp(masked - log_seq[..., None])
            value_grad = jnp.einsum(
                "hqk,qhd->khd",
                probs.astype(jnp.bfloat16),
                grad_seq,
                preferred_element_type=jnp.float32,
            )
            prob_grad = jnp.einsum(
                "qhd,khd->hqk", grad_seq, value_seq, preferred_element_type=jnp.float32
            )
            center = jnp.sum(probs * prob_grad, axis=-1, keepdims=True)
            score_grad = (probs * (prob_grad - center)).astype(jnp.bfloat16)
            query_grad = (
                jnp.einsum("hqk,khd->qhd", score_grad, key_seq, preferred_element_type=jnp.float32)
                * scale_head
            )
            key_grad = (
                jnp.einsum(
                    "hqk,qhd->khd", score_grad, query_seq, preferred_element_type=jnp.float32
                )
                * scale_head
            )
            table_grad = jnp.einsum(
                "hn,bn->hb",
                score_grad.reshape(HEADS, SEQ_LEN * SEQ_LEN),
                bucket_hot,
                preferred_element_type=jnp.float32,
            )
            return (
                query_grad.astype(jnp.bfloat16).reshape(SEQ_LEN, D),
                key_grad.astype(jnp.bfloat16).reshape(SEQ_LEN, D),
                value_grad.astype(jnp.bfloat16).reshape(SEQ_LEN, D),
                table_grad,
            )

        seq_grads = lax.map(
            backward_seq,
            (heads(query), heads(keys), heads(values), heads(attended_grad), starts, log_total),
        )
        query_grad = seq_grads[0].reshape(TOK_MB, D)
        key_grad = seq_grads[1].reshape(TOK_MB, D)
        value_grad = seq_grads[2].reshape(TOK_MB, D)
        grad_table = jnp.sum(seq_grads[3], axis=0).reshape(-1)
        grad_query_w = matmul_tn(attn_in, query_grad)
        grad_key_w = matmul_tn(attn_in, key_grad)
        grad_value_w = matmul_tn(attn_in, value_grad)
        in_grad = (
            matmul_nt(query_grad, query_w)
            + matmul_nt(key_grad, key_w)
            + matmul_nt(value_grad, value_w)
        )
        input_norm_grad, grad_gain_one = norm_backward(in_grad, normal_one, scale_one, gain_one)
        grad_parts.append((hidden_grad + input_norm_grad).astype(jnp.bfloat16))
        step_terms = (
            lax.psum_scatter(grad_gain_one, "expert", scatter_dimension=0, tiled=True),
            lax.psum_scatter(grad_query_w, "expert", scatter_dimension=0, tiled=True),
            lax.psum_scatter(grad_key_w, "expert", scatter_dimension=0, tiled=True),
            lax.psum_scatter(grad_value_w, "expert", scatter_dimension=0, tiled=True),
            lax.psum_scatter(grad_out_w, "expert", scatter_dimension=0, tiled=True),
            lax.psum_scatter(grad_table, "expert", scatter_dimension=0, tiled=True),
            lax.psum_scatter(grad_gain_two, "expert", scatter_dimension=0, tiled=True),
            lax.psum_scatter(grad_router_w, "expert", scatter_dimension=0, tiled=True),
        )
        if micro_step == 0:
            dense_total = step_terms
        else:
            dense_total = add_trees(dense_total, step_terms)
    summed = (
        lax.psum(dense_total[0].astype(jnp.bfloat16), "group").astype(jnp.float32),
        lax.psum(dense_total[1].astype(jnp.bfloat16), "group").astype(jnp.float32),
        lax.psum(dense_total[2].astype(jnp.bfloat16), "group").astype(jnp.float32),
        lax.psum(dense_total[3].astype(jnp.bfloat16), "group").astype(jnp.float32),
        lax.psum(dense_total[4].astype(jnp.bfloat16), "group").astype(jnp.float32),
        lax.psum(dense_total[5].astype(jnp.bfloat16), "group").astype(jnp.float32),
        lax.psum(dense_total[6].astype(jnp.bfloat16), "group").astype(jnp.float32),
        lax.psum(dense_total[7].astype(jnp.bfloat16), "group").astype(jnp.float32),
        lax.psum(grad_inner_sum.astype(jnp.bfloat16), "group").astype(jnp.float32),
        lax.psum(grad_outer_sum.astype(jnp.bfloat16), "group").astype(jnp.float32),
    )
    mixed = jnp.concatenate(mixed_parts, axis=0)
    grad_tokens = jnp.concatenate(grad_parts, axis=0)
    return (
        mixed,
        grad_tokens,
        summed[0],
        summed[1],
        summed[2],
        summed[3],
        summed[4],
        summed[5],
        summed[6],
        summed[7],
        summed[8],
        summed[9],
    )


def solution(mesh):
    return jax.shard_map(
        shards,
        mesh=mesh,
        in_specs=(
            P(("group", "expert"), None),
            P(("group", "expert"), None),
            P("expert"),
            P("expert", None),
            P("expert", None),
            P("expert", None),
            P("expert", None),
            P("expert"),
            P("expert"),
            P("expert", None),
            P("expert", None, None),
            P("expert", None, None),
            P(("group", "expert"), None),
            P(("group", "expert")),
        ),
        out_specs=(
            P(("group", "expert"), None),
            P(("group", "expert"), None),
            P("expert"),
            P("expert", None),
            P("expert", None),
            P("expert", None),
            P("expert", None),
            P("expert"),
            P("expert"),
            P("expert", None),
            P("expert", None, None),
            P("expert", None, None),
        ),
        check_vma=False,
    )
```

profile of v0, /device:TPU:8, one launch (start us, length us, event | category | flops | bytes accessed | tf_op | source)
XLA Modules:
  0.0 1242.3 jit_solution(18116726308981102539)
XLA Ops:
  19.2 14.1 %all-reduce.7 = (bf16[768]{0:T(1024)(128)(2,1)S(1)}, bf16[384]{0:T(512)(128)(2,1)S(1)}, bf16[768]{0:T(1024)(128)(2,1)}) all-reduce(bf16[768]{0:T(1024)(128)(2,1)S(1)} %dynamic-update-slice, bf16[384]{0:T(512)(128)(2,1)S(1)} %dynamic-update-slice.1, bf16[768]{0:T(1024)(128)(2,1)S(1)} %dynamic-update-slice.2), channel_id=1, replica_groups=mesh['group'=4,'expert'=8] {'expert'}, use_global_device_ids=true, to_apply=%add | all-reduce | flops 1920 | bytes 7680
  44.5 19.1 %copy.158 = f32[2,8,512,512]{3,2,1,0:T(8,128)} copy(f32[2,8,512,512]{3,1,2,0:T(8,128)S(1)} %bitcast.362) | data formatting | bytes 33554432
  63.6 10.9 slice.58
  74.5 12.7 %copy.109 = f32[12,512,512]{1,2,0:T(8,128)} copy(f32[12,512,512]{2,1,0:T(8,128)} %slice.58) | data formatting | bytes 25165824 | tf_op jit(solution)/shard_map/reshape | solution.py:125
  128.0 59.1 %all_to_all.40 = bf16[8,192,768]{2,1,0:T(8,128)(2,1)S(1)} all-to-all(bf16[8,192,768]{2,1,0:T(8,128)(2,1)S(1)} %bitcast.407), channel_id=1, replica_groups=mesh['group'=4,'expert'=8] {'expert'}, dimensions={0} | all-to-all | bytes 4718592 | tf_op jit(solution)/shard_map/all_to_all | solution.py:175
  188.5 13.0 %fusion.73 = f32[8,192,3072]{2,1,0:T(8,128)} fusion(bf16[8,192,768]{2,1,0:T(8,128)(2,1)S(1)} %all_to_all.40, bf16[1,768,3072]{2,1,0:T(8,128)(2,1)} %param.26), kind=kOutput, calls=%fused_computation.102 | convolution fusion | flops 7247757312 | bytes 25952256 | tf_op jit(solution)/shard_map/sjcd,jdf->sjcf/dot_general | solution.py:178
  201.5 15.8 %fusion.98 = bf16[8,192,768]{2,1,0:T(8,128)(2,1)} fusion(bf16[1,3072,768]{2,1,0:T(8,128)(2,1)S(1)} %bitcast.417, f32[8,192,3072]{2,1,0:T(8,128)} %fusion.73), kind=kOutput, calls=%fused_computation.133 | convolution fusion | flops 7291404288 | bytes 25952256 | tf_op jit(solution)/shard_map/sjcf,jfd->sjcd/dot_general | solution.py:180
  223.4 56.7 %all-gather = bf16[8,96,8]{1,2,0:T(8,128)(2,1)S(1)} all-gather(bf16[1,96,8]{1,2,0:T(8,128)(2,1)S(1)} %bitcast.415), channel_id=1, replica_groups=mesh['group'=4,'expert'=8] {'expert'}, dimensions={0}, use_global_device_ids=true | all-gather | bytes 13824 | tf_op jit(solution)/shard_map/all_gather | solution.py:110
  330.6 33.8 %all-to-all-done.4 = bf16[8,192,768]{2,1,0:T(8,128)(2,1)} async-done(((bf16[8,192,768]{2,1,0:T(8,128)(2,1)}), bf16[8,192,768]{2,1,0:T(8,128)(2,1)}, u32[]{:S(2)}, u32[]{:S(2)}) %all-to-all-start.4) | async-done | bytes 2359328 | tf_op jit(solution)/shard_map/all_to_all | solution.py:207
  364.4 22.0 %fusion.9 = bf16[8,1,192,3072]{3,2,0,1:T(8,128)(2,1)S(1)} fusion(f32[8,192,3072]{2,1,0:T(8,128)} %fusion.73, bf16[8,192,768]{2,1,0:T(8,128)(2,1)} %all-to-all-done.4, bf16[1,3072,768]{2,1,0:T(8,128)(2,1)} %param.27), kind=kOutput, calls=%fused_computation.18 | convolution fusion | flops 7342129152 | bytes 35389440 | tf_op jit(solution)/shard_map/sjcd,jfd->sjcf/dot_general | solution.py:216
  390.1 11.6 fusion.108
  424.3 35.8 %all-to-all-done.5 = bf16[8,192,768]{2,1,0:T(8,128)(2,1)S(1)} async-done(((bf16[8,192,768]{2,1,0:T(8,128)(2,1)}), bf16[8,192,768]{2,1,0:T(8,128)(2,1)S(1)}, u32[]{:S(2)}, u32[]{:S(2)}) %all-to-all-start.5) | async-done | bytes 2359328 | tf_op jit(solution)/shard_map/all_to_all | solution.py:226
  484.9 58.7 %all_to_all.41 = bf16[8,192,768]{2,1,0:T(8,128)(2,1)S(1)} all-to-all(bf16[8,192,768]{2,1,0:T(8,128)(2,1)S(1)} %bitcast.408), channel_id=1, replica_groups=mesh['group'=4,'expert'=8] {'expert'}, dimensions={0} | all-to-all | bytes 4718592 | tf_op jit(solution)/shard_map/all_to_all | solution.py:175
  545.0 10.8 fusion.71
  555.8 15.8 %fusion.103 = bf16[8,192,768]{2,1,0:T(8,128)(2,1)} fusion(bf16[1,3072,768]{2,1,0:T(8,128)(2,1)S(1)} %bitcast.419, f32[8,192,3072]{2,1,0:T(8,128)} %fusion.71), kind=kOutput, calls=%fused_computation.134 | convolution fusion | flops 7291404288 | bytes 25952256 | tf_op jit(solution)/shard_map/sjcf,jfd->sjcd/dot_general | solution.py:180
  587.8 41.2 %all-to-all-done.3 = bf16[8,192,768]{2,1,0:T(8,128)(2,1)S(1)} async-done(((bf16[8,192,768]{2,1,0:T(8,128)(2,1)}), bf16[8,192,768]{2,1,0:T(8,128)(2,1)S(1)}, u32[]{:S(2)}, u32[]{:S(2)}) %all-to-all-start.3) | async-done | bytes 2359328 | tf_op jit(solution)/shard_map/all_to_all | solution.py:183
  641.4 58.5 %all_to_all.42 = bf16[8,192,768]{2,1,0:T(8,128)(2,1)S(1)} all-to-all(bf16[8,192,768]{2,1,0:T(8,128)(2,1)S(1)} %bitcast.406), channel_id=1, replica_groups=mesh['group'=4,'expert'=8] {'expert'}, dimensions={0} | all-to-all | bytes 4718592 | tf_op jit(solution)/shard_map/all_to_all | solution.py:207
  699.9 21.3 %fusion.16 = bf16[8,1,192,3072]{3,2,0,1:T(8,128)(2,1)S(1)} fusion(f32[8,192,3072]{2,1,0:T(8,128)} %fusion.71, bf16[8,192,768]{2,1,0:T(8,128)(2,1)S(1)} %all_to_all.42, bf16[1,3072,768]{2,1,0:T(8,128)(2,1)} %param.27), kind=kOutput, calls=%fused_computation.25 | convolution fusion | flops 7342129152 | bytes 35389440 | tf_op jit(solution)/shard_map/sjcd,jfd->sjcf/dot_general | solution.py:216
  751.9 39.0 %all-to-all-done.7 = bf16[8,192,768]{2,1,0:T(8,128)(2,1)S(1)} async-done(((bf16[8,192,768]{2,1,0:T(8,128)(2,1)}), bf16[8,192,768]{2,1,0:T(8,128)(2,1)S(1)}, u32[]{:S(2)}, u32[]{:S(2)}) %all-to-all-start.7) | async-done | bytes 2359328 | tf_op jit(solution)/shard_map/all_to_all | solution.py:226
  858.9 10.7 multiply_reduce_fusion.1
  869.6 10.1 multiply_convert_fusion.1
  920.0 17.3 %fusion.42 = f32[3072,768,1]{1,0,2:T(8,128)} fusion(bf16[8,192,768]{2,1,0:T(8,128)(2,1)} %copy-done.65, f32[8,192,3072]{2,1,0:T(8,128)} %fusion.71), kind=kOutput, calls=%fused_computation.71 | convolution fusion | flops 7290224640 | bytes 30670848 | tf_op jit(solution)/shard_map/sjcf,sjcd->jfd/dot_general | solution.py:213
  937.3 12.5 %fusion.34 = f32[768,3072,1]{1,0,2:T(8,128)} fusion(bf16[8,192,768]{2,1,0:T(8,128)(2,1)S(1)} %copy-done.64, bf16[8,1,192,3072]{3,2,0,1:T(8,128)(2,1)} %copy-done.111), kind=kOutput, calls=%fused_computation.63 | convolution fusion | flops 7247757312 | bytes 21233664 | tf_op jit(solution)/shard_map/sjcd,sjcf->jdf/dot_general | solution.py:220
  949.8 18.2 %fusion.64 = bf16[1,3072,768]{2,1,0:T(8,128)(2,1)} fusion(f32[3072,768,1]{1,0,2:T(8,128)} %fusion.42, bf16[8,192,768]{2,1,0:T(8,128)(2,1)} %all-to-all-done.4, f32[8,192,3072]{2,1,0:T(8,128)} %fusion.73), kind=kOutput, calls=%fused_computation.93 | convolution fusion | flops 7294943232 | bytes 35389440 | tf_op jit(solution)/shard_map/sjcf,sjcd->jfd/dot_general | solution.py:213
  968.0 13.9 %fusion.77 = bf16[1,768,3072]{2,1,0:T(8,128)(2,1)} fusion(f32[768,3072,1]{1,0,2:T(8,128)} %fusion.34, bf16[8,192,768]{2,1,0:T(8,128)(2,1)S(1)} %copy-done.62, bf16[8,1,192,3072]{3,2,0,1:T(8,128)(2,1)} %copy-done.110), kind=kOutput, calls=%fused_computation.104 | convolution fusion | flops 7252475904 | bytes 25952256 | tf_op jit(solution)/shard_map/sjcd,sjcf->jdf/dot_general | solution.py:220
  989.8 21.3 %reduce-scatter.16.cloned.1.call-done = f32[96,8]{1,0:T(8,128)} async-done(((f32[768,8]{1,0:T(8,128)}), f32[96,8]{1,0:T(8,128)}) %reduce-scatter.16.cloned.1.call-update) | async-done | bytes 3088
  1020.6 8.9 copy.140
  1036.3 11.8 copy.161
  1055.1 11.8 copy.162
  1093.9 25.9 %all-reduce.6 = (bf16[768]{0:T(1024)(128)(2,1)S(1)}, bf16[384]{0:T(512)(128)(2,1)S(1)}, bf16[768]{0:T(1024)(128)(2,1)S(1)}) all-reduce(f32[768]{0:T(1024)S(1)} %add.474, f32[384]{0:T(512)S(1)} %reshape.917, f32[768]{0:T(1024)S(1)} %add.480), channel_id=10, replica_groups=mesh['group'=4,'expert'=8] {'expert'}, use_global_device_ids=true, to_apply=%region_39.41.clone | all-reduce | flops 1920 | bytes 11520
  1120.0 10.7 all-reduce.8
  1139.5 80.5 %all-reduce.12.cloned.1.call-done = (bf16[96,768]{1,0:T(8,128)(2,1)}, bf16[96,768]{1,0:T(8,128)(2,1)}, bf16[96,768]{1,0:T(8,128)(2,1)}, bf16[96,768]{1,0:T(8,128...) async-done(((bf16[96,768]{1,0:T(8,128)(2,1)}, bf16[96,768]{1,0:T(8,128)(2,1)}, bf16[96,768]{1,0:T(8,128)(2,1)}, bf16[96,768]{1,0:T(8,128)(2,1)}, ...) | async-done | bytes 10027024 | tf_op jit(solution)/shard_map/psum | solution.py:317
  (485 shorter events, 418.6 us)
Async XLA Ops:
  7.2 88.7 %all-gather.8.cloned.1.call-start = ((), (), s32[]{:S(2)}) async-start(), calls=%async_computation.14 | async-start | bytes 1327104 | tf_op jit(solution)/shard_map/all_gather | solution.py:104
  7.9 90.4 %all-gather.10.cloned.1.call-start = ((), (), s32[]{:S(2)}) async-start(), calls=%async_computation.15 | async-start | bytes 1327104 | tf_op jit(solution)/shard_map/all_gather | solution.py:105
  8.7 94.4 %all-gather.6.cloned.1.call-start = ((), (), s32[]{:S(2)}) async-start(), calls=%async_computation.13 | async-start | bytes 1327104 | tf_op jit(solution)/shard_map/all_gather | solution.py:106
  9.4 112.8 %all-gather.12.cloned.1.call-start = ((), (), s32[]{:S(2)}) async-start(), calls=%async_computation.16 | async-start | bytes 1327104 | tf_op jit(solution)/shard_map/all_gather | solution.py:107
  11.4 21.9 %copy-start.4 = (bf16[1024,768]{1,0:T(8,128)(2,1)S(1)}, bf16[1024,768]{1,0:T(8,128)(2,1)}, u32[]{:S(2)}) copy-start(bf16[1024,768]{1,0:T(8,128)(2,1)} %param.16) | copy-start | bytes 4718596
  15.1 21.8 %copy-start.43 = (s32[512,2]{1,0:T(8,128)}, s32[512,2]{1,0:T(8,128)S(1)}, u32[]{:S(2)}) copy-start(s32[512,2]{1,0:T(8,128)S(1)} %copy.151) | copy-start | bytes 12292
  33.4 293.6 %copy-start.75 = (f32[768]{0:T(1024)}, f32[768]{0:T(1024)S(1)}, u32[]{:S(2)}) copy-start(f32[768]{0:T(1024)S(1)} %convert_element_type.593) | copy-start | bytes 9220
  95.9 231.1 %copy-start.85 = (f32[512]{0:T(512)}, f32[512]{0:T(512)S(1)}, u32[]{:S(2)}) copy-start(f32[512]{0:T(512)S(1)} %get-tuple-element.209) | copy-start | bytes 6148
  126.6 164.4 %copy-start.29 = (bf16[512,768]{1,0:T(8,128)(2,1)}, bf16[512,768]{1,0:T(8,128)(2,1)S(1)}, u32[]{:S(2)}) copy-start(bf16[512,768]{1,0:T(8,128)(2,1)S(1)} %multiply_convert_fusion.11) | copy-start | bytes 2359300
  128.0 73.5 %slice-start.3 = ((s8[4718592]{0:T(1024)(128)(4,1)}), s8[4194304]{0:T(1024)(128)(4,1)S(1)}, s32[]{:S(2)}) async-start(s8[4718592]{0:T(1024)(128)(4,1)} %bitcast.416), calls=%async_computation.26 | async-start | bytes 8388608
  217.4 74.0 %all-to-all-start.1 = ((bf16[8,192,768]{2,1,0:T(8,128)(2,1)}), bf16[8,192,768]{2,1,0:T(8,128)(2,1)S(1)}, u32[]{:S(2)}, u32[]{:S(2)}) async-start(bf16[8,192,768]{2,1,0:T(8,128)(2,1)} %fusion.98), calls=%async_computation.1 | async-start | bytes 4718592 | tf_op jit(solution)/shard_map/all_to_all | solution.py:183
  304.8 59.6 %all-to-all-start.4 = ((bf16[8,192,768]{2,1,0:T(8,128)(2,1)}), bf16[8,192,768]{2,1,0:T(8,128)(2,1)}, u32[]{:S(2)}, u32[]{:S(2)}) async-start(bf16[8,192,768]{2,1,0:T(8,128)(2,1)} %bitcast.405), calls=%async_computation.4 | async-start | bytes 4718592 | tf_op jit(solution)/shard_map/all_to_all | solution.py:207
  327.0 81.9 %copy-start.22 = (bf16[512,768]{0,1:T(8,128)(2,1)}, bf16[512,768]{0,1:T(8,128)(2,1)S(1)}, u32[]{:S(2)}) copy-start(bf16[512,768]{0,1:T(8,128)(2,1)S(1)} %copy.118) | copy-start | bytes 2359300
  401.7 58.3 %all-to-all-start.5 = ((bf16[8,192,768]{2,1,0:T(8,128)(2,1)}), bf16[8,192,768]{2,1,0:T(8,128)(2,1)S(1)}, u32[]{:S(2)}, u32[]{:S(2)}) async-start(bf16[8,192,768]{2,1,0:T(8,128)(2,1)} %fusion.108), calls=%async_computation.5 | async-start | bytes 4718592 | tf_op jit(solution)/shard_map/all_to_all | solution.py:226
  424.3 55.1 %copy-start.83 = (bf16[512,8]{0,1:T(8,128)(2,1)}, bf16[512,8]{0,1:T(8,128)(2,1)S(1)}, u32[]{:S(2)}) copy-start(bf16[512,8]{0,1:T(8,128)(2,1)S(1)} %select_reduce_fusion.1) | copy-start | bytes 24580
  479.5 65.5 %slice-start.7 = ((s8[4718592]{0:T(1024)(128)(4,1)}), s8[4194304]{0:T(1024)(128)(4,1)S(1)}, s32[]{:S(2)}) async-start(s8[4718592]{0:T(1024)(128)(4,1)} %bitcast.420), calls=%async_computation.30 | async-start | bytes 8388608
  483.4 61.6 %slice-start.8 = ((s8[4718592]{0:T(1024)(128)(4,1)}), s8[524288]{0:T(1024)(128)(4,1)S(1)}, s32[]{:S(2)}) async-start(s8[4718592]{0:T(1024)(128)(4,1)} %bitcast.420), calls=%async_computation.31 | async-start | bytes 1048576
  484.9 70.9 %slice-start.5 = ((s8[4718592]{0:T(1024)(128)(4,1)}), s8[4194304]{0:T(1024)(128)(4,1)S(1)}, s32[]{:S(2)}) async-start(s8[4718592]{0:T(1024)(128)(4,1)} %bitcast.418), calls=%async_computation.28 | async-start | bytes 8388608
  571.6 57.4 %all-to-all-start.3 = ((bf16[8,192,768]{2,1,0:T(8,128)(2,1)}), bf16[8,192,768]{2,1,0:T(8,128)(2,1)S(1)}, u32[]{:S(2)}, u32[]{:S(2)}) async-start(bf16[8,192,768]{2,1,0:T(8,128)(2,1)} %fusion.103), calls=%async_computation.3 | async-start | bytes 4718592 | tf_op jit(solution)/shard_map/all_to_all | solution.py:183
  638.1 86.9 %slice-start.9 = ((s8[4718592]{0:T(1024)(128)(4,1)}), s8[524288]{0:T(1024)(128)(4,1)S(1)}, s32[]{:S(2)}) async-start(s8[4718592]{0:T(1024)(128)(4,1)} %bitcast.422), calls=%async_computation.32 | async-start | bytes 1048576
  699.9 21.3 %copy-start.65 = (bf16[8,192,768]{2,1,0:T(8,128)(2,1)}, bf16[8,192,768]{2,1,0:T(8,128)(2,1)S(1)}, u32[]{:S(2)}) copy-start(bf16[8,192,768]{2,1,0:T(8,128)(2,1)S(1)} %all_to_all.42) | copy-start | bytes 7077892
  699.9 25.1 %slice-start.10 = ((s8[4718592]{0:T(1024)(128)(4,1)}), s8[4194304]{0:T(1024)(128)(4,1)S(1)}, s32[]{:S(2)}) async-start(s8[4718592]{0:T(1024)(128)(4,1)} %bitcast.422), calls=%async_computation.33 | async-start | bytes 8388608
  733.7 57.1 %all-to-all-start.7 = ((bf16[8,192,768]{2,1,0:T(8,128)(2,1)}), bf16[8,192,768]{2,1,0:T(8,128)(2,1)S(1)}, u32[]{:S(2)}, u32[]{:S(2)}) async-start(bf16[8,192,768]{2,1,0:T(8,128)(2,1)} %fusion.113), calls=%async_computation.7 | async-start | bytes 4718592 | tf_op jit(solution)/shard_map/all_to_all | solution.py:226
  739.7 242.2 %reduce-scatter.14.cloned.1.call-start = ((), (), s32[]{:S(2)}) async-start(), calls=%async_computation.20 | async-start | bytes 2654208 | tf_op jit(solution)/shard_map/reduce_scatter | solution.py:306
  831.0 152.6 %reduce-scatter.12.cloned.1.call-start = ((), (), s32[]{:S(2)}) async-start(), calls=%async_computation.19 | async-start | bytes 2654208 | tf_op jit(solution)/shard_map/reduce_scatter | solution.py:305
  858.6 126.6 %reduce-scatter.10.cloned.1.call-start = ((), (), s32[]{:S(2)}) async-start(), calls=%async_computation.18 | async-start | bytes 2654208 | tf_op jit(solution)/shard_map/reduce_scatter | solution.py:304
  858.9 25.3 %slice-start = ((s8[12582912]{0:T(1024)(128)(4,1)}), s8[4194304]{0:T(1024)(128)(4,1)S(1)}, s32[]{:S(2)}) async-start(s8[12582912]{0:T(1024)(128)(4,1)} %bitcast.360), calls=%async_computation.23 | async-start | bytes 8388608
  858.9 25.3 %slice-start.1 = ((s8[12582912]{0:T(1024)(128)(4,1)}), s8[4194304]{0:T(1024)(128)(4,1)S(1)}, s32[]{:S(2)}) async-start(s8[12582912]{0:T(1024)(128)(4,1)} %bitcast.360), calls=%async_computation.24 | async-start | bytes 8388608
  903.3 83.6 %reduce-scatter.8.cloned.1.call-start = ((), (), s32[]{:S(2)}) async-start(), calls=%async_computation.17 | async-start | bytes 2654208 | tf_op jit(solution)/shard_map/reduce_scatter | solution.py:303
  917.4 93.7 %reduce-scatter.16.cloned.1.call-start = ((), (), s32[]{:S(2)}) async-start(), calls=%async_computation.21 | async-start | bytes 442368
  920.0 300.0 %all-reduce.12.cloned.1.call-start = ((), (), s32[]{:S(2)}) async-start(), calls=%async_computation.22 | async-start | bytes 20054016 | tf_op jit(solution)/shard_map/psum | solution.py:317
  1091.0 41.8 %copy-start.10 = (f32[512,768]{1,0:T(8,128)S(1)}, f32[512,768]{1,0:T(8,128)}, u32[]{:S(2)}) copy-start(f32[512,768]{1,0:T(8,128)} %copy-done.9) | copy-start | bytes 4718596
  (106 other events, 555.1 us)
Sparse Core Ops, SparseCore 0:
  9.7 23.9 all-gather.7
  35.3 22.3 all-gather.9
  59.3 22.4 all-gather.5
  83.2 22.5 all-gather.11
  831.1 34.2 reduce-scatter.13
  867.6 35.6 reduce-scatter.11
  905.6 35.3 reduce-scatter.9
  943.4 35.4 reduce-scatter.7
  981.1 29.9 reduce-scatter.15
  1016.8 203.0 all-reduce.11
where the time goes:
time: 1250 us; the launch traced here: 1240 us
  matrix products  326 us (26%)
  blocking collectives  284 us (23%)
  waiting for transfers between devices  254 us (20%)
  local copies, waits for them, and re-layouts  207 us (17%)
  other arithmetic  116 us (9%)
  starting transfers between devices  35.1 us (3%)
  between operations  20.2 us (2%)
    all_to_all x2, blocking collectives, shards(): lax.all_to_all(outgoing, 'expert', split_axis=0, concat_axis=0, tiled=True)  118 us
    unnamed x271, local copies, waits for them, and re-layouts  94.9 us
    psum x1, waiting for transfers between devices, shards(): lax.psum(dense_total[1].astype(jnp.bfloat16), 'group').astype(jnp.float32)  80.5 us
    all_to_all x2, waiting for transfers between devices, shards(): lax.all_to_all(row_grad.reshape(senders * local_experts, capacity, D), 'e...  74.8 us
    all_to_all x1, blocking collectives, shards(): lax.all_to_all(slot_grad, 'expert', split_axis=0, concat_axis=0, tiled=True)  58.5 us
    all_gather x1, blocking collectives, shards(): lax.all_gather(w_router, 'expert', axis=0, tiled=True)  56.7 us
    dot_general x2, matrix products, shards(): jnp.einsum('sjcd,jfd->sjcf', grouped_grad, expert_out, preferred_element_...  43.3 us
    all_to_all x2, waiting for transfers between devices, shards(): lax.all_to_all(result.reshape(senders * local_experts, count, D), 'expert...  41.2 us
  transfers between devices with their start and end apart: 15, of which 6 were waited for; matrix products, arithmetic and copies ran while one was open for 31% of the time, Pallas kernels for 0%

commit v1 on v0

v1 whole, which is shorter than its diff:
```python
import functools

import jax
import jax.numpy as jnp
import numpy as np
from jax import lax
from jax.experimental import pallas as pl
from jax.experimental.pallas import tpu as pltpu
from jax.sharding import PartitionSpec as P

D = 768
HEADS = 12
HEAD_DIM = 64
FF = 3072
TOP = 2
BUCKETS = 32
SEQ_LEN = 512
PIC = 256
MICRO = 2
TOK_MB = 512
ROW_TILE = 256
DIRECT_MAX = 8
COST_BYTES = 3600000

epsilon = 1e-06
bucket_edges = (1, 2, 3, 4, 5, 6, 7, 8, 12, 16, 23, 32, 45, 64, 91)
f32 = jnp.float32
bf16 = jnp.bfloat16
MIB = 1 << 20


def dot_nn(left, right):
    return lax.dot_general(left, right, (((1,), (0,)), ((), ())), preferred_element_type=f32)


def dot_nt(left, right):
    return lax.dot_general(left, right, (((1,), (1,)), ((), ())), preferred_element_type=f32)


def dot_tn(left, right):
    return lax.dot_general(left, right, (((0,), (0,)), ((), ())), preferred_element_type=f32)


def iota(shape, dim):
    return lax.broadcasted_iota(jnp.int32, shape, dim)


def diagonal_offsets():
    place = np.arange(1024)
    return np.where(place < 896, 384 - place, 1408 - place)


def bucket_hot():
    offset = diagonal_offsets()
    magnitude = sum((np.abs(offset) >= edge).astype(np.int32) for edge in bucket_edges)
    bucket = magnitude + 16 * (offset > 0)
    hot = bucket[None, :] == np.arange(BUCKETS)[:, None]
    return hot & (np.abs(offset) < SEQ_LEN)[None, :]


def lasting(microseconds):
    return pl.CostEstimate(flops=0, bytes_accessed=int(microseconds * COST_BYTES), transcendentals=0)


def resident(shape, index):
    return pl.BlockSpec(shape, index, pipeline_mode=pl.Buffered(1))


def split_rows(values):
    high = values.astype(bf16).astype(f32)
    row = iota((8, values.shape[1]), 0)
    return jnp.where(row == 0, high, jnp.where(row == 1, values - high, 0.0)).astype(bf16)


def row_to_column(row):
    size = row.shape[1]
    step = 128 if size % 128 == 0 else size
    eye = iota((step, step), 0) == iota((step, step), 1)
    columns = [
        jnp.sum(jnp.where(eye, row[:, i : i + step], 0.0), axis=1, keepdims=True)
        for i in range(0, size, step)
    ]
    return columns[0] if len(columns) == 1 else jnp.concatenate(columns, axis=0)


def column_to_row(column):
    size = column.shape[0]
    step = 128 if size % 128 == 0 else size
    eye = iota((step, step), 0) == iota((step, step), 1)
    rows = [
        jnp.sum(jnp.where(eye, column[i : i + step], 0.0), axis=0, keepdims=True)
        for i in range(0, size, step)
    ]
    return rows[0] if len(rows) == 1 else jnp.concatenate(rows, axis=1)


def slot_hot(slot_row, first, size):
    return iota((size, TOK_MB), 0) + first == slot_row


def route_kernel(me_ref, ids_ref, cot_ref, slots_ref, *block_refs, experts, capacity):
    place = iota((experts, TOK_MB), 0)
    earlier = earlier_places()
    for step in range(MICRO):
        here = slice(step * TOK_MB, (step + 1) * TOK_MB)
        hots = [ids_ref[k : k + 1, here] == place for k in range(TOP)]
        both = jnp.where(hots[0] | hots[1], 1.0, 0.0).astype(bf16)
        at = dot_nn(both, earlier) + ((place ^ me_ref[0]) * capacity).astype(f32)
        slots = [jnp.sum(jnp.where(hot, at, 0.0), axis=0, keepdims=True).astype(jnp.int32) for hot in hots]
        for k in range(TOP):
            slots_ref[step, k : k + 1, :] = slots[k]
        rows = block_refs[0].shape[0] // MICRO
        half = min(rows // 2, 384)
        for first in range(0, experts * capacity, half):
            hot = slot_hot(slots[0], first, half) | slot_hot(slots[1], first, half)
            value = dot_nn(jnp.where(hot, 1.0, 0.0).astype(bf16), cot_ref[here, :]).astype(bf16)
            index, low = first // rows, first % rows
            if len(block_refs) > 1:
                low = 2 * low + step * half
            else:
                low = low + step * rows
            block_refs[index][low : low + half, :] = value


def earlier_places():
    return jnp.where(iota((TOK_MB, TOK_MB), 0) < iota((TOK_MB, TOK_MB), 1), 1.0, 0.0).astype(bf16)


def route(me, ids, cotangent, blocks, experts, capacity):
    size = MICRO * experts * capacity // blocks
    return pl.pallas_call(
        functools.partial(route_kernel, experts=experts, capacity=capacity),
        in_specs=[pl.BlockSpec(memory_space=pltpu.SMEM)] + [pl.BlockSpec(memory_space=pltpu.VMEM)] * 2,
        out_shape=[jax.ShapeDtypeStruct((MICRO, TOP, TOK_MB), jnp.int32)]
        + [jax.ShapeDtypeStruct((size, D), bf16)] * blocks,
        compiler_params=pltpu.CompilerParams(vmem_limit_bytes=32 * MIB),
        cost_estimate=lasting(4),
        name="route",
    )(me, ids, cotangent)


def partner_kernel(me_ref, ids_ref, other_ref, *, xor):
    devices, capacity = other_ref.shape[1:]
    earlier = earlier_places()
    mine = me_ref[0].astype(f32)
    for step in range(MICRO):
        first, second = ids_ref[step], ids_ref[MICRO + step]
        hot = (first == mine) | (second == mine)
        order = dot_nn(jnp.where(hot, 1.0, 0.0).astype(bf16), earlier).astype(jnp.int32)
        order = jnp.where(hot, order, -1)
        partner = (first + second - mine).astype(bf16)
        for sender in range(devices):
            pick = jnp.where(iota((capacity, TOK_MB), 0) == order[sender : sender + 1, :], 1.0, 0.0).astype(bf16)
            found = dot_nt(partner, pick)[sender : sender + 1, :]
            row = sender ^ me_ref[0] if xor else sender
            other_ref[step, pl.ds(row, 1), :] = found


def partners(me, ids, devices, capacity, xor):
    return pl.pallas_call(
        functools.partial(partner_kernel, xor=xor),
        in_specs=[pl.BlockSpec(memory_space=pltpu.SMEM)] + [pl.BlockSpec(memory_space=pltpu.VMEM)],
        out_shape=jax.ShapeDtypeStruct((MICRO, devices, capacity), f32),
        compiler_params=pltpu.CompilerParams(vmem_limit_bytes=32 * MIB),
        cost_estimate=lasting(1.3),
        name="partners",
    )(me, ids)


def unpack_kernel(place_ref, *refs, groups, chips, lines):
    own, passed, small, (out_ref, narrow_ref, ids_ref) = refs[:groups], refs[groups], refs[groups + 1], refs[groups + 2 :]
    rows = own[0].shape[0] // chips
    me = place_ref[1]
    for k in range(groups):
        for j in range(chips):
            low = (k * chips + j) * rows
            values = own[k][j * rows : (j + 1) * rows, :], passed[low : low + rows, :]
            for core in range(2):
                here = pl.ds(pl.multiple_of((me ^ (2 * j + core)) * rows, rows), rows)
                out_ref[place_ref[0] ^ k, here, :] = values[core]
    gathered = jnp.zeros((16, D), f32)
    lane = iota((16, D), 1)
    for k in range(2 * chips):
        source = small if k % 2 == 0 else passed
        low = k // 2 * 16 + (0 if k % 2 == 0 else groups * chips * rows)
        block = source[low : low + 16, :].astype(f32)
        device = me ^ k
        gathered = gathered + pltpu.roll(jnp.where(lane < rows, block, 0.0), device * rows, 1)
        for pick in range(TOP * MICRO):
            ids_ref[pick, pl.ds(device, 1), :] = block[lines + pick : lines + pick + 1, :TOK_MB]
    narrow_ref[...] = gathered.astype(bf16)


def gather_weights(matrices, narrow, ids, groups, devices):
    lines, shard = narrow.shape
    if devices > DIRECT_MAX:
        whole = jnp.stack([lax.all_gather(w, "expert", axis=0, tiled=True) for w in matrices])
        flat = jnp.concatenate([narrow.reshape(-1), ids.astype(bf16).reshape(-1)])
        flat = lax.all_gather(flat, "expert", axis=0)
        narrow = flat[:, : lines * shard].reshape(devices, lines, shard).transpose(1, 0, 2).reshape(lines, D)
        ids = flat[:, lines * shard :].astype(f32).reshape(devices, TOP * MICRO, TOK_MB).transpose(1, 0, 2)
        return whole, narrow, ids
    chips = devices // 2
    group, me = lax.axis_index("group"), lax.axis_index("expert")
    mine = matrices[0]
    for index in range(1, groups):
        mine = jnp.where(group == index, matrices[index], mine)
    small = jnp.concatenate(
        [
            jnp.pad(narrow, ((0, 0), (0, D - shard))),
            jnp.pad(ids.astype(bf16).reshape(TOP * MICRO, TOK_MB), ((0, 0), (0, D - TOK_MB))),
            jnp.zeros((16 - lines - TOP * MICRO, D), bf16),
        ],
        axis=0,
    )
    mine = jnp.concatenate([mine, small], axis=0)
    mine = [mine] + [lax.ppermute(mine, "expert", swap(devices, 2 * j)) for j in range(1, chips)]
    small = jnp.concatenate([m[shard:] for m in mine], axis=0)
    mine = jnp.concatenate([m[:shard] for m in mine], axis=0)
    own = [mine] + [lax.ppermute(mine, "group", swap(groups, k)) for k in range(1, groups)]
    passed = lax.ppermute(jnp.concatenate([*own, small], axis=0), "expert", swap(devices, 1))
    place = jnp.stack([group, me]).astype(jnp.int32)
    return pl.pallas_call(
        functools.partial(unpack_kernel, groups=groups, chips=chips, lines=lines),
        in_specs=[pl.BlockSpec(memory_space=pltpu.SMEM)] + [pl.BlockSpec(memory_space=pltpu.VMEM)] * (groups + 2),
        out_shape=[
            jax.ShapeDtypeStruct((groups, D, D), bf16),
            jax.ShapeDtypeStruct((16, D), bf16),
            jax.ShapeDtypeStruct((TOP * MICRO, devices, TOK_MB), f32),
        ],
        compiler_params=pltpu.CompilerParams(vmem_limit_bytes=32 * MIB),
        cost_estimate=lasting(3),
        name="unpack",
    )(place, *own, passed, small)


def swap(devices, mask):
    return [(i, i ^ mask) for i in range(devices)]


def bias_places(devices):
    place = np.arange(D)
    wide, share = D // devices, HEADS * BUCKETS // devices
    flat = place // wide * share + place % wide
    used = place % wide < share
    bucket = (flat[:, None] % BUCKETS == np.arange(BUCKETS)[None, :]) & used[:, None]
    head = (flat[None, :] // BUCKETS == np.arange(16)[:, None]) & used[None, :]
    return bucket.astype(np.float32), head.astype(np.float32)


def attend_kernel(
    starts_ref, x_ref, query_w, key_w, value_w, out_w, narrow_ref, hot_ref, bucket_ref, heads_ref, ids_ref, slots_ref,
    query_ref, key_ref, value_ref, probs_ref, attended_ref, hidden_ref, rows_ref, gates_ref, normed_ref,
    *refs, step, experts,
):
    block_refs, (mask_ref, table_ref) = refs[:-2], refs[-2:]
    head = pl.program_id(0)

    @pl.when(head == 0)
    def _():
        x = x_ref[...].astype(f32)
        scale = lax.rsqrt(jnp.mean(x * x, axis=-1, keepdims=True) + epsilon)
        normed = (x * scale * narrow_ref[experts : experts + 1, :].astype(f32)).astype(bf16)
        normed_ref[...] = normed
        query = dot_nn(normed, query_w[0]).astype(bf16).astype(f32) * HEAD_DIM**-0.5
        query_ref[...] = query.T.astype(bf16)
        key_ref[...] = dot_nn(normed, key_w[0]).T.astype(bf16)
        value_ref[...] = dot_nn(normed, value_w[0]).T.astype(bf16)
        rel = (heads_ref[...].astype(f32) * narrow_ref[experts + 2 : experts + 3, :].astype(f32)).astype(bf16)
        table_ref[...] = dot_nn(dot_nn(rel, bucket_ref[...]).astype(bf16), hot_ref[...])
        start = starts_ref[step]
        key_place, query_place = iota((SEQ_LEN, SEQ_LEN), 0), iota((SEQ_LEN, SEQ_LEN), 1)
        inside = (
            (key_place >= start)
            & (key_place < start + PIC)
            & (query_place >= start)
            & (query_place < start + PIC)
        )
        mask_ref[...] = jnp.where((key_place <= query_place) | inside, 0.0, -1e30)

    span = pl.ds(pl.multiple_of(head * HEAD_DIM, HEAD_DIM), HEAD_DIM)
    table = jnp.broadcast_to(table_ref[pl.ds(head, 1), :], (8, 1024))
    low_row = iota((8, 1024), 0)
    for bit in (1, 2, 4):
        table = jnp.where((low_row & bit) != 0, pltpu.roll(table, bit, 1), table)
    for shift in (8, 16, 32, 64):
        table = jnp.concatenate([table, pltpu.roll(table, shift, 1)], axis=0)
    scores = dot_tn(key_ref[span, :], query_ref[span, :])
    bias = jnp.concatenate([table[:, 384 - a * 128 : 896 - a * 128] for a in range(4)], axis=0)
    scores = scores + bias + mask_ref[...]
    expo = jnp.exp(scores - jnp.max(scores, axis=0, keepdims=True))
    probs = (expo * (1.0 / jnp.sum(expo, axis=0, keepdims=True))).astype(bf16)
    probs_ref[0] = probs
    attended_ref[span, :] = dot_nn(value_ref[span, :], probs).astype(bf16)

    @pl.when(head == HEADS - 1)
    def _():
        hidden = x_ref[...].astype(f32) + dot_tn(attended_ref[...], out_w[0])
        hidden_ref[...] = hidden
        scale = lax.rsqrt(jnp.mean(hidden * hidden, axis=-1, keepdims=True) + epsilon)
        rows = (hidden * scale * narrow_ref[experts + 1 : experts + 2, :].astype(f32)).astype(bf16)
        rows_ref[...] = rows
        router = dot_nt(narrow_ref[:experts, :], rows)
        place = iota((experts, TOK_MB), 0)
        chosen = [
            jnp.sum(jnp.where(ids_ref[k : k + 1, :] == place, router, 0.0), axis=0, keepdims=True)
            for k in range(TOP)
        ]
        gates_ref[0:1, :] = 1.0 / (1.0 + jnp.exp(chosen[1] - chosen[0]))
        gates_ref[1:2, :] = 1.0 / (1.0 + jnp.exp(chosen[0] - chosen[1]))
        size = block_refs[0].shape[0]
        for index, ref in enumerate(block_refs):
            for low in range(0, size, 384):
                hots = [slot_hot(slots_ref[k : k + 1, :], index * size + low, 384) for k in range(TOP)]
                pick = jnp.where(hots[0] | hots[1], 1.0, 0.0).astype(bf16)
                ref[low : low + 384, :] = dot_nn(pick, rows).astype(bf16)


def matrix_specs():
    return [
        pl.BlockSpec((1, D, D), functools.partial(lambda i, h: (i, 0, 0), i), pipeline_mode=pl.Buffered(1))
        for i in range(4)
    ]


def attend(starts, tokens, matrices, narrow, constants, ids, slots, step, blocks, experts, capacity):
    size = experts * capacity // blocks
    fixed = lambda h: (0, 0)
    out_shapes = (
        [((D, TOK_MB), bf16)] * 3
        + [((HEADS, SEQ_LEN, SEQ_LEN), bf16), ((D, TOK_MB), bf16), ((TOK_MB, D), f32), ((TOK_MB, D), bf16)]
        + [((TOP, TOK_MB), f32), ((TOK_MB, D), bf16)]
        + [((size, D), bf16)] * blocks
    )
    out_specs = [
        pl.BlockSpec((1, SEQ_LEN, SEQ_LEN), lambda h: (h, 0, 0)) if len(s) == 3 else resident(s, fixed)
        for s, _ in out_shapes
    ]
    return pl.pallas_call(
        functools.partial(attend_kernel, step=step, experts=experts),
        grid=(HEADS,),
        in_specs=[pl.BlockSpec(memory_space=pltpu.SMEM), resident((TOK_MB, D), lambda h: (step, 0))]
        + matrix_specs()
        + [resident(narrow.shape, fixed)]
        + [resident(c.shape, fixed) for c in constants]
        + [resident((TOP, TOK_MB), lambda h: (0, step)), resident((TOP, TOK_MB), fixed)],
        out_specs=out_specs,
        out_shape=[jax.ShapeDtypeStruct(*s) for s in out_shapes],
        scratch_shapes=[pltpu.VMEM((SEQ_LEN, SEQ_LEN), f32), pltpu.VMEM((16, 1024), f32)],
        compiler_params=pltpu.CompilerParams(vmem_limit_bytes=48 * MIB),
        cost_estimate=lasting(23),
        name="attend",
    )(starts, tokens, *[matrices] * 4, narrow, *constants, ids, slots)


def collect(target, direct, passed, size):
    for index, ref in enumerate(direct):
        low = 2 * index * size
        if passed is None:
            target[...] = ref[...]
        else:
            target[low : low + size, :] = ref[:size, :]
            target[low + size : low + 2 * size, :] = passed[index * size : (index + 1) * size, :]


def expert_kernel(place_ref, *refs, blocks, passes, micro):
    accumulate = micro > 0
    take = blocks + passes
    rows_refs, cot_refs, refs = refs[:take], refs[take : 2 * take], refs[2 * take :]
    other_ref, router_ref, in_ref, out_ref = refs[:4]
    refs = refs[4:]
    if accumulate:
        prior, refs = refs[:5], refs[5:]
    grads, refs = refs[:5], refs[5:]
    result_refs, back_refs = refs[:blocks], refs[blocks : 2 * blocks]
    rows, picks, rows_t, gate_column, result, back, active, inner_grad = refs[2 * blocks :]
    step, me = pl.program_id(0), place_ref[0]
    total, tile = rows.shape[0], ROW_TILE
    senders, capacity = other_ref.shape
    experts = grads[4].shape[0]
    width = capacity if passes else total
    place = iota((experts, width), 0)

    @pl.when(step == 0)
    def _():
        collect(rows, rows_refs[:blocks], rows_refs[blocks] if passes else None, width)
        for index, ref in enumerate(cot_refs[:blocks]):
            low = 2 * index * width if passes else 0
            picks[low : low + width, :] = ref[...]
            if passes:
                first = (MICRO * index + micro) * width
                picks[low + width : low + 2 * width, :] = cot_refs[blocks][first : first + width, :]
        for sender in range(senders):
            here = slice(sender * width, (sender + 1) * width)
            logits = dot_nt(router_ref[:experts, :], rows[here, :])
            other = other_ref[sender : sender + 1, :].astype(jnp.int32)
            own_logit = jnp.sum(jnp.where(place == me, logits, 0.0), axis=0, keepdims=True)
            other_logit = jnp.sum(jnp.where(place == other, logits, 0.0), axis=0, keepdims=True)
            column = row_to_column(1.0 / (1.0 + jnp.exp(other_logit - own_logit)))
            gate_column[here, :] = column
            picks[here, :] = (picks[here, :].astype(f32) * column).astype(bf16)
        for low in range(0, total, tile):
            rows_t[:, low : low + tile] = rows[low : low + tile, :].astype(f32).T.astype(bf16)
        result[...] = jnp.zeros_like(result)
        back[...] = jnp.zeros_like(back)

    def one_tile(index, carry):
        here = pl.ds(pl.multiple_of(index * tile, tile), tile)
        inner = dot_nn(rows[here, :], in_ref[0])
        square = inner * inner
        bend = jnp.tanh(inner * (0.7978845608028654 + 0.035677408136300125 * square))
        half = 0.5 * inner
        low = (half + half * bend).astype(bf16)
        active[here, :] = low
        result[here, :] += dot_nn(low, out_ref[0])
        slope = 0.5 + 0.5 * bend + half * (1.0 - bend * bend) * (0.7978845608028654 + 0.1070322244089004 * square)
        grad = (dot_nt(picks[here, :], out_ref[0]) * slope).astype(bf16)
        inner_grad[here, :] = grad
        back[here, :] += dot_nt(grad, in_ref[0])
        return carry

    lax.fori_loop(0, total // tile, one_tile, 0)

    def store(index, where, value):
        if accumulate:
            value = value + prior[index][where].astype(f32)
        grads[index][where] = value.astype(bf16)

    quarter = D // 4
    for index in range(4):
        first = pl.multiple_of((index ^ place_ref[1]) * quarter, quarter)
        store(index // 2, index % 2, dot_nn(rows_t[pl.ds(first, quarter), :], inner_grad[...]))
    outer = dot_tn(active[...], picks[...])

    @pl.when(step >= 2)
    def _():
        store(2, 0, outer)

    @pl.when(step < 2)
    def _():
        store(3, 0, outer)

    @pl.when(step == pl.num_programs(0) - 1)
    def _():
        router_sum = prior[4][...] if accumulate else jnp.zeros((experts, D), f32)
        for sender in range(senders):
            here = slice(sender * width, (sender + 1) * width)
            low = result[here, :].astype(bf16)
            score = jnp.sum(low.astype(f32) * picks[here, :].astype(f32), axis=-1, keepdims=True)
            choice = column_to_row((1.0 - gate_column[here, :]) * score)
            other = other_ref[sender : sender + 1, :].astype(jnp.int32)
            logit_grad = jnp.where(place == me, choice, 0.0) - jnp.where(place == other, choice, 0.0)
            logit_grad = logit_grad.astype(bf16)
            router_sum = router_sum + dot_nn(logit_grad, rows[here, :])
            total_back = back[here, :] + dot_tn(logit_grad, router_ref[:experts, :])
            index, first = (sender // 2, sender % 2 * width) if passes else (0, 0)
            result_refs[index][first : first + width, :] = low
            back_refs[index][first : first + width, :] = total_back.astype(bf16)
        grads[4][...] = router_sum


def run_expert(place, rows_blocks, cot_blocks, other, narrow, expert_in, expert_out, prior, micro, blocks, experts):
    passes = len(rows_blocks) - blocks
    size = rows_blocks[0].shape[0]
    total = blocks * size
    chunk, quarter = FF // 4, D // 4
    fixed = lambda i, place: (0, 0)
    at = lambda i, place: i ^ 2 ^ place[2]
    weights = [
        pl.BlockSpec((1, D, chunk), lambda i, place: (0, 0, at(i, place))),
        pl.BlockSpec((1, chunk, D), lambda i, place: (0, at(i, place), 0)),
    ]
    grad_specs = [
        pl.BlockSpec((2, quarter, chunk), lambda i, place: (0, 0, at(i, place))),
        pl.BlockSpec((2, quarter, chunk), lambda i, place: (0, 0, at(i, place))),
        pl.BlockSpec((1, chunk, D), lambda i, place: (jnp.maximum(i - 2, 0), 0, 0)),
        pl.BlockSpec((1, chunk, D), lambda i, place: (jnp.minimum(i, 1), 0, 0)),
        resident((experts, D), fixed),
    ]
    grad_shapes = [((2, quarter, FF), bf16)] * 2 + [((2, chunk, D), bf16)] * 2 + [((experts, D), f32)]
    wide = resident((size, D), fixed)
    taken = [wide] * blocks + [resident((blocks * (size // 2), D), fixed)] * passes
    cot_size = size // (1 + passes)
    taken += [resident((cot_size, D), lambda i, place: (micro, 0))] * blocks
    taken += [resident((MICRO * blocks * cot_size, D), fixed)] * passes
    out = pl.pallas_call(
        functools.partial(expert_kernel, blocks=blocks, passes=passes, micro=micro),
        grid_spec=pltpu.PrefetchScalarGridSpec(
            num_scalar_prefetch=1,
            grid=(4,),
            in_specs=taken
            + [resident(other.shape, fixed), resident(narrow.shape, fixed)]
            + weights
            + (grad_specs if prior else []),
            out_specs=grad_specs + [wide] * (2 * blocks),
            scratch_shapes=[
                pltpu.VMEM((total, D), bf16),
                pltpu.VMEM((total, D), bf16),
                pltpu.VMEM((D, total), bf16),
                pltpu.VMEM((total, 1), f32),
                pltpu.VMEM((total, D), f32),
                pltpu.VMEM((total, D), f32),
                pltpu.VMEM((total, chunk), bf16),
                pltpu.VMEM((total, chunk), bf16),
            ],
        ),
        out_shape=[jax.ShapeDtypeStruct(*s) for s in grad_shapes]
        + [jax.ShapeDtypeStruct((size, D), bf16)] * (2 * blocks),
        compiler_params=pltpu.CompilerParams(vmem_limit_bytes=62 * MIB),
        cost_estimate=lasting(62),
        name="expert",
    )(place, *rows_blocks, *cot_blocks, other, narrow, expert_in, expert_out, *(prior or ()))
    return out[:5], out[5 : 5 + blocks], out[5 + blocks :]


def trade(value, groups, mask):
    return lax.ppermute(value, "group", swap(groups, mask))


def add_low(left, right):
    return (left.astype(f32) + right.astype(f32)).astype(bf16)


def first_half(keep, send_away, groups, mask):
    return add_low(keep, trade(send_away, groups, mask))


def second_half(half, groups, mask):
    return half[0], half[1], trade(half[1], groups, mask)


def doubled(kept, _, received, groups, first, second):
    own = add_low(kept, received)
    beside = trade(own, groups, second)
    far = trade(jnp.stack([own, beside]), groups, first)
    return own[None], beside[None], far


def spread_kernel(place_ref, own_ref, beside_ref, far_ref, out_ref, *, code):
    index = pl.program_id(0) ^ place_ref[code]

    @pl.when(index == 0)
    def _():
        out_ref[...] = own_ref[...].astype(f32)

    @pl.when(index == 1)
    def _():
        out_ref[...] = beside_ref[...].astype(f32)

    @pl.when(index > 1)
    def _():
        out_ref[...] = far_ref[...].astype(f32)


def spread_pieces(place, pieces, code):
    shape = pieces[0].shape[1:]
    block = (1, *shape)
    return pl.pallas_call(
        functools.partial(spread_kernel, code=code),
        grid_spec=pltpu.PrefetchScalarGridSpec(
            num_scalar_prefetch=1,
            grid=(4,),
            in_specs=[pl.BlockSpec(block, lambda i, place: (0, 0, 0))] * 2
            + [pl.BlockSpec(block, lambda i, place: ((i ^ place[code]) & 1, 0, 0))],
            out_specs=pl.BlockSpec(block, lambda i, place: (i, 0, 0)),
        ),
        out_shape=jax.ShapeDtypeStruct((4, *shape), f32),
        compiler_params=pltpu.CompilerParams(vmem_limit_bytes=32 * MIB),
        cost_estimate=lasting(6),
        name="spread",
    )(place, *pieces)


def back_kernel(*refs, blocks, passes, experts, devices, final):
    me_ref, refs = refs[0], refs[1:]
    take = blocks + passes
    back_refs, refs = refs[:take], refs[take:]
    (x_ref, cot_ref, query_w, key_w, value_w, out_w, narrow_ref, hot_ref, bucket_ref, heads_ref, slots_ref) = refs[:11]
    (query_ref, key_ref, value_ref, probs_ref, attended_ref, hidden_ref, normed_ref) = refs[11:18]
    refs = refs[18:]
    if final:
        prior, router_grad, refs = refs[: 1 + passes], refs[1 + passes], refs[2 + passes :]
    token_ref, dense_refs, refs = refs[0], refs[1 : 2 + passes], refs[2 + passes :]
    gathered, hidden_grad, out_grad, query_grad, key_grad, value_grad, whole, lines, diagonals = refs
    head = pl.program_id(0)
    total = gathered.shape[0]

    def dense(first, value):
        columns = slice(first, first + value.shape[1])
        if not passes:
            if final:
                value = value + prior[0][:, columns].astype(f32)
            dense_refs[0][:, columns] = value.astype(bf16)
            return
        whole[:, : value.shape[1]] = value
        rows = D // devices
        for k in range(devices):
            start = pl.multiple_of((me_ref[0] ^ k) * rows, 32)
            piece = whole[pl.ds(start, rows), : value.shape[1]]
            here = slice(k // 2 * rows, (k // 2 + 1) * rows)
            if final:
                piece = piece + prior[k % 2][here, columns].astype(f32)
            dense_refs[k % 2][here, columns] = piece.astype(bf16)

    @pl.when(head == 0)
    def _():
        lines[...] = jnp.zeros_like(lines)
        diagonals[...] = jnp.zeros_like(diagonals)
        cot = cot_ref[...].astype(f32)
        collect(gathered, back_refs[:blocks], back_refs[blocks] if passes else None, back_refs[0].shape[0] // 2)
        columns = [row_to_column(slots_ref[k : k + 1, :].astype(f32)).astype(jnp.int32) for k in range(TOP)]
        rows_grad = jnp.zeros((TOK_MB, D), f32)
        for low in range(0, total, 512):
            place = iota((TOK_MB, 512), 1) + low
            pick = jnp.where((place == columns[0]) | (place == columns[1]), 1.0, 0.0).astype(bf16)
            rows_grad = rows_grad + dot_nn(pick, gathered[low : low + 512, :])
        hidden = hidden_ref[...]
        scale = lax.rsqrt(jnp.mean(hidden * hidden, axis=-1, keepdims=True) + epsilon)
        normal = hidden * scale
        lines[experts + 1 : experts + 2, :] = jnp.sum(rows_grad * normal, axis=0, keepdims=True)
        scaled = rows_grad * narrow_ref[experts + 1 : experts + 2, :].astype(f32)
        total_grad = cot + scale * (scaled - normal * jnp.mean(scaled * normal, axis=-1, keepdims=True))
        hidden_grad[...] = total_grad
        branch = total_grad.astype(bf16)
        dense(3 * D, dot_nn(attended_ref[...], branch))
        out_grad[...] = dot_nt(out_w[0], branch).astype(bf16)

    span = pl.ds(pl.multiple_of(head * HEAD_DIM, HEAD_DIM), HEAD_DIM)
    low = probs_ref[0]
    grad_here = out_grad[span, :]
    probs = low.astype(f32)
    value_grad[span, :] = dot_nt(grad_here, low).astype(bf16)
    prob_grad = dot_tn(value_ref[span, :], grad_here)
    center = jnp.sum(probs * prob_grad, axis=0, keepdims=True)
    score_grad = (probs * (prob_grad - center)).astype(bf16)
    query_grad[span, :] = (dot_nn(key_ref[span, :], score_grad) * HEAD_DIM**-0.5).astype(bf16)
    key_grad[span, :] = dot_nt(query_ref[span, :], score_grad).astype(bf16)
    wide = score_grad.astype(f32)
    pieces = []
    for a in range(4):
        piece = wide[a * 128 : a * 128 + 128, :]
        left, right = 384 - a * 128, 128 + a * 128
        ends = [jnp.zeros((128, left), f32)] if left else []
        pieces.append(jnp.concatenate(ends + [piece, jnp.zeros((128, right), f32)], axis=1))
    folded = pieces[0] + pieces[1] + pieces[2] + pieces[3]
    for half in (64, 32, 16, 8):
        folded = folded[:half] + pltpu.roll(folded[half:], 1024 - half, 1)
    low_row = iota((8, 1024), 0)
    for bit in (4, 2, 1):
        folded = jnp.where((low_row & bit) != 0, pltpu.roll(folded, 1024 - bit, 1), folded)
    diagonals[pl.ds(head, 1), :] = jnp.sum(folded, axis=0, keepdims=True)

    @pl.when(head == HEADS - 1)
    def _():
        normed_t = normed_ref[...].astype(f32).T.astype(bf16)
        grads = (query_grad[...], key_grad[...], value_grad[...])
        in_grad = jnp.zeros((D, TOK_MB), f32)
        for i, (grad, weight) in enumerate(zip(grads, (query_w, key_w, value_w))):
            dense(i * D, dot_nt(normed_t, grad))
            in_grad = in_grad + dot_nn(weight[0], grad)
        in_grad = in_grad.T
        x = x_ref[...].astype(f32)
        scale = lax.rsqrt(jnp.mean(x * x, axis=-1, keepdims=True) + epsilon)
        normal = x * scale
        lines[experts : experts + 1, :] = jnp.sum(in_grad * normal, axis=0, keepdims=True)
        scaled = in_grad * narrow_ref[experts : experts + 1, :].astype(f32)
        grad = hidden_grad[...] + scale * (scaled - normal * jnp.mean(scaled * normal, axis=-1, keepdims=True))
        token_ref[...] = grad.astype(bf16)
        if final:
            lines[:experts, :] = router_grad[...]
        by_bucket = sum_dot(diagonals[...], hot_ref[...], dot_nt)
        by_place = sum_dot(by_bucket, bucket_ref[...], dot_nt)
        lines[experts + 2 : experts + 3, :] = jnp.sum(by_place * heads_ref[...].astype(f32), axis=0, keepdims=True)
        dense(4 * D, lines[...].T)


def sum_dot(values, hot, dot):
    high = values.astype(bf16)
    return dot(high, hot) + dot((values - high.astype(f32)).astype(bf16), hot)


def backward(me, back_blocks, tokens, cotangent, matrices, narrow, constants, slots, saved, prior, step, blocks, experts, devices):
    passes = len(back_blocks) - blocks
    size = back_blocks[0].shape[0]
    fixed = lambda h: (0, 0)
    block = lambda h: (step, 0)
    head_block = pl.BlockSpec((1, SEQ_LEN, SEQ_LEN), lambda h: (h, 0, 0))
    wide = 4 * D + 128
    dense_shapes = [(D // (1 + passes), wide)] * (1 + passes)
    dense_specs = [resident(s, fixed) for s in dense_shapes]
    return pl.pallas_call(
        functools.partial(
            back_kernel, blocks=blocks, passes=passes, experts=experts, devices=devices, final=prior is not None
        ),
        grid=(HEADS,),
        in_specs=[pl.BlockSpec(memory_space=pltpu.SMEM)]
        + [resident(b.shape, fixed) for b in back_blocks]
        + [resident((TOK_MB, D), block)] * 2
        + matrix_specs()
        + [resident(narrow.shape, fixed)]
        + [resident(c.shape, fixed) for c in constants]
        + [resident((TOP, TOK_MB), fixed)]
        + [head_block if s.ndim == 3 else resident(s.shape, fixed) for s in saved]
        + (dense_specs + [resident((experts, D), fixed)] if prior else []),
        out_specs=[resident((TOK_MB, D), fixed)] + dense_specs,
        out_shape=[jax.ShapeDtypeStruct((TOK_MB, D), bf16)] + [jax.ShapeDtypeStruct(s, bf16) for s in dense_shapes],
        scratch_shapes=[
            pltpu.VMEM((blocks * size, D), bf16),
            pltpu.VMEM((TOK_MB, D), f32),
            pltpu.VMEM((D, TOK_MB), bf16),
            pltpu.VMEM((D, TOK_MB), bf16),
            pltpu.VMEM((D, TOK_MB), bf16),
            pltpu.VMEM((D, TOK_MB), bf16),
            pltpu.VMEM((D, D), f32),
            pltpu.VMEM((128, D), f32),
            pltpu.VMEM((16, 1024), f32),
        ],
        compiler_params=pltpu.CompilerParams(vmem_limit_bytes=58 * MIB),
        cost_estimate=lasting(34),
        name="backward",
    )(me, *back_blocks, tokens, cotangent, *[matrices] * 4, narrow, *constants, slots, *saved, *(prior or ()))


def combine_kernel(*refs, blocks, passes):
    result_refs = refs[: blocks + passes]
    hidden_ref, slots_ref, gates_ref, mixed_ref, gathered = refs[blocks + passes :]
    collect(gathered, result_refs[:blocks], result_refs[blocks] if passes else None, result_refs[0].shape[0] // 2)
    slots = [row_to_column(slots_ref[k : k + 1, :].astype(f32)).astype(jnp.int32) for k in range(TOP)]
    gates = [row_to_column(gates_ref[k : k + 1, :]) for k in range(TOP)]
    output = hidden_ref[...]
    for k in range(TOP):
        picked = jnp.zeros((TOK_MB, D), f32)
        for low in range(0, gathered.shape[0], 512):
            pick = jnp.where(iota((TOK_MB, 512), 1) + low == slots[k], 1.0, 0.0).astype(bf16)
            picked = picked + dot_nn(pick, gathered[low : low + 512, :])
        output = output + gates[k] * picked
    mixed_ref[...] = output.astype(bf16)


def combine(result_blocks, hidden, slots, gates, blocks):
    total = blocks * result_blocks[0].shape[0]
    return pl.pallas_call(
        functools.partial(combine_kernel, blocks=blocks, passes=len(result_blocks) - blocks),
        out_shape=jax.ShapeDtypeStruct((TOK_MB, D), bf16),
        scratch_shapes=[pltpu.VMEM((total, D), bf16)],
        compiler_params=pltpu.CompilerParams(vmem_limit_bytes=32 * MIB),
        cost_estimate=lasting(3),
        name="combine",
    )(*result_blocks, hidden, slots, gates)


def tie(values, *after):
    count = len(values)
    return list(lax.optimization_barrier((*values, *after)))[:count]


def send(blocks, devices):
    if len(blocks) == 1:
        whole = blocks[0]
        moved = whole.reshape(devices, -1, D)
        moved = lax.all_to_all(moved, "expert", split_axis=0, concat_axis=0, tiled=True)
        return [moved.reshape(whole.shape)]
    return [blocks[0]] + [
        lax.ppermute(blocks[j], "expert", swap(devices, 2 * j)) for j in range(1, len(blocks))
    ]


def pass_on(blocks, devices):
    if len(blocks) == 1:
        return blocks
    half = blocks[0].shape[0] // 2
    second = jnp.concatenate([b[half:] for b in blocks], axis=0)
    return [*blocks, lax.ppermute(second, "expert", swap(devices, 1))]


def reduce_dense(pieces, devices):
    if len(pieces) == 1:
        return lax.psum_scatter(pieces[0], "expert", scatter_dimension=0, tiled=True).astype(f32)
    near, cross = pieces
    chips = devices // 2
    rows = near.shape[0] // chips
    summed = near.astype(f32) + lax.ppermute(cross, "expert", swap(devices, 1)).astype(f32)
    low = summed.astype(bf16)
    total = summed[:rows]
    for j in range(1, chips):
        total = total + lax.ppermute(low[j * rows : (j + 1) * rows], "expert", swap(devices, 2 * j)).astype(f32)
    return total


def reduce_group(total, groups):
    mask = 1
    while mask < groups:
        low = total.astype(bf16)
        total = low.astype(f32) + lax.ppermute(low, "group", swap(groups, mask)).astype(f32)
        mask *= 2
    return total


def shards(
    tokens, cotangent, norm_attn, w_query, w_key, w_value, w_out, rel_bias, norm_expert, w_router,
    expert_in, expert_out, expert_ids, span_starts,
):
    experts = w_router.shape[1]
    capacity = 3 * TOK_MB * TOP // (2 * experts)
    groups, devices = lax.axis_size("group"), lax.axis_size("expert")
    direct = devices <= DIRECT_MAX
    blocks = devices // 2 if direct else 1
    shard, share = w_query.shape[0], rel_bias.shape[0]
    me = lax.axis_index("expert").reshape(1).astype(jnp.int32)
    order = me if direct else jnp.zeros_like(me)
    ids = expert_ids.T
    group = lax.axis_index("group").reshape(1).astype(jnp.int32)
    place = jnp.concatenate([me, group % 2 * 2 + group // 2, group])

    padded = jnp.pad(rel_bias, (0, shard - share))
    narrow = jnp.concatenate([w_router.T, norm_attn[None], norm_expert[None], padded[None]], axis=0)
    matrices, narrow, all_ids = gather_weights(
        (w_query, w_key, w_value, w_out), narrow, ids, groups, devices
    )
    bucket, heads = bias_places(devices)
    constants = (bucket_hot().astype(bf16), bucket.astype(bf16), heads.astype(bf16))

    slots, *cots = route(order, ids, cotangent, blocks, experts, capacity)
    if not direct:
        cots = cots[0].reshape(MICRO, devices, capacity, D).transpose(1, 0, 2, 3).reshape(-1, D)
        cots = send([cots], devices)[0].reshape(devices, MICRO, capacity, D).transpose(1, 0, 2, 3).reshape(-1, D)
        cots = [cots]
    else:
        cots = send(cots, devices)
    other = partners(me, all_ids, devices, capacity, direct)
    if not direct:
        other = other.reshape(MICRO, 1, devices * capacity)
    saved, sent = [], []
    for step in range(MICRO):
        out = attend(
            span_starts, tokens, matrices, narrow, constants, ids, slots[step], step, blocks, experts, capacity
        )
        saved.append(out[:9])
        sent.append(out[9:])
    cots = tie(cots, saved[0][0], saved[1][0])
    sent[0] = send(tie(sent[0], *cots[1:]), devices)
    sent[1] = send(tie(sent[1], *sent[0][1:]), devices)
    cots = pass_on(cots, devices)
    sent[0] = pass_on(sent[0], devices)

    grads, result, back = run_expert(
        place, sent[0], cots, other[0], narrow, expert_in, expert_out, None, 0, blocks, experts
    )
    sent[1] = pass_on(tie(sent[1], back[0]), devices)
    backs, results = [send(back, devices)], [result]
    grads, result, back = run_expert(
        place, sent[1], cots, other[1], narrow, expert_in, expert_out, grads, 1, blocks, experts
    )
    results.append(result)
    inward = first_half(grads[0], grads[1], groups, 1)
    outward = first_half(grads[2], grads[3], groups, 2)
    backs[0] = pass_on(tie(backs[0], back[0]), devices)
    backs.append(send(tie(back, *backs[0]), devices))

    def run_back(step, prior):
        query, key, value, probs, attended, hidden, _, _, normed = saved[step]
        return backward(
            order, backs[step], tokens, cotangent, matrices, narrow, constants, slots[step],
            (query, key, value, probs, attended, hidden, normed), prior, step, blocks, experts, devices,
        )

    token_grads = [None, None]
    token_grads[0], *dense = run_back(0, None)
    backs[1] = pass_on(tie(backs[1], token_grads[0]), devices)
    results[0] = send(tie(results[0], *backs[1]), devices)
    backs[1] = tie(backs[1], inward, outward)
    inward = second_half(inward, groups, 2)
    outward = second_half(outward, groups, 1)
    token_grads[1], *dense = run_back(1, (*dense, grads[4]))
    results[0] = tie(results[0], token_grads[1])
    total = reduce_dense(tie(dense, *results[0][1:]), devices)
    results[1] = send(tie(results[1], total), devices)
    inward = doubled(*inward, groups, 1, 2)
    outward = doubled(*outward, groups, 2, 1)
    total = reduce_group(total, groups)
    mixed = [
        combine(pass_on(results[step], devices), saved[step][5], slots[step], saved[step][7], blocks)
        for step in range(MICRO)
    ]
    thin = total[:, 4 * D :]
    grad_in = spread_pieces(place, inward, 1).reshape(expert_in.shape)
    grad_out = spread_pieces(place, outward, 2).reshape(expert_out.shape)
    return (
        jnp.concatenate(mixed, axis=0),
        jnp.concatenate(token_grads, axis=0),
        thin[:, experts],
        total[:, :D],
        total[:, D : 2 * D],
        total[:, 2 * D : 3 * D],
        total[:, 3 * D : 4 * D],
        thin[:share, experts + 2],
        thin[:, experts + 1],
        thin[:, :experts],
        grad_in,
        grad_out,
    )


def solution(mesh):
    rows, split = P(("group", "expert"), None), P("expert", None)
    stacked = P("expert", None, None)
    return jax.shard_map(
        shards,
        mesh=mesh,
        in_specs=(
            rows, rows, P("expert"), split, split, split, split, P("expert"), P("expert"), split,
            stacked, stacked, rows, P(("group", "expert")),
        ),
        out_specs=(
            rows, rows, P("expert"), split, split, split, split, P("expert"), P("expert"), split, stacked, stacked,
        ),
        check_vma=False,
    )
```

time: 1250 us -> 669 us (0.54)
  matrix products: 326 us -> 0 us
  blocking collectives: 284 us -> 0 us
  Pallas kernels: 0 us -> 274 us
  local copies, waits for them, and re-layouts: 207 us -> 48.8 us
  other arithmetic: 116 us -> 15.9 us
  between operations: 20.2 us -> 2.12 us
  starting transfers between devices: 35.1 us -> 51.9 us
  waiting for transfers between devices: 254 us -> 267 us
    dot_general x61 -> x0, matrix products: 326 us -> none  [the longest x2 43.3 us: shards(): jnp.einsum('sjcd,jfd->sjcf', grouped_grad, expert_out, preferred_element_...]
    pallas_call x0 -> x13, Pallas kernels: none -> 274 us  [the longest x2 136 us: run_expert(): pl.pallas_call(functools.partial(expert_kernel, blocks=blocks, passes=pas...]
    ppermute x0 -> x49, waiting for transfers between devices: none -> 267 us  [the longest x21 122 us: send(): lax.ppermute(blocks[j], 'expert', swap(devices, 2 * j))]
    all_to_all x3 -> x0, blocking collectives: 176 us -> none  [the longest x2 118 us: shards(): lax.all_to_all(outgoing, 'expert', split_axis=0, concat_axis=0, tiled=True)]
    all_to_all x5 -> x0, waiting for transfers between devices: 150 us -> none  [the longest x2 74.8 us: shards(): lax.all_to_all(row_grad.reshape(senders * local_experts, capacity, D), 'e...]
    psum x1 -> x0, waiting for transfers between devices: 80.5 us -> none  [shards(): lax.psum(dense_total[1].astype(jnp.bfloat16), 'group').astype(jnp.float32)]
    unnamed x271 -> x141, local copies, waits for them, and re-layouts: 94.9 us -> 16.1 us
    all_gather x1 -> x0, blocking collectives: 56.7 us -> none  [shards(): lax.all_gather(w_router, 'expert', axis=0, tiled=True)]
  transfers between devices with their start and end apart: 15 -> 49, of which waited for: 6 -> 22; matrix products, arithmetic and copies ran while one was open for 31% -> 4% of each run, Pallas kernels for 0% -> 41%
where the time goes in v1:
time: 669 us; the launch traced here: 659 us
  Pallas kernels  274 us (41%)
  waiting for transfers between devices  267 us (40%)
  starting transfers between devices  51.9 us (8%)
  local copies, waits for them, and re-layouts  48.8 us (7%)
  other arithmetic  15.9 us (2%)
    pallas_call x2, Pallas kernels, run_expert(): pl.pallas_call(functools.partial(expert_kernel, blocks=blocks, passes=pas...  136 us
    ppermute x21, waiting for transfers between devices, send(): lax.ppermute(blocks[j], 'expert', swap(devices, 2 * j))  122 us
    pallas_call x2, Pallas kernels, backward(): pl.pallas_call(functools.partial(back_kernel, blocks=blocks, passes=passe...  68.2 us
    ppermute x8, waiting for transfers between devices, trade(): return lax.ppermute(value, 'group', swap(groups, mask))  46.5 us
    pallas_call x2, Pallas kernels, attend(): pl.pallas_call(functools.partial(attend_kernel, step=step, experts=expert...  46.2 us
    ppermute x2, waiting for transfers between devices, reduce_group(): lax.ppermute(low, 'group', swap(groups, mask)).astype(f32)  32.7 us
    ppermute x21, starting transfers between devices, send(): lax.ppermute(blocks[j], 'expert', swap(devices, 2 * j))  26.6 us
    ppermute x3, waiting for transfers between devices, reduce_dense(): lax.ppermute(low[j * rows:(j + 1) * rows], 'expert', swap(devices, 2 * j))  25.4 us
  transfers between devices with their start and end apart: 49, of which 22 were waited for; matrix products, arithmetic and copies ran while one was open for 4% of the time, Pallas kernels for 41%

profile of v1, /device:TPU:8, one launch (start us, length us, event | category | flops | bytes accessed | tf_op | source)
XLA Modules:
  0.0 659.1 jit_solution(18032558142736422871)
XLA Ops:
  7.9 10.4 %collective-permute-done.2 = bf16[112,768]{1,0:T(8,128)(2,1)S(1)} collective-permute-done((bf16[112,768]{1,0:T(8,128)(2,1)S(1)}, bf16[112,768]{1,0:T(8,128)(2,1)S(1)}, u32[]{:S(2)}, u32[]{:S(2)}) %collective-permute-start.2) | collective-permute-done | bytes 172064 | tf_op jit(solution)/shard_map/ppermute | solution.py:217
  24.6 12.9 %collective-permute-done.5.refs_3_ = bf16[384,768]{1,0:T(8,128)(2,1)S(1)} collective-permute-done((bf16[384,768]{1,0:T(8,128)(2,1)S(1)}, bf16[384,768]{1,0:T(8,128)(2,1)S(1)}, u32[]{:S(2)}, u32[]{:S(2)}) %collective-permute-start.5) | collective-permute-done | bytes 589856 | tf_op jit(solution)/shard_map/ppermute | solution.py:220
  37.5 10.5 %collective-permute-done.4.refs_2_ = bf16[384,768]{1,0:T(8,128)(2,1)S(1)} collective-permute-done((bf16[384,768]{1,0:T(8,128)(2,1)S(1)}, bf16[384,768]{1,0:T(8,128)(2,1)S(1)}, u32[]{:S(2)}, u32[]{:S(2)}) %collective-permute-start.4) | collective-permute-done | bytes 589856 | tf_op jit(solution)/shard_map/ppermute | solution.py:220
  48.3 14.1 %concatenate.53 = bf16[1600,768]{1,0:T(8,128)(2,1)} concatenate(bf16[96,768]{1,0:T(8,128)(2,1)S(1)} %select_select_fusion, bf16[96,768]{1,0:T(8,128)(2,1)S(1)} %slice.225, bf16[96,768]{1,0:T(8,128)(2,1)S(1)} %slice.226, bf16[96,768]{1,0:T(8,128)(2,1)S(1)} %slice.227, bf16[384,768]{1,0:T(8,128)(2,1)} %collective-permute-done.3.refs_1_, ...), dimensions={0} | concatenate | bytes 4915200 | tf_op jit(solution)/shard_map/concatenate | solution.py:221
  62.5 4.2 route.1
  80.0 22.7 %attend.2 = (bf16[768,512]{1,0:T(8,128)(2,1)S(1)}, bf16[768,512]{1,0:T(8,128)(2,1)S(1)}, bf16[768,512]{1,0:T(8,128)(2,1)S(1)}, bf16[12,512,512]{2,1,0:T(8,128)(2...) custom-call(s32[2]{0:T(128)S(1)} %copy-done.43, ...), custom_call_target="tpu_custom_call" | custom-call | bytes 82800000 | tf_op jit(solution)/shard_map/attend/pallas_call | solution.py:339
  106.2 23.5 %attend.3 = (bf16[768,512]{1,0:T(8,128)(2,1)S(1)}, bf16[768,512]{1,0:T(8,128)(2,1)S(1)}, bf16[768,512]{1,0:T(8,128)(2,1)S(1)}, bf16[12,512,512]{2,1,0:T(8,128)(2...) custom-call(s32[2]{0:T(128)S(1)} %copy-done.43, ...), custom_call_target="tpu_custom_call" | custom-call | bytes 82800000 | tf_op jit(solution)/shard_map/attend/pallas_call | solution.py:339
  129.8 17.5 %collective-permute-done.8.refs_7_ = bf16[768,768]{1,0:T(8,128)(2,1)} collective-permute-done((bf16[768,768]{1,0:T(8,128)(2,1)}, bf16[768,768]{1,0:T(8,128)(2,1)}, u32[]{:S(2)}, u32[]{:S(2)}) %collective-permute-start.8) | collective-permute-done | bytes 1179680 | tf_op jit(solution)/shard_map/ppermute | solution.py:764
  147.2 26.0 %collective-permute-done.9.refs_8_ = bf16[768,768]{1,0:T(8,128)(2,1)} collective-permute-done((bf16[768,768]{1,0:T(8,128)(2,1)}, bf16[768,768]{1,0:T(8,128)(2,1)}, u32[]{:S(2)}, u32[]{:S(2)}) %collective-permute-start.9) | collective-permute-done | bytes 1179680 | tf_op jit(solution)/shard_map/ppermute | solution.py:764
  176.9 2.8 collective-permute-start.11
  180.4 22.1 %collective-permute-done.10.refs_1_ = bf16[384,768]{1,0:T(8,128)(2,1)S(1)} collective-permute-done((bf16[384,768]{1,0:T(8,128)(2,1)S(1)}, bf16[384,768]{1,0:T(8,128)(2,1)S(1)}, u32[]{:S(2)}, u32[]{:S(2)}) %collective-permute-start.10) | collective-permute-done | bytes 589856 | tf_op jit(solution)/shard_map/ppermute | solution.py:764
  202.5 16.3 %collective-permute-done.11.refs_2_ = bf16[384,768]{1,0:T(8,128)(2,1)S(1)} collective-permute-done((bf16[384,768]{1,0:T(8,128)(2,1)S(1)}, bf16[384,768]{1,0:T(8,128)(2,1)S(1)}, u32[]{:S(2)}, u32[]{:S(2)}) %collective-permute-start.11) | collective-permute-done | bytes 589856 | tf_op jit(solution)/shard_map/ppermute | solution.py:764
  218.8 12.9 %collective-permute-done.12.refs_3_ = bf16[384,768]{1,0:T(8,128)(2,1)S(1)} collective-permute-done((bf16[384,768]{1,0:T(8,128)(2,1)S(1)}, bf16[384,768]{1,0:T(8,128)(2,1)S(1)}, u32[]{:S(2)}, u32[]{:S(2)}) %collective-permute-start.12) | collective-permute-done | bytes 589856 | tf_op jit(solution)/shard_map/ppermute | solution.py:764
  239.0 66.5 %expert.2 = (bf16[2,192,3072]{2,1,0:T(8,128)(2,1)}, bf16[2,192,3072]{2,1,0:T(8,128)(2,1)}, bf16[2,768,768]{2,1,0:T(8,128)(2,1)}, bf16[2,768,768]{2,1,0:T(8,128)(...) custom-call(s32[3]{0:T(128)} %pad_add_fusion.place_ref, ...), custom_call_target="tpu_custom_call" | custom-call | bytes 223200000 | tf_op jit(solution)/shard_map/expert/pallas_call | solution.py:486
  312.4 69.0 %expert.3 = (bf16[2,192,3072]{2,1,0:T(8,128)(2,1)}, bf16[2,192,3072]{2,1,0:T(8,128)(2,1)}, bf16[2,768,768]{2,1,0:T(8,128)(2,1)}, bf16[2,768,768]{2,1,0:T(8,128)(...) custom-call(s32[3]{0:T(128)} %pad_add_fusion.place_ref, ...), custom_call_target="tpu_custom_call" | custom-call | bytes 223200000 | tf_op jit(solution)/shard_map/expert/pallas_call | solution.py:486
  391.8 32.8 %backward.2 = (bf16[512,768]{1,0:T(8,128)(2,1)}, bf16[384,3200]{1,0:T(8,128)(2,1)}, bf16[384,3200]{1,0:T(8,128)(2,1)}) custom-call(s32[1]{0:T(128)} %bitcast.me_ref.refs_0_, bf16[384,768]{1,0:T(8,128)(2,1)} %get-tuple-element.174.refs_1_, bf16[384,768]{1,0:T(8,128)(2,1)} %copy-done.55, bf16[384,768]{1,0:T(8,128)(2,1)} %collective-permute-done.20.refs_3_, ...), custom_call_target="tpu_custom_call" | custom-call | bytes 122400000 | tf_op jit(solution)/shard_map/backward/pallas_call | solution.py:691
  424.6 4.1 collective-permute-done.24.refs_3_
  428.7 12.8 %collective-permute-done.25.refs_4_ = bf16[384,768]{1,0:T(8,128)(2,1)S(1)} collective-permute-done((bf16[384,768]{1,0:T(8,128)(2,1)S(1)}, bf16[384,768]{1,0:T(8,128)(2,1)S(1)}, u32[]{:S(2)}, u32[]{:S(2)}) %collective-permute-start.25) | collective-permute-done | bytes 589856 | tf_op jit(solution)/shard_map/ppermute | solution.py:764
  446.2 2.9 collective-permute-start.28
  449.7 4.1 add_convert_fusion.1
  456.0 35.3 %backward.3 = (bf16[512,768]{1,0:T(8,128)(2,1)}, bf16[384,3200]{1,0:T(8,128)(2,1)}, bf16[384,3200]{1,0:T(8,128)(2,1)}) custom-call(s32[1]{0:T(128)} %bitcast.me_ref.refs_0_, bf16[384,768]{1,0:T(8,128)(2,1)} %get-tuple-element.201.refs_1_, bf16[384,768]{1,0:T(8,128)(2,1)} %copy-done.56, bf16[384,768]{1,0:T(8,128)(2,1)} %copy-done.57, ...), custom_call_target="tpu_custom_call" | custom-call | bytes 122400000 | tf_op jit(solution)/shard_map/backward/pallas_call | solution.py:691
  491.4 9.5 %collective-permute-done.29.refs_3_ = bf16[384,768]{1,0:T(8,128)(2,1)S(1)} collective-permute-done((bf16[384,768]{1,0:T(8,128)(2,1)}, bf16[384,768]{1,0:T(8,128)(2,1)S(1)}, u32[]{:S(2)}, u32[]{:S(2)}) %collective-permute-start.29) | collective-permute-done | bytes 589856 | tf_op jit(solution)/shard_map/ppermute | solution.py:764
  505.0 25.7 %collective-permute-done.43 = bf16[192,3072]{1,0:T(8,128)(2,1)S(1)} collective-permute-done((bf16[192,3072]{1,0:T(8,128)(2,1)S(1)}, bf16[192,3072]{1,0:T(8,128)(2,1)S(1)}, u32[]{:S(2)}, u32[]{:S(2)}) %collective-permute-start.43) | collective-permute-done | bytes 1179680 | tf_op jit(solution)/shard_map/ppermute | solution.py:517
  536.2 2.9 collective-permute-start.35
  539.2 19.4 %collective-permute-done.44 = bf16[192,3072]{1,0:T(8,128)(2,1)S(1)} collective-permute-done((bf16[192,3072]{1,0:T(8,128)(2,1)S(1)}, bf16[192,3072]{1,0:T(8,128)(2,1)S(1)}, u32[]{:S(2)}, u32[]{:S(2)}) %collective-permute-start.44) | collective-permute-done | bytes 1179680 | tf_op jit(solution)/shard_map/ppermute | solution.py:517
  562.5 15.4 %collective-permute-done.36 = bf16[96,3200]{1,0:T(8,128)(2,1)S(1)} collective-permute-done((bf16[96,3200]{1,0:T(8,128)(2,1)S(1)}, bf16[96,3200]{1,0:T(8,128)(2,1)S(1)}, u32[]{:S(2)}, u32[]{:S(2)}) %collective-permute-start.36) | collective-permute-done | bytes 614432 | tf_op jit(solution)/shard_map/ppermute | solution.py:786
  577.9 10.0 %collective-permute-done.35 = bf16[96,3200]{1,0:T(8,128)(2,1)S(1)} collective-permute-done((bf16[96,3200]{1,0:T(8,128)(2,1)S(1)}, bf16[96,3200]{1,0:T(8,128)(2,1)S(1)}, u32[]{:S(2)}, u32[]{:S(2)}) %collective-permute-start.35) | collective-permute-done | bytes 614432 | tf_op jit(solution)/shard_map/ppermute | solution.py:786
  593.0 32.7 %collective-permute-done.41 = bf16[96,3200]{1,0:T(8,128)(2,1)S(1)} collective-permute-done((bf16[96,3200]{1,0:T(8,128)(2,1)S(1)}, bf16[96,3200]{1,0:T(8,128)(2,1)S(1)}, u32[]{:S(2)}, u32[]{:S(2)}) %collective-permute-start.41) | collective-permute-done | bytes 614432 | tf_op jit(solution)/shard_map/ppermute | solution.py:794
  630.1 3.0 combine.2
  633.1 4.5 spread.3
  637.6 4.5 spread.2
  653.2 4.2 combine.3
  (298 shorter events, 102.1 us)
Async XLA Ops:
  66.7 63.1 %collective-permute-start.7 = (bf16[768,768]{1,0:T(8,128)(2,1)}, bf16[768,768]{1,0:T(8,128)(2,1)}, u32[]{:S(2)}, u32[]{:S(2)}) collective-permute-start(bf16[768,768]{1,0:T(8,128)(2,1)} %get-tuple-element.131), channel_id=1, source_target_pairs={{0,2},{1,3},{2,0},{3,1},{4,6},{5,7},{6,4},{7,5},{8,10},{9,11},{10,... | collective-permute-start | bytes 3538952 | tf_op jit(solution)/shard_map/ppermute | solution.py:764
  69.2 78.0 %collective-permute-start.8 = (bf16[768,768]{1,0:T(8,128)(2,1)}, bf16[768,768]{1,0:T(8,128)(2,1)}, u32[]{:S(2)}, u32[]{:S(2)}) collective-permute-start(bf16[768,768]{1,0:T(8,128)(2,1)} %get-tuple-element.132), channel_id=1, source_target_pairs={{0,4},{1,5},{2,6},{3,7},{4,0},{5,1},{6,2},{7,3},{8,12},{9,13},{10,... | collective-permute-start | bytes 3538952 | tf_op jit(solution)/shard_map/ppermute | solution.py:764
  70.0 103.2 %collective-permute-start.9 = (bf16[768,768]{1,0:T(8,128)(2,1)}, bf16[768,768]{1,0:T(8,128)(2,1)}, u32[]{:S(2)}, u32[]{:S(2)}) collective-permute-start(bf16[768,768]{1,0:T(8,128)(2,1)} %get-tuple-element.133), channel_id=1, source_target_pairs={{0,6},{1,7},{2,4},{3,5},{4,2},{5,3},{6,0},{7,1},{8,14},{9,15},{10,... | collective-permute-start | bytes 3538952 | tf_op jit(solution)/shard_map/ppermute | solution.py:764
  176.8 61.2 %collective-permute-start.14 = (bf16[1536,768]{1,0:T(8,128)(2,1)S(1)}, bf16[1536,768]{1,0:T(8,128)(2,1)}, u32[]{:S(2)}, u32[]{:S(2)}) collective-permute-start(bf16[1536,768]{1,0:T(8,128)(2,1)S(1)} %pad_maximum_fusion), channel_id=1, source_target_pairs={{0,1},{1,0},{2,3},{3,2},{4,5},{5,4},{6,7},{7,6},{8,9},{9,8},{10,11... | collective-permute-start | bytes 7077896 | tf_op jit(solution)/shard_map/ppermute | solution.py:773
  176.9 41.9 %collective-permute-start.11 = (bf16[384,768]{1,0:T(8,128)(2,1)S(1)}, bf16[384,768]{1,0:T(8,128)(2,1)S(1)}, u32[]{:S(2)}, u32[]{:S(2)}) collective-permute-start(bf16[384,768]{1,0:T(8,128)(2,1)S(1)} %get-tuple-element.141), channel_id=1, source_target_pairs={{0,4},{1,5},{2,6},{3,7},{4,0},{5,1},{6,2},{7,3},{8,12},{9,13},{10,... | collective-permute-start | bytes 1769480 | tf_op jit(solution)/shard_map/ppermute | solution.py:764
  179.8 52.0 %collective-permute-start.12 = (bf16[384,768]{1,0:T(8,128)(2,1)S(1)}, bf16[384,768]{1,0:T(8,128)(2,1)S(1)}, u32[]{:S(2)}, u32[]{:S(2)}) collective-permute-start(bf16[384,768]{1,0:T(8,128)(2,1)S(1)} %get-tuple-element.142), channel_id=1, source_target_pairs={{0,6},{1,7},{2,4},{3,5},{4,2},{5,3},{6,0},{7,1},{8,14},{9,15},{10,... | collective-permute-start | bytes 1769480 | tf_op jit(solution)/shard_map/ppermute | solution.py:764
  231.9 73.5 %collective-permute-start.15 = (bf16[384,768]{1,0:T(8,128)(2,1)}, bf16[384,768]{1,0:T(8,128)(2,1)S(1)}, u32[]{:S(2)}, u32[]{:S(2)}) collective-permute-start(bf16[384,768]{1,0:T(8,128)(2,1)} %get-tuple-element.154), channel_id=1, source_target_pairs={{0,2},{1,3},{2,0},{3,1},{4,6},{5,7},{6,4},{7,5},{8,10},{9,11},{10,... | collective-permute-start | bytes 1769480 | tf_op jit(solution)/shard_map/ppermute | solution.py:764
  232.0 73.5 %collective-permute-start.16 = (bf16[384,768]{1,0:T(8,128)(2,1)}, bf16[384,768]{1,0:T(8,128)(2,1)}, u32[]{:S(2)}, u32[]{:S(2)}) collective-permute-start(bf16[384,768]{1,0:T(8,128)(2,1)} %get-tuple-element.155), channel_id=1, source_target_pairs={{0,4},{1,5},{2,6},{3,7},{4,0},{5,1},{6,2},{7,3},{8,12},{9,13},{10,... | collective-permute-start | bytes 1769480 | tf_op jit(solution)/shard_map/ppermute | solution.py:764
  234.9 70.6 %collective-permute-start.17 = (bf16[384,768]{1,0:T(8,128)(2,1)}, bf16[384,768]{1,0:T(8,128)(2,1)}, u32[]{:S(2)}, u32[]{:S(2)}) collective-permute-start(bf16[384,768]{1,0:T(8,128)(2,1)} %get-tuple-element.156), channel_id=1, source_target_pairs={{0,6},{1,7},{2,4},{3,5},{4,2},{5,3},{6,0},{7,1},{8,14},{9,15},{10,... | collective-permute-start | bytes 1769480 | tf_op jit(solution)/shard_map/ppermute | solution.py:764
  307.8 73.6 %collective-permute-start.19 = (bf16[384,768]{1,0:T(8,128)(2,1)}, bf16[384,768]{1,0:T(8,128)(2,1)S(1)}, u32[]{:S(2)}, u32[]{:S(2)}) collective-permute-start(bf16[384,768]{1,0:T(8,128)(2,1)} %get-tuple-element.171), channel_id=1, source_target_pairs={{0,2},{1,3},{2,0},{3,1},{4,6},{5,7},{6,4},{7,5},{8,10},{9,11},{10,... | collective-permute-start | bytes 1769480 | tf_op jit(solution)/shard_map/ppermute | solution.py:764
  308.9 72.6 %collective-permute-start.20 = (bf16[384,768]{1,0:T(8,128)(2,1)}, bf16[384,768]{1,0:T(8,128)(2,1)}, u32[]{:S(2)}, u32[]{:S(2)}) collective-permute-start(bf16[384,768]{1,0:T(8,128)(2,1)} %get-tuple-element.172), channel_id=1, source_target_pairs={{0,4},{1,5},{2,6},{3,7},{4,0},{5,1},{6,2},{7,3},{8,12},{9,13},{10,... | collective-permute-start | bytes 1769480 | tf_op jit(solution)/shard_map/ppermute | solution.py:764
  310.8 70.7 %collective-permute-start.21 = (bf16[384,768]{1,0:T(8,128)(2,1)}, bf16[384,768]{1,0:T(8,128)(2,1)}, u32[]{:S(2)}, u32[]{:S(2)}) collective-permute-start(bf16[384,768]{1,0:T(8,128)(2,1)} %get-tuple-element.173), channel_id=1, source_target_pairs={{0,6},{1,7},{2,4},{3,5},{4,2},{5,3},{6,0},{7,1},{8,14},{9,15},{10,... | collective-permute-start | bytes 1769480 | tf_op jit(solution)/shard_map/ppermute | solution.py:764
  384.0 65.7 %collective-permute-start.30 = (bf16[2,192,3072]{2,1,0:T(8,128)(2,1)}, bf16[2,192,3072]{2,1,0:T(8,128)(2,1)}, u32[]{:S(2)}, u32[]{:S(2)}) collective-permute-start(bf16[2,192,3072]{2,1,0:T(8,128)(2,1)} %get-tuple-element.198), channel_id=1, source_target_pairs={{0,8},{8,0},{16,24},{24,16},{1,9},{9,1},{17,25},{25,17},{2,10},{10... | collective-permute-start | bytes 7077896 | tf_op jit(solution)/shard_map/ppermute | solution.py:517
  386.8 37.8 %collective-permute-start.23 = (bf16[384,768]{1,0:T(8,128)(2,1)}, bf16[384,768]{1,0:T(8,128)(2,1)S(1)}, u32[]{:S(2)}, u32[]{:S(2)}) collective-permute-start(bf16[384,768]{1,0:T(8,128)(2,1)} %get-tuple-element.179), channel_id=1, source_target_pairs={{0,2},{1,3},{2,0},{3,1},{4,6},{5,7},{6,4},{7,5},{8,10},{9,11},{10,... | collective-permute-start | bytes 1769480 | tf_op jit(solution)/shard_map/ppermute | solution.py:764
  388.7 40.0 %collective-permute-start.24 = (bf16[384,768]{1,0:T(8,128)(2,1)S(1)}, bf16[384,768]{1,0:T(8,128)(2,1)S(1)}, u32[]{:S(2)}, u32[]{:S(2)}) collective-permute-start(bf16[384,768]{1,0:T(8,128)(2,1)S(1)} %copy-done.69), channel_id=1, source_target_pairs={{0,4},{1,5},{2,6},{3,7},{4,0},{5,1},{6,2},{7,3},{8,12},{9,13},{10,... | collective-permute-start | bytes 1769480 | tf_op jit(solution)/shard_map/ppermute | solution.py:764
  389.7 51.8 %collective-permute-start.25 = (bf16[384,768]{1,0:T(8,128)(2,1)S(1)}, bf16[384,768]{1,0:T(8,128)(2,1)S(1)}, u32[]{:S(2)}, u32[]{:S(2)}) collective-permute-start(bf16[384,768]{1,0:T(8,128)(2,1)S(1)} %copy-done.68), channel_id=1, source_target_pairs={{0,6},{1,7},{2,4},{3,5},{4,2},{5,3},{6,0},{7,1},{8,14},{9,15},{10,... | collective-permute-start | bytes 1769480 | tf_op jit(solution)/shard_map/ppermute | solution.py:764
  390.3 63.5 %collective-permute-start.31 = (bf16[2,768,768]{2,1,0:T(8,128)(2,1)}, bf16[2,768,768]{2,1,0:T(8,128)(2,1)}, u32[]{:S(2)}, u32[]{:S(2)}) collective-permute-start(bf16[2,768,768]{2,1,0:T(8,128)(2,1)} %get-tuple-element.200), channel_id=1, source_target_pairs={{0,16},{8,24},{16,0},{24,8},{1,17},{9,25},{17,1},{25,9},{2,18},{10... | collective-permute-start | bytes 7077896 | tf_op jit(solution)/shard_map/ppermute | solution.py:517
  446.2 45.2 %collective-permute-start.27 = (bf16[384,768]{1,0:T(8,128)(2,1)}, bf16[384,768]{1,0:T(8,128)(2,1)S(1)}, u32[]{:S(2)}, u32[]{:S(2)}) collective-permute-start(bf16[384,768]{1,0:T(8,128)(2,1)} %get-tuple-element.194), channel_id=1, source_target_pairs={{0,2},{1,3},{2,0},{3,1},{4,6},{5,7},{6,4},{7,5},{8,10},{9,11},{10,... | collective-permute-start | bytes 1769480 | tf_op jit(solution)/shard_map/ppermute | solution.py:764
  446.2 45.2 %collective-permute-start.28 = (bf16[384,768]{1,0:T(8,128)(2,1)}, bf16[384,768]{1,0:T(8,128)(2,1)S(1)}, u32[]{:S(2)}, u32[]{:S(2)}) collective-permute-start(bf16[384,768]{1,0:T(8,128)(2,1)} %get-tuple-element.195), channel_id=1, source_target_pairs={{0,4},{1,5},{2,6},{3,7},{4,0},{5,1},{6,2},{7,3},{8,12},{9,13},{10,... | collective-permute-start | bytes 1769480 | tf_op jit(solution)/shard_map/ppermute | solution.py:764
  449.0 51.9 %collective-permute-start.29 = (bf16[384,768]{1,0:T(8,128)(2,1)}, bf16[384,768]{1,0:T(8,128)(2,1)S(1)}, u32[]{:S(2)}, u32[]{:S(2)}) collective-permute-start(bf16[384,768]{1,0:T(8,128)(2,1)} %get-tuple-element.196), channel_id=1, source_target_pairs={{0,6},{1,7},{2,4},{3,5},{4,2},{5,3},{6,0},{7,1},{8,14},{9,15},{10,... | collective-permute-start | bytes 1769480 | tf_op jit(solution)/shard_map/ppermute | solution.py:764
  500.9 33.0 %collective-permute-start.33 = (bf16[384,3200]{1,0:T(8,128)(2,1)}, bf16[384,3200]{1,0:T(8,128)(2,1)S(1)}, u32[]{:S(2)}, u32[]{:S(2)}) collective-permute-start(bf16[384,3200]{1,0:T(8,128)(2,1)} %get-tuple-element.228), channel_id=1, source_target_pairs={{0,1},{1,0},{2,3},{3,2},{4,5},{5,4},{6,7},{7,6},{8,9},{9,8},{10,11... | collective-permute-start | bytes 7372808 | tf_op jit(solution)/shard_map/ppermute | solution.py:782
  502.5 28.2 %collective-permute-start.43 = (bf16[192,3072]{1,0:T(8,128)(2,1)S(1)}, bf16[192,3072]{1,0:T(8,128)(2,1)S(1)}, u32[]{:S(2)}, u32[]{:S(2)}) collective-permute-start(bf16[192,3072]{1,0:T(8,128)(2,1)S(1)} %slice_bitcast_fusion.2), channel_id=1, source_target_pairs={{0,16},{8,24},{16,0},{24,8},{1,17},{9,25},{17,1},{25,9},{2,18},{10... | collective-permute-start | bytes 3538952 | tf_op jit(solution)/shard_map/ppermute | solution.py:517
  504.1 28.6 %collective-permute-start.46 = (bf16[768,768]{1,0:T(8,128)(2,1)S(1)}, bf16[768,768]{1,0:T(8,128)(2,1)S(1)}, u32[]{:S(2)}, u32[]{:S(2)}) collective-permute-start(bf16[768,768]{1,0:T(8,128)(2,1)S(1)} %slice_bitcast_fusion), channel_id=1, source_target_pairs={{0,8},{8,0},{16,24},{24,16},{1,9},{9,1},{17,25},{25,17},{2,10},{10... | collective-permute-start | bytes 3538952 | tf_op jit(solution)/shard_map/ppermute | solution.py:517
  531.1 27.4 %collective-permute-start.44 = (bf16[192,3072]{1,0:T(8,128)(2,1)S(1)}, bf16[192,3072]{1,0:T(8,128)(2,1)S(1)}, u32[]{:S(2)}, u32[]{:S(2)}) collective-permute-start(bf16[192,3072]{1,0:T(8,128)(2,1)S(1)} %fusion.1), channel_id=1, source_target_pairs={{0,16},{8,24},{16,0},{24,8},{1,17},{9,25},{17,1},{25,9},{2,18},{10... | collective-permute-start | bytes 3538952 | tf_op jit(solution)/shard_map/ppermute | solution.py:517
  534.7 43.2 %collective-permute-start.36 = (bf16[96,3200]{1,0:T(8,128)(2,1)S(1)}, bf16[96,3200]{1,0:T(8,128)(2,1)S(1)}, u32[]{:S(2)}, u32[]{:S(2)}) collective-permute-start(bf16[96,3200]{1,0:T(8,128)(2,1)S(1)} %get-tuple-element.263), channel_id=1, source_target_pairs={{0,6},{1,7},{2,4},{3,5},{4,2},{5,3},{6,0},{7,1},{8,14},{9,15},{10,... | collective-permute-start | bytes 1843208 | tf_op jit(solution)/shard_map/ppermute | solution.py:786
  536.2 51.7 %collective-permute-start.35 = (bf16[96,3200]{1,0:T(8,128)(2,1)S(1)}, bf16[96,3200]{1,0:T(8,128)(2,1)S(1)}, u32[]{:S(2)}, u32[]{:S(2)}) collective-permute-start(bf16[96,3200]{1,0:T(8,128)(2,1)S(1)} %get-tuple-element.264), channel_id=1, source_target_pairs={{0,4},{1,5},{2,6},{3,7},{4,0},{5,1},{6,2},{7,3},{8,12},{9,13},{10,... | collective-permute-start | bytes 1843208 | tf_op jit(solution)/shard_map/ppermute | solution.py:786
  558.5 33.5 %collective-permute-start.32 = (bf16[768,768]{1,0:T(8,128)(2,1)S(1)}, bf16[768,768]{1,0:T(8,128)(2,1)S(1)}, u32[]{:S(2)}, u32[]{:S(2)}) collective-permute-start(bf16[768,768]{1,0:T(8,128)(2,1)S(1)} %pad_maximum_fusion.9), channel_id=1, source_target_pairs={{0,1},{1,0},{2,3},{3,2},{4,5},{5,4},{6,7},{7,6},{8,9},{9,8},{10,11... | collective-permute-start | bytes 3538952 | tf_op jit(solution)/shard_map/ppermute | solution.py:773
  560.1 77.5 %collective-permute-start.45 = (bf16[2,192,3072]{2,1,0:T(8,128)(2,1)S(1)}, bf16[2,192,3072]{2,1,0:T(8,128)(2,1)S(1)}, u32[]{:S(2)}, u32[]{:S(2)}) collective-permute-start(bf16[2,192,3072]{2,1,0:T(8,128)(2,1)S(1)} %pad_maximum_fusion.1), channel_id=1, source_target_pairs={{0,8},{8,0},{16,24},{24,16},{1,9},{9,1},{17,25},{25,17},{2,10},{10... | collective-permute-start | bytes 7077896 | tf_op jit(solution)/shard_map/ppermute | solution.py:517
  561.2 66.0 %collective-permute-start.48 = (bf16[2,768,768]{2,1,0:T(8,128)(2,1)S(1)}, bf16[2,768,768]{2,1,0:T(8,128)(2,1)S(1)}, u32[]{:S(2)}, u32[]{:S(2)}) collective-permute-start(bf16[2,768,768]{2,1,0:T(8,128)(2,1)S(1)} %pad_maximum_fusion.2), channel_id=1, source_target_pairs={{0,16},{8,24},{16,0},{24,8},{1,17},{9,25},{17,1},{25,9},{2,18},{10... | collective-permute-start | bytes 7077896 | tf_op jit(solution)/shard_map/ppermute | solution.py:517
  588.1 37.5 %collective-permute-start.41 = (bf16[96,3200]{1,0:T(8,128)(2,1)S(1)}, bf16[96,3200]{1,0:T(8,128)(2,1)S(1)}, u32[]{:S(2)}, u32[]{:S(2)}) collective-permute-start(bf16[96,3200]{1,0:T(8,128)(2,1)S(1)} %fusion.3), channel_id=1, source_target_pairs={{0,8},{8,0},{16,24},{24,16},{1,9},{9,1},{17,25},{25,17},{2,10},{10... | collective-permute-start | bytes 1843208 | tf_op jit(solution)/shard_map/ppermute | solution.py:794
  589.4 52.6 %collective-permute-start.37 = (bf16[384,768]{1,0:T(8,128)(2,1)}, bf16[384,768]{1,0:T(8,128)(2,1)S(1)}, u32[]{:S(2)}, u32[]{:S(2)}) collective-permute-start(bf16[384,768]{1,0:T(8,128)(2,1)} %get-tuple-element.230), channel_id=1, source_target_pairs={{0,2},{1,3},{2,0},{3,1},{4,6},{5,7},{6,4},{7,5},{8,10},{9,11},{10,... | collective-permute-start | bytes 1769480 | tf_op jit(solution)/shard_map/ppermute | solution.py:764
  592.1 50.0 %collective-permute-start.38 = (bf16[384,768]{1,0:T(8,128)(2,1)}, bf16[384,768]{1,0:T(8,128)(2,1)S(1)}, u32[]{:S(2)}, u32[]{:S(2)}) collective-permute-start(bf16[384,768]{1,0:T(8,128)(2,1)} %get-tuple-element.231), channel_id=1, source_target_pairs={{0,4},{1,5},{2,6},{3,7},{4,0},{5,1},{6,2},{7,3},{8,12},{9,13},{10,... | collective-permute-start | bytes 1769480 | tf_op jit(solution)/shard_map/ppermute | solution.py:764
  (90 other events, 1860.3 us)

commit v2 on v1

--- a/solution.py
+++ b/solution.py
@@ -109,17 +109,12 @@
         slots = [jnp.sum(jnp.where(hot, at, 0.0), axis=0, keepdims=True).astype(jnp.int32) for hot in hots]
         for k in range(TOP):
             slots_ref[step, k : k + 1, :] = slots[k]
-        rows = block_refs[0].shape[0] // MICRO
-        half = min(rows // 2, 384)
-        for first in range(0, experts * capacity, half):
-            hot = slot_hot(slots[0], first, half) | slot_hot(slots[1], first, half)
+        blocks = block_refs[step * len(block_refs) // MICRO : (step + 1) * len(block_refs) // MICRO]
+        size = blocks[0].shape[0]
+        for first in range(0, experts * capacity, 384):
+            hot = slot_hot(slots[0], first, 384) | slot_hot(slots[1], first, 384)
             value = dot_nn(jnp.where(hot, 1.0, 0.0).astype(bf16), cot_ref[here, :]).astype(bf16)
-            index, low = first // rows, first % rows
-            if len(block_refs) > 1:
-                low = 2 * low + step * half
-            else:
-                low = low + step * rows
-            block_refs[index][low : low + half, :] = value
+            blocks[first // size][first % size : first % size + 384, :] = value
 
 
 def earlier_places():
@@ -127,16 +122,17 @@
 
 
 def route(me, ids, cotangent, blocks, experts, capacity):
-    size = MICRO * experts * capacity // blocks
-    return pl.pallas_call(
+    size = experts * capacity // blocks
+    slots, *out = pl.pallas_call(
         functools.partial(route_kernel, experts=experts, capacity=capacity),
         in_specs=[pl.BlockSpec(memory_space=pltpu.SMEM)] + [pl.BlockSpec(memory_space=pltpu.VMEM)] * 2,
         out_shape=[jax.ShapeDtypeStruct((MICRO, TOP, TOK_MB), jnp.int32)]
-        + [jax.ShapeDtypeStruct((size, D), bf16)] * blocks,
+        + [jax.ShapeDtypeStruct((size, D), bf16)] * (MICRO * blocks),
         compiler_params=pltpu.CompilerParams(vmem_limit_bytes=32 * MIB),
         cost_estimate=lasting(4),
         name="route",
     )(me, ids, cotangent)
+    return slots, [out[step * blocks : (step + 1) * blocks] for step in range(MICRO)]
 
 
 def partner_kernel(me_ref, ids_ref, other_ref, *, xor):
@@ -168,7 +164,7 @@
 
 
 def unpack_kernel(place_ref, *refs, groups, chips, lines):
-    own, passed, small, (out_ref, narrow_ref, ids_ref) = refs[:groups], refs[groups], refs[groups + 1], refs[groups + 2 :]
+    own, (passed, *smalls, out_ref, narrow_ref, ids_ref) = refs[:groups], refs[groups:]
     rows = own[0].shape[0] // chips
     me = place_ref[1]
     for k in range(groups):
@@ -181,9 +177,7 @@
     gathered = jnp.zeros((16, D), f32)
     lane = iota((16, D), 1)
     for k in range(2 * chips):
-        source = small if k % 2 == 0 else passed
-        low = k // 2 * 16 + (0 if k % 2 == 0 else groups * chips * rows)
-        block = source[low : low + 16, :].astype(f32)
+        block = smalls[k % 2][k // 2 * 16 : k // 2 * 16 + 16, :].astype(f32)
         device = me ^ k
         gathered = gathered + pltpu.roll(jnp.where(lane < rows, block, 0.0), device * rows, 1)
         for pick in range(TOP * MICRO):
@@ -191,7 +185,7 @@
     narrow_ref[...] = gathered.astype(bf16)
 
 
-def gather_weights(matrices, narrow, ids, groups, devices):
+def gather_weights(matrices, narrow, ids, blocks, groups, devices):
     lines, shard = narrow.shape
     if devices > DIRECT_MAX:
         whole = jnp.stack([lax.all_gather(w, "expert", axis=0, tiled=True) for w in matrices])
@@ -199,7 +193,7 @@
         flat = lax.all_gather(flat, "expert", axis=0)
         narrow = flat[:, : lines * shard].reshape(devices, lines, shard).transpose(1, 0, 2).reshape(lines, D)
         ids = flat[:, lines * shard :].astype(f32).reshape(devices, TOP * MICRO, TOK_MB).transpose(1, 0, 2)
-        return whole, narrow, ids
+        return whole, narrow, ids, send(blocks, devices)
     chips = devices // 2
     group, me = lax.axis_index("group"), lax.axis_index("expert")
     mine = matrices[0]
@@ -217,12 +211,21 @@
     mine = [mine] + [lax.ppermute(mine, "expert", swap(devices, 2 * j)) for j in range(1, chips)]
     small = jnp.concatenate([m[shard:] for m in mine], axis=0)
     mine = jnp.concatenate([m[:shard] for m in mine], axis=0)
-    own = [mine] + [lax.ppermute(mine, "group", swap(groups, k)) for k in range(1, groups)]
-    passed = lax.ppermute(jnp.concatenate([*own, small], axis=0), "expert", swap(devices, 1))
+    blocks = send(tie(blocks, mine), devices)
+    near = lax.ppermute(mine, "group", swap(groups, 1))
+    far = lax.ppermute(mine, "group", swap(groups, 2))
+    near, far = tie([near, far], blocks[chips // 2])
+    half = mine.shape[0] // 2
+    low = lax.ppermute(far[:half], "group", swap(groups, 1))
+    high = lax.ppermute(near[half:], "group", swap(groups, 2))
+    own = [mine, near, far, jnp.concatenate([low, high], axis=0)]
+    (passed,) = tie([jnp.concatenate(own, axis=0)], *blocks[1:])
+    passed = lax.ppermute(passed, "expert", swap(devices, 1))
+    passed_small = lax.ppermute(small, "expert", swap(devices, 1))
     place = jnp.stack([group, me]).astype(jnp.int32)
-    return pl.pallas_call(
+    whole, narrow, ids = pl.pallas_call(
         functools.partial(unpack_kernel, groups=groups, chips=chips, lines=lines),
-        in_specs=[pl.BlockSpec(memory_space=pltpu.SMEM)] + [pl.BlockSpec(memory_space=pltpu.VMEM)] * (groups + 2),
+        in_specs=[pl.BlockSpec(memory_space=pltpu.SMEM)] + [pl.BlockSpec(memory_space=pltpu.VMEM)] * (groups + 3),
         out_shape=[
             jax.ShapeDtypeStruct((groups, D, D), bf16),
             jax.ShapeDtypeStruct((16, D), bf16),
@@ -231,7 +234,8 @@
         compiler_params=pltpu.CompilerParams(vmem_limit_bytes=32 * MIB),
         cost_estimate=lasting(3),
         name="unpack",
-    )(place, *own, passed, small)
+    )(place, *own, passed, small, passed_small)
+    return whole, narrow, ids, blocks
 
 
 def swap(devices, mask):
@@ -308,12 +312,16 @@
         ]
         gates_ref[0:1, :] = 1.0 / (1.0 + jnp.exp(chosen[1] - chosen[0]))
         gates_ref[1:2, :] = 1.0 / (1.0 + jnp.exp(chosen[0] - chosen[1]))
-        size = block_refs[0].shape[0]
-        for index, ref in enumerate(block_refs):
-            for low in range(0, size, 384):
-                hots = [slot_hot(slots_ref[k : k + 1, :], index * size + low, 384) for k in range(TOP)]
-                pick = jnp.where(hots[0] | hots[1], 1.0, 0.0).astype(bf16)
-                ref[low : low + 384, :] = dot_nn(pick, rows).astype(bf16)
+        half = block_refs[0].shape[0] // (4 // len(block_refs))
+        for first in range(0, 4 * half, half):
+            hots = [slot_hot(slots_ref[k : k + 1, :], first, half) for k in range(TOP)]
+            value = dot_nn(jnp.where(hots[0] | hots[1], 1.0, 0.0).astype(bf16), rows).astype(bf16)
+            low = first // 2
+            if len(block_refs) == 1:
+                block_refs[0][first : first + half, :] = value
+            else:
+                block_refs[0][low : low + half // 2, :] = value[: half // 2]
+                block_refs[1][low : low + half // 2, :] = value[half // 2 :]
 
 
 def matrix_specs():
@@ -323,14 +331,14 @@
     ]
 
 
-def attend(starts, tokens, matrices, narrow, constants, ids, slots, step, blocks, experts, capacity):
-    size = experts * capacity // blocks
+def attend(starts, tokens, matrices, narrow, constants, ids, slots, step, direct, experts, capacity):
+    size = experts * capacity // (1 + direct)
     fixed = lambda h: (0, 0)
     out_shapes = (
         [((D, TOK_MB), bf16)] * 3
         + [((HEADS, SEQ_LEN, SEQ_LEN), bf16), ((D, TOK_MB), bf16), ((TOK_MB, D), f32), ((TOK_MB, D), bf16)]
         + [((TOP, TOK_MB), f32), ((TOK_MB, D), bf16)]
-        + [((size, D), bf16)] * blocks
+        + [((size, D), bf16)] * (1 + direct)
     )
     out_specs = [
         pl.BlockSpec((1, SEQ_LEN, SEQ_LEN), lambda h: (h, 0, 0)) if len(s) == 3 else resident(s, fixed)
@@ -354,19 +362,24 @@
 
 
 def collect(target, direct, passed, size):
+    if passed is None:
+        for index, ref in enumerate(direct):
+            target[index * ref.shape[0] : (index + 1) * ref.shape[0], :] = ref[...]
+        return
     for index, ref in enumerate(direct):
         low = 2 * index * size
-        if passed is None:
-            target[...] = ref[...]
-        else:
-            target[low : low + size, :] = ref[:size, :]
-            target[low + size : low + 2 * size, :] = passed[index * size : (index + 1) * size, :]
+        target[low : low + size, :] = ref[...]
+        target[low + size : low + 2 * size, :] = passed[index * size : (index + 1) * size, :]
+
+
+def received_specs(received, blocks, size):
+    first = lambda *_: (0, 0)
+    return [resident((size, D), first)] * blocks + [resident(r.shape, first) for r in received[blocks:]]
 
 
 def expert_kernel(place_ref, *refs, blocks, passes, micro):
     accumulate = micro > 0
-    take = blocks + passes
-    rows_refs, cot_refs, refs = refs[:take], refs[take : 2 * take], refs[2 * take :]
+    rows_refs, cot_refs, refs = refs[:blocks], refs[blocks : 2 * blocks + passes], refs[2 * blocks + passes :]
     other_ref, router_ref, in_ref, out_ref = refs[:4]
     refs = refs[4:]
     if accumulate:
@@ -383,13 +396,8 @@
 
     @pl.when(step == 0)
     def _():
-        collect(rows, rows_refs[:blocks], rows_refs[blocks] if passes else None, width)
-        for index, ref in enumerate(cot_refs[:blocks]):
-            low = 2 * index * width if passes else 0
-            picks[low : low + width, :] = ref[...]
-            if passes:
-                first = (MICRO * index + micro) * width
-                picks[low + width : low + 2 * width, :] = cot_refs[blocks][first : first + width, :]
+        collect(rows, rows_refs, None, width)
+        collect(picks, cot_refs[:blocks], cot_refs[blocks] if passes else None, width)
         for sender in range(senders):
             here = slice(sender * width, (sender + 1) * width)
             logits = dot_nt(router_ref[:experts, :], rows[here, :])
@@ -404,8 +412,8 @@
         result[...] = jnp.zeros_like(result)
         back[...] = jnp.zeros_like(back)
 
-    def one_tile(index, carry):
-        here = pl.ds(pl.multiple_of(index * tile, tile), tile)
+    def one_tile(index):
+        here = slice(index * tile, (index + 1) * tile)
         inner = dot_nn(rows[here, :], in_ref[0])
         square = inner * inner
         bend = jnp.tanh(inner * (0.7978845608028654 + 0.035677408136300125 * square))
@@ -417,9 +425,9 @@
         grad = (dot_nt(picks[here, :], out_ref[0]) * slope).astype(bf16)
         inner_grad[here, :] = grad
         back[here, :] += dot_nt(grad, in_ref[0])
-        return carry
-
-    lax.fori_loop(0, total // tile, one_tile, 0)
+
+    for index in range(total // tile):
+        one_tile(index)
 
     def store(index, where, value):
         if accumulate:
@@ -454,17 +462,17 @@
             router_sum = router_sum + dot_nn(logit_grad, rows[here, :])
             total_back = back[here, :] + dot_tn(logit_grad, router_ref[:experts, :])
             index, first = (sender // 2, sender % 2 * width) if passes else (0, 0)
+            back_refs[index][first : first + width, :] = total_back.astype(bf16)
             result_refs[index][first : first + width, :] = low
-            back_refs[index][first : first + width, :] = total_back.astype(bf16)
         grads[4][...] = router_sum
 
 
 def run_expert(place, rows_blocks, cot_blocks, other, narrow, expert_in, expert_out, prior, micro, blocks, experts):
-    passes = len(rows_blocks) - blocks
+    passes = len(cot_blocks) - blocks
     size = rows_blocks[0].shape[0]
     total = blocks * size
+    fixed = lambda i, place: (0, 0)
     chunk, quarter = FF // 4, D // 4
-    fixed = lambda i, place: (0, 0)
     at = lambda i, place: i ^ 2 ^ place[2]
     weights = [
         pl.BlockSpec((1, D, chunk), lambda i, place: (0, 0, at(i, place))),
@@ -478,11 +486,8 @@
         resident((experts, D), fixed),
     ]
     grad_shapes = [((2, quarter, FF), bf16)] * 2 + [((2, chunk, D), bf16)] * 2 + [((experts, D), f32)]
-    wide = resident((size, D), fixed)
-    taken = [wide] * blocks + [resident((blocks * (size // 2), D), fixed)] * passes
-    cot_size = size // (1 + passes)
-    taken += [resident((cot_size, D), lambda i, place: (micro, 0))] * blocks
-    taken += [resident((MICRO * blocks * cot_size, D), fixed)] * passes
+    taken = received_specs(rows_blocks, blocks, size)
+    taken += received_specs(cot_blocks, blocks, size // (1 + passes))
     out = pl.pallas_call(
         functools.partial(expert_kernel, blocks=blocks, passes=passes, micro=micro),
         grid_spec=pltpu.PrefetchScalarGridSpec(
@@ -492,7 +497,7 @@
             + [resident(other.shape, fixed), resident(narrow.shape, fixed)]
             + weights
             + (grad_specs if prior else []),
-            out_specs=grad_specs + [wide] * (2 * blocks),
+            out_specs=grad_specs + [resident((size, D), fixed)] * (2 * blocks),
             scratch_shapes=[
                 pltpu.VMEM((total, D), bf16),
                 pltpu.VMEM((total, D), bf16),
@@ -510,7 +515,7 @@
         cost_estimate=lasting(62),
         name="expert",
     )(place, *rows_blocks, *cot_blocks, other, narrow, expert_in, expert_out, *(prior or ()))
-    return out[:5], out[5 : 5 + blocks], out[5 + blocks :]
+    return out[:5], out[5:]
 
 
 def trade(value, groups, mask):
@@ -521,19 +526,8 @@
     return (left.astype(f32) + right.astype(f32)).astype(bf16)
 
 
-def first_half(keep, send_away, groups, mask):
-    return add_low(keep, trade(send_away, groups, mask))
-
-
 def second_half(half, groups, mask):
-    return half[0], half[1], trade(half[1], groups, mask)
-
-
-def doubled(kept, _, received, groups, first, second):
-    own = add_low(kept, received)
-    beside = trade(own, groups, second)
-    far = trade(jnp.stack([own, beside]), groups, first)
-    return own[None], beside[None], far
+    return add_low(half[0], trade(half[1], groups, mask))
 
 
 def spread_kernel(place_ref, own_ref, beside_ref, far_ref, out_ref, *, code):
@@ -607,7 +601,7 @@
         lines[...] = jnp.zeros_like(lines)
         diagonals[...] = jnp.zeros_like(diagonals)
         cot = cot_ref[...].astype(f32)
-        collect(gathered, back_refs[:blocks], back_refs[blocks] if passes else None, back_refs[0].shape[0] // 2)
+        collect(gathered, back_refs[:blocks], back_refs[blocks] if passes else None, back_refs[0].shape[0])
         columns = [row_to_column(slots_ref[k : k + 1, :].astype(f32)).astype(jnp.int32) for k in range(TOP)]
         rows_grad = jnp.zeros((TOK_MB, D), f32)
         for low in range(0, total, 512):
@@ -679,9 +673,9 @@
     return dot(high, hot) + dot((values - high.astype(f32)).astype(bf16), hot)
 
 
-def backward(me, back_blocks, tokens, cotangent, matrices, narrow, constants, slots, saved, prior, step, blocks, experts, devices):
+def backward(me, back_blocks, tokens, cotangent, matrices, narrow, constants, slots, saved, prior, step, blocks, experts, devices, slot_count):
     passes = len(back_blocks) - blocks
-    size = back_blocks[0].shape[0]
+    size = slot_count // blocks // (1 + passes)
     fixed = lambda h: (0, 0)
     block = lambda h: (step, 0)
     head_block = pl.BlockSpec((1, SEQ_LEN, SEQ_LEN), lambda h: (h, 0, 0))
@@ -694,7 +688,7 @@
         ),
         grid=(HEADS,),
         in_specs=[pl.BlockSpec(memory_space=pltpu.SMEM)]
-        + [resident(b.shape, fixed) for b in back_blocks]
+        + received_specs(back_blocks, blocks, size)
         + [resident((TOK_MB, D), block)] * 2
         + matrix_specs()
         + [resident(narrow.shape, fixed)]
@@ -705,7 +699,7 @@
         out_specs=[resident((TOK_MB, D), fixed)] + dense_specs,
         out_shape=[jax.ShapeDtypeStruct((TOK_MB, D), bf16)] + [jax.ShapeDtypeStruct(s, bf16) for s in dense_shapes],
         scratch_shapes=[
-            pltpu.VMEM((blocks * size, D), bf16),
+            pltpu.VMEM((slot_count, D), bf16),
             pltpu.VMEM((TOK_MB, D), f32),
             pltpu.VMEM((D, TOK_MB), bf16),
             pltpu.VMEM((D, TOK_MB), bf16),
@@ -724,7 +718,8 @@
 def combine_kernel(*refs, blocks, passes):
     result_refs = refs[: blocks + passes]
     hidden_ref, slots_ref, gates_ref, mixed_ref, gathered = refs[blocks + passes :]
-    collect(gathered, result_refs[:blocks], result_refs[blocks] if passes else None, result_refs[0].shape[0] // 2)
+    size = result_refs[0].shape[0]
+    collect(gathered, result_refs[:blocks], result_refs[blocks] if passes else None, size)
     slots = [row_to_column(slots_ref[k : k + 1, :].astype(f32)).astype(jnp.int32) for k in range(TOP)]
     gates = [row_to_column(gates_ref[k : k + 1, :]) for k in range(TOP)]
     output = hidden_ref[...]
@@ -737,16 +732,22 @@
     mixed_ref[...] = output.astype(bf16)
 
 
-def combine(result_blocks, hidden, slots, gates, blocks):
-    total = blocks * result_blocks[0].shape[0]
+def combine(received, hidden, slots, gates, blocks, slot_count):
+    passes = len(received) - blocks
+    size = slot_count // blocks // (1 + passes)
+    fixed = lambda i: (0, 0)
     return pl.pallas_call(
-        functools.partial(combine_kernel, blocks=blocks, passes=len(result_blocks) - blocks),
+        functools.partial(combine_kernel, blocks=blocks, passes=passes),
+        grid=(1,),
+        in_specs=received_specs(received, blocks, size)
+        + [resident(a.shape, fixed) for a in (hidden, slots, gates)],
+        out_specs=resident((TOK_MB, D), fixed),
         out_shape=jax.ShapeDtypeStruct((TOK_MB, D), bf16),
-        scratch_shapes=[pltpu.VMEM((total, D), bf16)],
+        scratch_shapes=[pltpu.VMEM((slot_count, D), bf16)],
         compiler_params=pltpu.CompilerParams(vmem_limit_bytes=32 * MIB),
         cost_estimate=lasting(3),
         name="combine",
-    )(*result_blocks, hidden, slots, gates)
+    )(*received, hidden, slots, gates)
 
 
 def tie(values, *after):
@@ -765,6 +766,12 @@
     ]
 
 
+def pair_up(near, cross, devices):
+    got = lax.ppermute(cross, "expert", swap(devices, 1))
+    size = 2 * near.shape[0] // devices
+    return [jnp.concatenate([a[low : low + size] for a in (near, got)]) for low in range(0, near.shape[0], size)]
+
+
 def pass_on(blocks, devices):
     if len(blocks) == 1:
         return blocks
@@ -773,24 +780,25 @@
     return [*blocks, lax.ppermute(second, "expert", swap(devices, 1))]
 
 
-def reduce_dense(pieces, devices):
-    if len(pieces) == 1:
-        return lax.psum_scatter(pieces[0], "expert", scatter_dimension=0, tiled=True).astype(f32)
+def sum_cores(pieces, devices):
     near, cross = pieces
+    return near.astype(f32) + lax.ppermute(cross, "expert", swap(devices, 1)).astype(f32)
+
+
+def sum_chips(own, low, devices):
     chips = devices // 2
-    rows = near.shape[0] // chips
-    summed = near.astype(f32) + lax.ppermute(cross, "expert", swap(devices, 1)).astype(f32)
-    low = summed.astype(bf16)
-    total = summed[:rows]
+    rows = low.shape[0] // chips
     for j in range(1, chips):
-        total = total + lax.ppermute(low[j * rows : (j + 1) * rows], "expert", swap(devices, 2 * j)).astype(f32)
-    return total
-
-
-def reduce_group(total, groups):
+        own = own + lax.ppermute(low[j * rows : (j + 1) * rows], "expert", swap(devices, 2 * j)).astype(f32)
+    return own
+
+
+def reduce_group(total, groups, *after):
     mask = 1
     while mask < groups:
         low = total.astype(bf16)
+        if mask > 1:
+            (low,) = tie([low], *after)
         total = low.astype(f32) + lax.ppermute(low, "group", swap(groups, mask)).astype(f32)
         mask *= 2
     return total
@@ -814,77 +822,94 @@
 
     padded = jnp.pad(rel_bias, (0, shard - share))
     narrow = jnp.concatenate([w_router.T, norm_attn[None], norm_expert[None], padded[None]], axis=0)
-    matrices, narrow, all_ids = gather_weights(
-        (w_query, w_key, w_value, w_out), narrow, ids, groups, devices
+    slots, cots = route(order, ids, cotangent, blocks, experts, capacity)
+    matrices, narrow, all_ids, cots[0] = gather_weights(
+        (w_query, w_key, w_value, w_out), narrow, ids, cots[0], groups, devices
     )
     bucket, heads = bias_places(devices)
     constants = (bucket_hot().astype(bf16), bucket.astype(bf16), heads.astype(bf16))
-
-    slots, *cots = route(order, ids, cotangent, blocks, experts, capacity)
-    if not direct:
-        cots = cots[0].reshape(MICRO, devices, capacity, D).transpose(1, 0, 2, 3).reshape(-1, D)
-        cots = send([cots], devices)[0].reshape(devices, MICRO, capacity, D).transpose(1, 0, 2, 3).reshape(-1, D)
-        cots = [cots]
-    else:
-        cots = send(cots, devices)
+    slot_count = experts * capacity
+    cots[1] = send(tie(cots[1], *cots[0][1:]), devices)
     other = partners(me, all_ids, devices, capacity, direct)
     if not direct:
-        other = other.reshape(MICRO, 1, devices * capacity)
+        other = other.reshape(MICRO, 1, slot_count)
+    (narrow,) = tie([narrow], *cots[0][1:], other)
     saved, sent = [], []
     for step in range(MICRO):
         out = attend(
-            span_starts, tokens, matrices, narrow, constants, ids, slots[step], step, blocks, experts, capacity
+            span_starts, tokens, matrices, narrow, constants, ids, slots[step], step, direct, experts, capacity
         )
         saved.append(out[:9])
         sent.append(out[9:])
-    cots = tie(cots, saved[0][0], saved[1][0])
-    sent[0] = send(tie(sent[0], *cots[1:]), devices)
+    cots[1] = tie(cots[1], saved[0][0], saved[1][0])
+    if direct:
+        sent = [pair_up(*tie(s, *cots[1][1:]), devices) for s in sent]
+    sent[0] = send(tie(sent[0], *cots[1][1:]), devices)
+    cots = [pass_on(tie(c, saved[1][0]), devices) for c in cots]
     sent[1] = send(tie(sent[1], *sent[0][1:]), devices)
-    cots = pass_on(cots, devices)
-    sent[0] = pass_on(sent[0], devices)
-
-    grads, result, back = run_expert(
-        place, sent[0], cots, other[0], narrow, expert_in, expert_out, None, 0, blocks, experts
+
+    grads, first = run_expert(
+        place, sent[0], cots[0], other[0], narrow, expert_in, expert_out, None, 0, blocks, experts
     )
-    sent[1] = pass_on(tie(sent[1], back[0]), devices)
-    backs, results = [send(back, devices)], [result]
-    grads, result, back = run_expert(
-        place, sent[1], cots, other[1], narrow, expert_in, expert_out, grads, 1, blocks, experts
+    sent[1] = tie(sent[1], first[0])
+    results, backs = [first[:blocks]], [send(tie(first[blocks:], *sent[1]), devices)]
+    grads, last = run_expert(
+        place, sent[1], cots[1], other[1], narrow, expert_in, expert_out, grads, 1, blocks, experts
     )
-    results.append(result)
-    inward = first_half(grads[0], grads[1], groups, 1)
-    outward = first_half(grads[2], grads[3], groups, 2)
-    backs[0] = pass_on(tie(backs[0], back[0]), devices)
-    backs.append(send(tie(back, *backs[0]), devices))
+    results.append(last[:blocks])
+    backs.append(last[blocks:])
+    *flat, router_grad = tie(grads, *backs[0][1:])
+    away = [trade(flat[1], groups, 1), trade(flat[3], groups, 2)]
+    backs[0] = pass_on(tie(backs[0], last[0]), devices)
+    backs[1] = send(tie(backs[1], *backs[0]), devices)
 
     def run_back(step, prior):
         query, key, value, probs, attended, hidden, _, _, normed = saved[step]
         return backward(
             order, backs[step], tokens, cotangent, matrices, narrow, constants, slots[step],
-            (query, key, value, probs, attended, hidden, normed), prior, step, blocks, experts, devices,
+            (query, key, value, probs, attended, hidden, normed), prior, step, blocks, experts, devices, slot_count,
         )
 
     token_grads = [None, None]
     token_grads[0], *dense = run_back(0, None)
     backs[1] = pass_on(tie(backs[1], token_grads[0]), devices)
-    results[0] = send(tie(results[0], *backs[1]), devices)
-    backs[1] = tie(backs[1], inward, outward)
-    inward = second_half(inward, groups, 2)
-    outward = second_half(outward, groups, 1)
-    token_grads[1], *dense = run_back(1, (*dense, grads[4]))
-    results[0] = tie(results[0], token_grads[1])
-    total = reduce_dense(tie(dense, *results[0][1:]), devices)
-    results[1] = send(tie(results[1], total), devices)
-    inward = doubled(*inward, groups, 1, 2)
-    outward = doubled(*outward, groups, 2, 1)
-    total = reduce_group(total, groups)
+    away = tie(away, *backs[1])
+    halves = [add_low(flat[0], away[0]), add_low(flat[2], away[1])]
+    owns = [second_half(halves[0], groups, 2), second_half(halves[1], groups, 1)]
+    if direct:
+        results[0] = send(tie(results[0], *backs[1]), devices)
+    else:
+        results = [send(r, devices) for r in results]
+    backs[1] = tie(backs[1], *halves)
+    token_grads[1], *dense = run_back(1, (*dense, router_grad))
+    owns = tie(owns, token_grads[1], *results[0])
+    if direct:
+        results[0] = pass_on(tie(results[0], token_grads[1]), devices)
+    if direct:
+        dense = tie(dense, *results[0][1:-1], *owns)
+        total = sum_cores(dense, devices)
+        low = total.astype(bf16)
+        owns = tie(owns, low)
+    besides = [trade(owns[0], groups, 2), trade(owns[1], groups, 1)]
+    fars = [jnp.stack(pair) for pair in zip(owns, besides)]
+    if direct:
+        total = sum_chips(total[:shard], low, devices)
+        results[1] = send(tie(results[1], total), devices)
+        (total,) = tie([total], results[1][1])
+        results[1] = pass_on(results[1], devices)
+    else:
+        total = lax.psum_scatter(dense[0], "expert", scatter_dimension=0, tiled=True).astype(f32)
+    fars = [trade(fars[0], groups, 1), trade(fars[1], groups, 2)]
+    inward, outward = [(own[None], beside[None], far) for own, beside, far in zip(owns, besides, fars)]
     mixed = [
-        combine(pass_on(results[step], devices), saved[step][5], slots[step], saved[step][7], blocks)
+        combine(results[step], saved[step][5], slots[step], saved[step][7], blocks, slot_count)
         for step in range(MICRO)
     ]
-    thin = total[:, 4 * D :]
+    (total,) = tie([total], mixed[0])
     grad_in = spread_pieces(place, inward, 1).reshape(expert_in.shape)
     grad_out = spread_pieces(place, outward, 2).reshape(expert_out.shape)
+    total = reduce_group(total, groups, grad_in, grad_out)
+    thin = total[:, 4 * D :]
     return (
         jnp.concatenate(mixed, axis=0),
         jnp.concatenate(token_grads, axis=0),

time: 669 us -> 606 us (0.906)
  waiting for transfers between devices: 267 us -> 239 us
  Pallas kernels: 274 us -> 256 us
  local copies, waits for them, and re-layouts: 48.8 us -> 32.4 us
    ppermute x21 -> x24, waiting for transfers between devices: 122 us -> 153 us  [send(): lax.ppermute(blocks[j], 'expert', swap(devices, 2 * j))]
    ppermute x8, waiting for transfers between devices: 46.5 us -> 22.3 us  [trade(): return lax.ppermute(value, 'group', swap(groups, mask))]
    ppermute x2, waiting for transfers between devices: 32.7 us -> 10.2 us  [reduce_group(): lax.ppermute(low, 'group', swap(groups, mask)).astype(f32)]
    pallas_call x2, Pallas kernels: 136 us -> 121 us  [run_expert(): pl.pallas_call(functools.partial(expert_kernel, blocks=blocks, passes=pas...]
    concatenate x1, local copies, waits for them, and re-layouts: 14.1 us -> 0.77 us  [gather_weights(): passed, = tie([jnp.concatenate(own, axis=0)], *blocks[1:])]
    ppermute x8 -> x12, waiting for transfers between devices: 49 us -> 43.6 us  [the longest x3 24.5 us: sum_chips(): lax.ppermute(low[j * rows:(j + 1) * rows], 'expert', swap(devices, 2 * j))]
    unnamed x141 -> x145, local copies, waits for them, and re-layouts: 16.1 us -> 20.3 us
    ppermute x21 -> x24, starting transfers between devices: 26.6 us -> 29.9 us  [send(): lax.ppermute(blocks[j], 'expert', swap(devices, 2 * j))]
  transfers between devices with their start and end apart: 49 -> 55, of which waited for: 22 -> 24; matrix products, arithmetic and copies ran while one was open for 4% -> 3% of each run, Pallas kernels for 41% -> 43%
where the time goes in v2:
time: 606 us; the launch traced here: 601 us
  Pallas kernels  256 us (42%)
  waiting for transfers between devices  239 us (39%)
  starting transfers between devices  52.2 us (9%)
  local copies, waits for them, and re-layouts  32.4 us (5%)
  other arithmetic  19 us (3%)
    ppermute x24, waiting for transfers between devices, send(): lax.ppermute(blocks[j], 'expert', swap(devices, 2 * j))  153 us
    pallas_call x2, Pallas kernels, run_expert(): pl.pallas_call(functools.partial(expert_kernel, blocks=blocks, passes=pas...  121 us
    pallas_call x2, Pallas kernels, backward(): pl.pallas_call(functools.partial(back_kernel, blocks=blocks, passes=passe...  67.2 us
    pallas_call x2, Pallas kernels, attend(): pl.pallas_call(functools.partial(attend_kernel, step=step, experts=expert...  46.6 us
    ppermute x24, starting transfers between devices, send(): lax.ppermute(blocks[j], 'expert', swap(devices, 2 * j))  29.9 us
    ppermute x3, waiting for transfers between devices, sum_chips(): lax.ppermute(low[j * rows:(j + 1) * rows], 'expert', swap(devices, 2 * j))  24.5 us
    ppermute x8, waiting for transfers between devices, trade(): return lax.ppermute(value, 'group', swap(groups, mask))  22.3 us
    unnamed x145, local copies, waits for them, and re-layouts  20.3 us
  transfers between devices with their start and end apart: 55, of which 24 were waited for; matrix products, arithmetic and copies ran while one was open for 3% of the time, Pallas kernels for 43%

profile of v2, /device:TPU:8, one launch (start us, length us, event | category | flops | bytes accessed | tf_op | source)
XLA Modules:
  0.0 601.0 jit_solution(14090442561470686087)
XLA Ops:
  4.6 3.1 collective-permute-start.2
  11.0 3.8 route.1
  15.6 6.5 %collective-permute-done.1 = bf16[112,768]{1,0:T(8,128)(2,1)S(1)} collective-permute-done((bf16[112,768]{1,0:T(8,128)(2,1)S(1)}, bf16[112,768]{1,0:T(8,128)(2,1)S(1)}, u32[]{:S(2)}, u32[]{:S(2)}) %collective-permute-start.1) | collective-permute-done | bytes 172064 | tf_op jit(solution)/shard_map/ppermute | solution.py:211
  26.7 3.4 collective-permute-start.5
  30.8 6.9 %collective-permute-done.4.refs_2_ = bf16[384,768]{1,0:T(8,128)(2,1)S(1)} collective-permute-done((bf16[384,768]{1,0:T(8,128)(2,1)S(1)}, bf16[384,768]{1,0:T(8,128)(2,1)S(1)}, u32[]{:S(2)}, u32[]{:S(2)}) %collective-permute-start.4) | collective-permute-done | bytes 589856 | tf_op jit(solution)/shard_map/ppermute | solution.py:216
  39.0 15.7 %collective-permute-done.5.refs_6_ = bf16[384,768]{1,0:T(8,128)(2,1)S(1)} collective-permute-done((bf16[384,768]{1,0:T(8,128)(2,1)S(1)}, bf16[384,768]{1,0:T(8,128)(2,1)S(1)}, u32[]{:S(2)}, u32[]{:S(2)}) %collective-permute-start.5) | collective-permute-done | bytes 589856 | tf_op jit(solution)/shard_map/ppermute | solution.py:765
  57.6 5.7 collective-permute-done.6
  64.8 15.0 %collective-permute-done.9.refs_7_ = bf16[384,768]{1,0:T(8,128)(2,1)S(1)} collective-permute-done((bf16[384,768]{1,0:T(8,128)(2,1)S(1)}, bf16[384,768]{1,0:T(8,128)(2,1)S(1)}, u32[]{:S(2)}, u32[]{:S(2)}) %collective-permute-start.9) | collective-permute-done | bytes 589856 | tf_op jit(solution)/shard_map/ppermute | solution.py:765
  90.4 23.4 %attend.3 = (bf16[768,512]{1,0:T(8,128)(2,1)S(1)}, bf16[768,512]{1,0:T(8,128)(2,1)S(1)}, bf16[768,512]{1,0:T(8,128)(2,1)S(1)}, bf16[12,512,512]{2,1,0:T(8,128)(2...) custom-call(s32[2]{0:T(128)S(1)} %copy-done.35, ...), custom_call_target="tpu_custom_call" | custom-call | bytes 82800000 | tf_op jit(solution)/shard_map/attend/pallas_call | solution.py:347
  118.5 23.2 %attend.2 = (bf16[768,512]{1,0:T(8,128)(2,1)S(1)}, bf16[768,512]{1,0:T(8,128)(2,1)S(1)}, bf16[768,512]{1,0:T(8,128)(2,1)S(1)}, bf16[12,512,512]{2,1,0:T(8,128)(2...) custom-call(s32[2]{0:T(128)S(1)} %copy-done.35, ...), custom_call_target="tpu_custom_call" | custom-call | bytes 82800000 | tf_op jit(solution)/shard_map/attend/pallas_call | solution.py:347
  155.3 16.4 %collective-permute-done.16.refs_1_ = bf16[384,768]{1,0:T(8,128)(2,1)S(1)} collective-permute-done((bf16[384,768]{1,0:T(8,128)(2,1)S(1)}, bf16[384,768]{1,0:T(8,128)(2,1)S(1)}, u32[]{:S(2)}, u32[]{:S(2)}) %collective-permute-start.16) | collective-permute-done | bytes 589856 | tf_op jit(solution)/shard_map/ppermute | solution.py:765
  171.7 15.6 %collective-permute-done.17.refs_2_ = bf16[384,768]{1,0:T(8,128)(2,1)} collective-permute-done((bf16[384,768]{1,0:T(8,128)(2,1)S(1)}, bf16[384,768]{1,0:T(8,128)(2,1)}, u32[]{:S(2)}, u32[]{:S(2)}) %collective-permute-start.17) | collective-permute-done | bytes 589856 | tf_op jit(solution)/shard_map/ppermute | solution.py:765
  187.3 13.8 %collective-permute-done.18.refs_3_ = bf16[384,768]{1,0:T(8,128)(2,1)} collective-permute-done((bf16[384,768]{1,0:T(8,128)(2,1)S(1)}, bf16[384,768]{1,0:T(8,128)(2,1)}, u32[]{:S(2)}, u32[]{:S(2)}) %collective-permute-start.18) | collective-permute-done | bytes 589856 | tf_op jit(solution)/shard_map/ppermute | solution.py:765
  206.9 59.1 %expert.2 = (bf16[2,192,3072]{2,1,0:T(8,128)(2,1)}, bf16[2,192,3072]{2,1,0:T(8,128)(2,1)}, bf16[2,768,768]{2,1,0:T(8,128)(2,1)}, bf16[2,768,768]{2,1,0:T(8,128)(...) custom-call(s32[3]{0:T(128)} %pad_add_fusion.place_ref, ...), custom_call_target="tpu_custom_call" | custom-call | bytes 223200000 | tf_op jit(solution)/shard_map/expert/pallas_call | solution.py:491
  270.3 61.5 %expert.3 = (bf16[2,192,3072]{2,1,0:T(8,128)(2,1)}, bf16[2,192,3072]{2,1,0:T(8,128)(2,1)}, bf16[2,768,768]{2,1,0:T(8,128)(2,1)}, bf16[2,768,768]{2,1,0:T(8,128)(...) custom-call(s32[3]{0:T(128)} %pad_add_fusion.place_ref, ...), custom_call_target="tpu_custom_call" | custom-call | bytes 223200000 | tf_op jit(solution)/shard_map/expert/pallas_call | solution.py:491
  339.7 32.3 %backward.2 = (bf16[512,768]{1,0:T(8,128)(2,1)}, bf16[384,3200]{1,0:T(8,128)(2,1)}, bf16[384,3200]{1,0:T(8,128)(2,1)}) custom-call(s32[1]{0:T(128)} %bitcast.me_ref.refs_0_, bf16[384,768]{1,0:T(8,128)(2,1)} %get-tuple-element.245.refs_1_, bf16[384,768]{1,0:T(8,128)(2,1)} %copy-done.50, bf16[384,768]{1,0:T(8,128)(2,1)} %copy-done.52, ...), custom_call_target="tpu_custom_call" | custom-call | bytes 122400000 | tf_op jit(solution)/shard_map/backward/pallas_call | solution.py:685
  372.1 5.4 collective-permute-done.30.refs_3_
  377.5 13.5 %collective-permute-done.31.refs_4_ = bf16[384,768]{1,0:T(8,128)(2,1)S(1)} collective-permute-done((bf16[384,768]{1,0:T(8,128)(2,1)}, bf16[384,768]{1,0:T(8,128)(2,1)S(1)}, u32[]{:S(2)}, u32[]{:S(2)}) %collective-permute-start.31) | collective-permute-done | bytes 589856 | tf_op jit(solution)/shard_map/ppermute | solution.py:765
  406.5 34.9 %backward.3 = (bf16[512,768]{1,0:T(8,128)(2,1)}, bf16[384,3200]{1,0:T(8,128)(2,1)}, bf16[384,3200]{1,0:T(8,128)(2,1)}) custom-call(s32[1]{0:T(128)} %bitcast.me_ref.refs_0_, bf16[384,768]{1,0:T(8,128)(2,1)} %get-tuple-element.279.refs_1_, bf16[384,768]{1,0:T(8,128)(2,1)} %copy-done.48, bf16[384,768]{1,0:T(8,128)(2,1)} %copy-done.49, ...), custom_call_target="tpu_custom_call" | custom-call | bytes 122400000 | tf_op jit(solution)/shard_map/backward/pallas_call | solution.py:685
  441.4 12.2 %collective-permute-done.35.refs_3_ = bf16[384,768]{1,0:T(8,128)(2,1)S(1)} collective-permute-done((bf16[384,768]{1,0:T(8,128)(2,1)S(1)}, bf16[384,768]{1,0:T(8,128)(2,1)S(1)}, u32[]{:S(2)}, u32[]{:S(2)}) %collective-permute-start.35) | collective-permute-done | bytes 589856 | tf_op jit(solution)/shard_map/ppermute | solution.py:765
  455.9 4.9 collective-permute-done.41
  464.5 3.7 collective-permute-start.43
  468.3 21.1 %collective-permute-done.50 = bf16[192,3072]{1,0:T(8,128)(2,1)S(1)} collective-permute-done((bf16[192,3072]{1,0:T(8,128)(2,1)S(1)}, bf16[192,3072]{1,0:T(8,128)(2,1)S(1)}, u32[]{:S(2)}, u32[]{:S(2)}) %collective-permute-start.50) | collective-permute-done | bytes 1179680 | tf_op jit(solution)/shard_map/ppermute | solution.py:522
  492.3 14.7 %collective-permute-done.44 = bf16[96,3200]{1,0:T(8,128)(2,1)S(1)} collective-permute-done((bf16[96,3200]{1,0:T(8,128)(2,1)S(1)}, bf16[96,3200]{1,0:T(8,128)(2,1)S(1)}, u32[]{:S(2)}, u32[]{:S(2)}) %collective-permute-start.44) | collective-permute-done | bytes 614432 | tf_op jit(solution)/shard_map/ppermute | solution.py:792
  507.1 9.8 %collective-permute-done.43 = bf16[96,3200]{1,0:T(8,128)(2,1)S(1)} collective-permute-done((bf16[96,3200]{1,0:T(8,128)(2,1)S(1)}, bf16[96,3200]{1,0:T(8,128)(2,1)S(1)}, u32[]{:S(2)}, u32[]{:S(2)}) %collective-permute-start.43) | collective-permute-done | bytes 614432 | tf_op jit(solution)/shard_map/ppermute | solution.py:792
  517.1 3.4 collective-permute-start.45
  525.2 18.0 %collective-permute-done.45.refs_1_ = bf16[384,768]{1,0:T(8,128)(2,1)S(1)} collective-permute-done((bf16[384,768]{1,0:T(8,128)(2,1)S(1)}, bf16[384,768]{1,0:T(8,128)(2,1)S(1)}, u32[]{:S(2)}, u32[]{:S(2)}) %collective-permute-start.45) | collective-permute-done | bytes 589856 | tf_op jit(solution)/shard_map/ppermute | solution.py:765
  544.8 15.0 %collective-permute-done.46.refs_2_ = bf16[384,768]{1,0:T(8,128)(2,1)S(1)} collective-permute-done((bf16[384,768]{1,0:T(8,128)(2,1)S(1)}, bf16[384,768]{1,0:T(8,128)(2,1)S(1)}, u32[]{:S(2)}, u32[]{:S(2)}) %collective-permute-start.46) | collective-permute-done | bytes 589856 | tf_op jit(solution)/shard_map/ppermute | solution.py:765
  559.8 12.2 %collective-permute-done.47.refs_3_ = bf16[384,768]{1,0:T(8,128)(2,1)S(1)} collective-permute-done((bf16[384,768]{1,0:T(8,128)(2,1)S(1)}, bf16[384,768]{1,0:T(8,128)(2,1)S(1)}, u32[]{:S(2)}, u32[]{:S(2)}) %collective-permute-start.47) | collective-permute-done | bytes 589856 | tf_op jit(solution)/shard_map/ppermute | solution.py:765
  572.4 4.5 spread.3
  576.8 4.5 spread.2
  587.4 10.2 %collective-permute-done.54 = bf16[96,3200]{1,0:T(8,128)(2,1)S(1)} collective-permute-done((bf16[96,3200]{1,0:T(8,128)(2,1)S(1)}, bf16[96,3200]{1,0:T(8,128)(2,1)S(1)}, u32[]{:S(2)}, u32[]{:S(2)}) %collective-permute-start.54) | collective-permute-done | bytes 614432 | tf_op jit(solution)/shard_map/ppermute | solution.py:802
  (323 shorter events, 105.4 us)
Async XLA Ops:
  30.1 34.7 %collective-permute-start.8 = (bf16[384,768]{1,0:T(8,128)(2,1)S(1)}, bf16[384,768]{1,0:T(8,128)(2,1)S(1)}, u32[]{:S(2)}, u32[]{:S(2)}) collective-permute-start(bf16[384,768]{1,0:T(8,128)(2,1)S(1)} %get-tuple-element.172), channel_id=1, source_target_pairs={{0,2},{1,3},{2,0},{3,1},{4,6},{5,7},{6,4},{7,5},{8,10},{9,11},{10,... | collective-permute-start | bytes 1769480 | tf_op jit(solution)/shard_map/ppermute | solution.py:765
  30.1 49.7 %collective-permute-start.9 = (bf16[384,768]{1,0:T(8,128)(2,1)S(1)}, bf16[384,768]{1,0:T(8,128)(2,1)S(1)}, u32[]{:S(2)}, u32[]{:S(2)}) collective-permute-start(bf16[384,768]{1,0:T(8,128)(2,1)S(1)} %get-tuple-element.173), channel_id=1, source_target_pairs={{0,6},{1,7},{2,4},{3,5},{4,2},{5,3},{6,0},{7,1},{8,14},{9,15},{10,... | collective-permute-start | bytes 1769480 | tf_op jit(solution)/shard_map/ppermute | solution.py:765
  79.8 61.9 %collective-permute-start.12 = (bf16[384,768]{1,0:T(8,128)(2,1)}, bf16[384,768]{1,0:T(8,128)(2,1)}, u32[]{:S(2)}, u32[]{:S(2)}) collective-permute-start(bf16[384,768]{1,0:T(8,128)(2,1)} %get-tuple-element.187), channel_id=1, source_target_pairs={{0,2},{1,3},{2,0},{3,1},{4,6},{5,7},{6,4},{7,5},{8,10},{9,11},{10,... | collective-permute-start | bytes 1769480 | tf_op jit(solution)/shard_map/ppermute | solution.py:765
  79.8 61.9 %collective-permute-start.13 = (bf16[384,768]{1,0:T(8,128)(2,1)}, bf16[384,768]{1,0:T(8,128)(2,1)}, u32[]{:S(2)}, u32[]{:S(2)}) collective-permute-start(bf16[384,768]{1,0:T(8,128)(2,1)} %get-tuple-element.188), channel_id=1, source_target_pairs={{0,4},{1,5},{2,6},{3,7},{4,0},{5,1},{6,2},{7,3},{8,12},{9,13},{10,... | collective-permute-start | bytes 1769480 | tf_op jit(solution)/shard_map/ppermute | solution.py:765
  81.7 60.0 %collective-permute-start.14 = (bf16[384,768]{1,0:T(8,128)(2,1)}, bf16[384,768]{1,0:T(8,128)(2,1)}, u32[]{:S(2)}, u32[]{:S(2)}) collective-permute-start(bf16[384,768]{1,0:T(8,128)(2,1)} %get-tuple-element.189), channel_id=1, source_target_pairs={{0,6},{1,7},{2,4},{3,5},{4,2},{5,3},{6,0},{7,1},{8,14},{9,15},{10,... | collective-permute-start | bytes 1769480 | tf_op jit(solution)/shard_map/ppermute | solution.py:765
  144.7 62.2 %collective-permute-start.19 = (bf16[768,768]{1,0:T(8,128)(2,1)S(1)}, bf16[768,768]{1,0:T(8,128)(2,1)}, u32[]{:S(2)}, u32[]{:S(2)}) collective-permute-start(bf16[768,768]{1,0:T(8,128)(2,1)S(1)} %pad_maximum_fusion.4), channel_id=1, source_target_pairs={{0,1},{1,0},{2,3},{3,2},{4,5},{5,4},{6,7},{7,6},{8,9},{9,8},{10,11... | collective-permute-start | bytes 3538952 | tf_op jit(solution)/shard_map/ppermute | solution.py:780
  147.3 40.0 %collective-permute-start.17 = (bf16[384,768]{1,0:T(8,128)(2,1)S(1)}, bf16[384,768]{1,0:T(8,128)(2,1)}, u32[]{:S(2)}, u32[]{:S(2)}) collective-permute-start(bf16[384,768]{1,0:T(8,128)(2,1)S(1)} %get-tuple-element.199), channel_id=1, source_target_pairs={{0,4},{1,5},{2,6},{3,7},{4,0},{5,1},{6,2},{7,3},{8,12},{9,13},{10,... | collective-permute-start | bytes 1769480 | tf_op jit(solution)/shard_map/ppermute | solution.py:765
  148.3 52.8 %collective-permute-start.18 = (bf16[384,768]{1,0:T(8,128)(2,1)S(1)}, bf16[384,768]{1,0:T(8,128)(2,1)}, u32[]{:S(2)}, u32[]{:S(2)}) collective-permute-start(bf16[384,768]{1,0:T(8,128)(2,1)S(1)} %get-tuple-element.200), channel_id=1, source_target_pairs={{0,6},{1,7},{2,4},{3,5},{4,2},{5,3},{6,0},{7,1},{8,14},{9,15},{10,... | collective-permute-start | bytes 1769480 | tf_op jit(solution)/shard_map/ppermute | solution.py:765
  201.1 64.9 %collective-permute-start.21 = (bf16[384,768]{1,0:T(8,128)(2,1)}, bf16[384,768]{1,0:T(8,128)(2,1)S(1)}, u32[]{:S(2)}, u32[]{:S(2)}) collective-permute-start(bf16[384,768]{1,0:T(8,128)(2,1)} %get-tuple-element.215), channel_id=1, source_target_pairs={{0,2},{1,3},{2,0},{3,1},{4,6},{5,7},{6,4},{7,5},{8,10},{9,11},{10,... | collective-permute-start | bytes 1769480 | tf_op jit(solution)/shard_map/ppermute | solution.py:765
  201.1 64.9 %collective-permute-start.22 = (bf16[384,768]{1,0:T(8,128)(2,1)}, bf16[384,768]{1,0:T(8,128)(2,1)}, u32[]{:S(2)}, u32[]{:S(2)}) collective-permute-start(bf16[384,768]{1,0:T(8,128)(2,1)} %get-tuple-element.216), channel_id=1, source_target_pairs={{0,4},{1,5},{2,6},{3,7},{4,0},{5,1},{6,2},{7,3},{8,12},{9,13},{10,... | collective-permute-start | bytes 1769480 | tf_op jit(solution)/shard_map/ppermute | solution.py:765
  203.0 63.0 %collective-permute-start.23 = (bf16[384,768]{1,0:T(8,128)(2,1)}, bf16[384,768]{1,0:T(8,128)(2,1)}, u32[]{:S(2)}, u32[]{:S(2)}) collective-permute-start(bf16[384,768]{1,0:T(8,128)(2,1)} %get-tuple-element.217), channel_id=1, source_target_pairs={{0,6},{1,7},{2,4},{3,5},{4,2},{5,3},{6,0},{7,1},{8,14},{9,15},{10,... | collective-permute-start | bytes 1769480 | tf_op jit(solution)/shard_map/ppermute | solution.py:765
  205.7 64.6 %collective-permute-start.24 = (bf16[768,768]{1,0:T(8,128)(2,1)}, bf16[768,768]{1,0:T(8,128)(2,1)}, u32[]{:S(2)}, u32[]{:S(2)}) collective-permute-start(bf16[768,768]{1,0:T(8,128)(2,1)} %pad_maximum_fusion.5), channel_id=1, source_target_pairs={{0,1},{1,0},{2,3},{3,2},{4,5},{5,4},{6,7},{7,6},{8,9},{9,8},{10,11... | collective-permute-start | bytes 3538952 | tf_op jit(solution)/shard_map/ppermute | solution.py:780
  266.8 65.0 %collective-permute-start.25 = (bf16[384,768]{1,0:T(8,128)(2,1)}, bf16[384,768]{1,0:T(8,128)(2,1)S(1)}, u32[]{:S(2)}, u32[]{:S(2)}) collective-permute-start(bf16[384,768]{1,0:T(8,128)(2,1)} %get-tuple-element.241), channel_id=1, source_target_pairs={{0,2},{1,3},{2,0},{3,1},{4,6},{5,7},{6,4},{7,5},{8,10},{9,11},{10,... | collective-permute-start | bytes 1769480 | tf_op jit(solution)/shard_map/ppermute | solution.py:765
  267.7 64.2 %collective-permute-start.26 = (bf16[384,768]{1,0:T(8,128)(2,1)}, bf16[384,768]{1,0:T(8,128)(2,1)S(1)}, u32[]{:S(2)}, u32[]{:S(2)}) collective-permute-start(bf16[384,768]{1,0:T(8,128)(2,1)} %get-tuple-element.242), channel_id=1, source_target_pairs={{0,4},{1,5},{2,6},{3,7},{4,0},{5,1},{6,2},{7,3},{8,12},{9,13},{10,... | collective-permute-start | bytes 1769480 | tf_op jit(solution)/shard_map/ppermute | solution.py:765
  268.8 63.2 %collective-permute-start.27 = (bf16[384,768]{1,0:T(8,128)(2,1)}, bf16[384,768]{1,0:T(8,128)(2,1)}, u32[]{:S(2)}, u32[]{:S(2)}) collective-permute-start(bf16[384,768]{1,0:T(8,128)(2,1)} %get-tuple-element.243), channel_id=1, source_target_pairs={{0,6},{1,7},{2,4},{3,5},{4,2},{5,3},{6,0},{7,1},{8,14},{9,15},{10,... | collective-permute-start | bytes 1769480 | tf_op jit(solution)/shard_map/ppermute | solution.py:765
  333.4 58.5 %collective-permute-start.36 = (bf16[2,192,3072]{2,1,0:T(8,128)(2,1)}, bf16[2,192,3072]{2,1,0:T(8,128)(2,1)}, u32[]{:S(2)}, u32[]{:S(2)}) collective-permute-start(bf16[2,192,3072]{2,1,0:T(8,128)(2,1)} %get-tuple-element.274), channel_id=1, source_target_pairs={{0,8},{8,0},{16,24},{24,16},{1,9},{9,1},{17,25},{25,17},{2,10},{10... | collective-permute-start | bytes 7077896 | tf_op jit(solution)/shard_map/ppermute | solution.py:522
  334.0 57.9 %collective-permute-start.37 = (bf16[2,768,768]{2,1,0:T(8,128)(2,1)}, bf16[2,768,768]{2,1,0:T(8,128)(2,1)S(1)}, u32[]{:S(2)}, u32[]{:S(2)}) collective-permute-start(bf16[2,768,768]{2,1,0:T(8,128)(2,1)} %get-tuple-element.275), channel_id=1, source_target_pairs={{0,16},{8,24},{16,0},{24,8},{1,17},{9,25},{17,1},{25,9},{2,18},{10... | collective-permute-start | bytes 7077896 | tf_op jit(solution)/shard_map/ppermute | solution.py:522
  336.2 35.8 %collective-permute-start.29 = (bf16[384,768]{1,0:T(8,128)(2,1)}, bf16[384,768]{1,0:T(8,128)(2,1)S(1)}, u32[]{:S(2)}, u32[]{:S(2)}) collective-permute-start(bf16[384,768]{1,0:T(8,128)(2,1)} %get-tuple-element.250), channel_id=1, source_target_pairs={{0,2},{1,3},{2,0},{3,1},{4,6},{5,7},{6,4},{7,5},{8,10},{9,11},{10,... | collective-permute-start | bytes 1769480 | tf_op jit(solution)/shard_map/ppermute | solution.py:765
  338.1 39.5 %collective-permute-start.30 = (bf16[384,768]{1,0:T(8,128)(2,1)}, bf16[384,768]{1,0:T(8,128)(2,1)S(1)}, u32[]{:S(2)}, u32[]{:S(2)}) collective-permute-start(bf16[384,768]{1,0:T(8,128)(2,1)} %get-tuple-element.251), channel_id=1, source_target_pairs={{0,4},{1,5},{2,6},{3,7},{4,0},{5,1},{6,2},{7,3},{8,12},{9,13},{10,... | collective-permute-start | bytes 1769480 | tf_op jit(solution)/shard_map/ppermute | solution.py:765
  338.2 52.9 %collective-permute-start.31 = (bf16[384,768]{1,0:T(8,128)(2,1)}, bf16[384,768]{1,0:T(8,128)(2,1)S(1)}, u32[]{:S(2)}, u32[]{:S(2)}) collective-permute-start(bf16[384,768]{1,0:T(8,128)(2,1)} %get-tuple-element.252), channel_id=1, source_target_pairs={{0,6},{1,7},{2,4},{3,5},{4,2},{5,3},{6,0},{7,1},{8,14},{9,15},{10,... | collective-permute-start | bytes 1769480 | tf_op jit(solution)/shard_map/ppermute | solution.py:765
  398.7 55.0 %collective-permute-start.39 = (bf16[192,3072]{1,0:T(8,128)(2,1)}, bf16[192,3072]{1,0:T(8,128)(2,1)S(1)}, u32[]{:S(2)}, u32[]{:S(2)}) collective-permute-start(bf16[192,3072]{1,0:T(8,128)(2,1)} %slice_bitcast_fusion.2), channel_id=1, source_target_pairs={{0,16},{8,24},{16,0},{24,8},{1,17},{9,25},{17,1},{25,9},{2,18},{10... | collective-permute-start | bytes 3538952 | tf_op jit(solution)/shard_map/ppermute | solution.py:522
  399.2 42.2 %collective-permute-start.33 = (bf16[384,768]{1,0:T(8,128)(2,1)}, bf16[384,768]{1,0:T(8,128)(2,1)S(1)}, u32[]{:S(2)}, u32[]{:S(2)}) collective-permute-start(bf16[384,768]{1,0:T(8,128)(2,1)} %get-tuple-element.265), channel_id=1, source_target_pairs={{0,2},{1,3},{2,0},{3,1},{4,6},{5,7},{6,4},{7,5},{8,10},{9,11},{10,... | collective-permute-start | bytes 1769480 | tf_op jit(solution)/shard_map/ppermute | solution.py:765
  399.2 42.2 %collective-permute-start.34 = (bf16[384,768]{1,0:T(8,128)(2,1)}, bf16[384,768]{1,0:T(8,128)(2,1)S(1)}, u32[]{:S(2)}, u32[]{:S(2)}) collective-permute-start(bf16[384,768]{1,0:T(8,128)(2,1)} %get-tuple-element.266), channel_id=1, source_target_pairs={{0,4},{1,5},{2,6},{3,7},{4,0},{5,1},{6,2},{7,3},{8,12},{9,13},{10,... | collective-permute-start | bytes 1769480 | tf_op jit(solution)/shard_map/ppermute | solution.py:765
  401.2 52.4 %collective-permute-start.35 = (bf16[384,768]{1,0:T(8,128)(2,1)S(1)}, bf16[384,768]{1,0:T(8,128)(2,1)S(1)}, u32[]{:S(2)}, u32[]{:S(2)}) collective-permute-start(bf16[384,768]{1,0:T(8,128)(2,1)S(1)} %copy-done.68), channel_id=1, source_target_pairs={{0,6},{1,7},{2,4},{3,5},{4,2},{5,3},{6,0},{7,1},{8,14},{9,15},{10,... | collective-permute-start | bytes 1769480 | tf_op jit(solution)/shard_map/ppermute | solution.py:765
  405.9 48.2 %collective-permute-start.40 = (bf16[768,768]{1,0:T(8,128)(2,1)}, bf16[768,768]{1,0:T(8,128)(2,1)}, u32[]{:S(2)}, u32[]{:S(2)}) collective-permute-start(bf16[768,768]{1,0:T(8,128)(2,1)} %slice_bitcast_fusion), channel_id=1, source_target_pairs={{0,8},{8,0},{16,24},{24,16},{1,9},{9,1},{17,25},{25,17},{2,10},{10... | collective-permute-start | bytes 3538952 | tf_op jit(solution)/shard_map/ppermute | solution.py:522
  463.9 43.2 %collective-permute-start.44 = (bf16[96,3200]{1,0:T(8,128)(2,1)S(1)}, bf16[96,3200]{1,0:T(8,128)(2,1)S(1)}, u32[]{:S(2)}, u32[]{:S(2)}) collective-permute-start(bf16[96,3200]{1,0:T(8,128)(2,1)S(1)} %get-tuple-element.349), channel_id=1, source_target_pairs={{0,6},{1,7},{2,4},{3,5},{4,2},{5,3},{6,0},{7,1},{8,14},{9,15},{10,... | collective-permute-start | bytes 1843208 | tf_op jit(solution)/shard_map/ppermute | solution.py:792
  464.5 52.4 %collective-permute-start.43 = (bf16[96,3200]{1,0:T(8,128)(2,1)S(1)}, bf16[96,3200]{1,0:T(8,128)(2,1)S(1)}, u32[]{:S(2)}, u32[]{:S(2)}) collective-permute-start(bf16[96,3200]{1,0:T(8,128)(2,1)S(1)} %get-tuple-element.350), channel_id=1, source_target_pairs={{0,4},{1,5},{2,6},{3,7},{4,0},{5,1},{6,2},{7,3},{8,12},{9,13},{10,... | collective-permute-start | bytes 1843208 | tf_op jit(solution)/shard_map/ppermute | solution.py:792
  489.5 31.2 %collective-permute-start.38 = (bf16[768,768]{1,0:T(8,128)(2,1)S(1)}, bf16[768,768]{1,0:T(8,128)(2,1)S(1)}, u32[]{:S(2)}, u32[]{:S(2)}) collective-permute-start(bf16[768,768]{1,0:T(8,128)(2,1)S(1)} %pad_maximum_fusion.8), channel_id=1, source_target_pairs={{0,1},{1,0},{2,3},{3,2},{4,5},{5,4},{6,7},{7,6},{8,9},{9,8},{10,11... | collective-permute-start | bytes 3538952 | tf_op jit(solution)/shard_map/ppermute | solution.py:780
  490.8 86.0 %collective-permute-start.51 = (bf16[2,192,3072]{2,1,0:T(8,128)(2,1)S(1)}, bf16[2,192,3072]{2,1,0:T(8,128)(2,1)S(1)}, u32[]{:S(2)}, u32[]{:S(2)}) collective-permute-start(bf16[2,192,3072]{2,1,0:T(8,128)(2,1)S(1)} %pad_maximum_fusion), channel_id=1, source_target_pairs={{0,8},{8,0},{16,24},{24,16},{1,9},{9,1},{17,25},{25,17},{2,10},{10... | collective-permute-start | bytes 7077896 | tf_op jit(solution)/shard_map/ppermute | solution.py:522
  491.7 80.6 %collective-permute-start.53 = (bf16[2,768,768]{2,1,0:T(8,128)(2,1)S(1)}, bf16[2,768,768]{2,1,0:T(8,128)(2,1)S(1)}, u32[]{:S(2)}, u32[]{:S(2)}) collective-permute-start(bf16[2,768,768]{2,1,0:T(8,128)(2,1)S(1)} %pad_maximum_fusion.1), channel_id=1, source_target_pairs={{0,16},{8,24},{16,0},{24,8},{1,17},{9,25},{17,1},{25,9},{2,18},{10... | collective-permute-start | bytes 7077896 | tf_op jit(solution)/shard_map/ppermute | solution.py:522
  520.6 39.2 %collective-permute-start.46 = (bf16[384,768]{1,0:T(8,128)(2,1)S(1)}, bf16[384,768]{1,0:T(8,128)(2,1)S(1)}, u32[]{:S(2)}, u32[]{:S(2)}) collective-permute-start(bf16[384,768]{1,0:T(8,128)(2,1)S(1)} %copy-done.66), channel_id=1, source_target_pairs={{0,4},{1,5},{2,6},{3,7},{4,0},{5,1},{6,2},{7,3},{8,12},{9,13},{10,... | collective-permute-start | bytes 1769480 | tf_op jit(solution)/shard_map/ppermute | solution.py:765
  520.7 51.3 %collective-permute-start.47 = (bf16[384,768]{1,0:T(8,128)(2,1)S(1)}, bf16[384,768]{1,0:T(8,128)(2,1)S(1)}, u32[]{:S(2)}, u32[]{:S(2)}) collective-permute-start(bf16[384,768]{1,0:T(8,128)(2,1)S(1)} %copy-done.65), channel_id=1, source_target_pairs={{0,6},{1,7},{2,4},{3,5},{4,2},{5,3},{6,0},{7,1},{8,14},{9,15},{10,... | collective-permute-start | bytes 1769480 | tf_op jit(solution)/shard_map/ppermute | solution.py:765
  (101 other events, 1570.6 us)

commit v3 on v2

--- a/solution.py
+++ b/solution.py
@@ -254,33 +254,36 @@
 
 def attend_kernel(
     starts_ref, x_ref, query_w, key_w, value_w, out_w, narrow_ref, hot_ref, bucket_ref, heads_ref, ids_ref, slots_ref,
-    query_ref, key_ref, value_ref, probs_ref, attended_ref, hidden_ref, rows_ref, gates_ref, normed_ref,
-    *refs, step, experts,
+    query_ref, key_ref, value_ref, probs_ref, attended_ref, hidden_ref, gates_ref, normed_ref,
+    *refs, experts,
 ):
     block_refs, (mask_ref, table_ref) = refs[:-2], refs[-2:]
     head = pl.program_id(0)
+    spans = [slice(step * TOK_MB, (step + 1) * TOK_MB) for step in range(MICRO)]
 
     @pl.when(head == 0)
     def _():
         x = x_ref[...].astype(f32)
         scale = lax.rsqrt(jnp.mean(x * x, axis=-1, keepdims=True) + epsilon)
         normed = (x * scale * narrow_ref[experts : experts + 1, :].astype(f32)).astype(bf16)
-        normed_ref[...] = normed
         query = dot_nn(normed, query_w[0]).astype(bf16).astype(f32) * HEAD_DIM**-0.5
-        query_ref[...] = query.T.astype(bf16)
-        key_ref[...] = dot_nn(normed, key_w[0]).T.astype(bf16)
-        value_ref[...] = dot_nn(normed, value_w[0]).T.astype(bf16)
+        key, value = dot_nn(normed, key_w[0]), dot_nn(normed, value_w[0])
+        key_place, query_place = iota((SEQ_LEN, SEQ_LEN), 0), iota((SEQ_LEN, SEQ_LEN), 1)
+        for step in range(MICRO):
+            normed_ref[step] = normed[spans[step]]
+            query_ref[step] = query[spans[step]].T.astype(bf16)
+            key_ref[step] = key[spans[step]].T.astype(bf16)
+            value_ref[step] = value[spans[step]].T.astype(bf16)
+            start = starts_ref[step]
+            inside = (
+                (key_place >= start)
+                & (key_place < start + PIC)
+                & (query_place >= start)
+                & (query_place < start + PIC)
+            )
+            mask_ref[step] = jnp.where((key_place <= query_place) | inside, 0.0, -1e30)
         rel = (heads_ref[...].astype(f32) * narrow_ref[experts + 2 : experts + 3, :].astype(f32)).astype(bf16)
         table_ref[...] = dot_nn(dot_nn(rel, bucket_ref[...]).astype(bf16), hot_ref[...])
-        start = starts_ref[step]
-        key_place, query_place = iota((SEQ_LEN, SEQ_LEN), 0), iota((SEQ_LEN, SEQ_LEN), 1)
-        inside = (
-            (key_place >= start)
-            & (key_place < start + PIC)
-            & (query_place >= start)
-            & (query_place < start + PIC)
-        )
-        mask_ref[...] = jnp.where((key_place <= query_place) | inside, 0.0, -1e30)
 
     span = pl.ds(pl.multiple_of(head * HEAD_DIM, HEAD_DIM), HEAD_DIM)
     table = jnp.broadcast_to(table_ref[pl.ds(head, 1), :], (8, 1024))
@@ -289,39 +292,42 @@
         table = jnp.where((low_row & bit) != 0, pltpu.roll(table, bit, 1), table)
     for shift in (8, 16, 32, 64):
         table = jnp.concatenate([table, pltpu.roll(table, shift, 1)], axis=0)
-    scores = dot_tn(key_ref[span, :], query_ref[span, :])
     bias = jnp.concatenate([table[:, 384 - a * 128 : 896 - a * 128] for a in range(4)], axis=0)
-    scores = scores + bias + mask_ref[...]
-    expo = jnp.exp(scores - jnp.max(scores, axis=0, keepdims=True))
-    probs = (expo * (1.0 / jnp.sum(expo, axis=0, keepdims=True))).astype(bf16)
-    probs_ref[0] = probs
-    attended_ref[span, :] = dot_nn(value_ref[span, :], probs).astype(bf16)
+    for step in range(MICRO):
+        scores = dot_tn(key_ref[step, span, :], query_ref[step, span, :])
+        scores = scores + bias + mask_ref[step]
+        expo = jnp.exp(scores - jnp.max(scores, axis=0, keepdims=True))
+        probs = (expo * (1.0 / jnp.sum(expo, axis=0, keepdims=True))).astype(bf16)
+        probs_ref[step, 0] = probs
+        attended_ref[step, span, :] = dot_nn(value_ref[step, span, :], probs).astype(bf16)
 
     @pl.when(head == HEADS - 1)
     def _():
-        hidden = x_ref[...].astype(f32) + dot_tn(attended_ref[...], out_w[0])
-        hidden_ref[...] = hidden
-        scale = lax.rsqrt(jnp.mean(hidden * hidden, axis=-1, keepdims=True) + epsilon)
-        rows = (hidden * scale * narrow_ref[experts + 1 : experts + 2, :].astype(f32)).astype(bf16)
-        rows_ref[...] = rows
-        router = dot_nt(narrow_ref[:experts, :], rows)
         place = iota((experts, TOK_MB), 0)
-        chosen = [
-            jnp.sum(jnp.where(ids_ref[k : k + 1, :] == place, router, 0.0), axis=0, keepdims=True)
-            for k in range(TOP)
-        ]
-        gates_ref[0:1, :] = 1.0 / (1.0 + jnp.exp(chosen[1] - chosen[0]))
-        gates_ref[1:2, :] = 1.0 / (1.0 + jnp.exp(chosen[0] - chosen[1]))
-        half = block_refs[0].shape[0] // (4 // len(block_refs))
-        for first in range(0, 4 * half, half):
-            hots = [slot_hot(slots_ref[k : k + 1, :], first, half) for k in range(TOP)]
-            value = dot_nn(jnp.where(hots[0] | hots[1], 1.0, 0.0).astype(bf16), rows).astype(bf16)
-            low = first // 2
-            if len(block_refs) == 1:
-                block_refs[0][first : first + half, :] = value
-            else:
-                block_refs[0][low : low + half // 2, :] = value[: half // 2]
-                block_refs[1][low : low + half // 2, :] = value[half // 2 :]
+        each = len(block_refs) // MICRO
+        for step in range(MICRO):
+            hidden = x_ref[spans[step], :].astype(f32) + dot_tn(attended_ref[step], out_w[0])
+            hidden_ref[step] = hidden
+            scale = lax.rsqrt(jnp.mean(hidden * hidden, axis=-1, keepdims=True) + epsilon)
+            rows = (hidden * scale * narrow_ref[experts + 1 : experts + 2, :].astype(f32)).astype(bf16)
+            router = dot_nt(narrow_ref[:experts, :], rows)
+            chosen = [
+                jnp.sum(jnp.where(ids_ref[k : k + 1, spans[step]] == place, router, 0.0), axis=0, keepdims=True)
+                for k in range(TOP)
+            ]
+            gates_ref[step, 0:1, :] = 1.0 / (1.0 + jnp.exp(chosen[1] - chosen[0]))
+            gates_ref[step, 1:2, :] = 1.0 / (1.0 + jnp.exp(chosen[0] - chosen[1]))
+            blocks = block_refs[step * each : (step + 1) * each]
+            half = blocks[0].shape[0] // (4 // each)
+            for first in range(0, 4 * half, half):
+                hots = [slot_hot(slots_ref[step, k : k + 1, :], first, half) for k in range(TOP)]
+                value = dot_nn(jnp.where(hots[0] | hots[1], 1.0, 0.0).astype(bf16), rows).astype(bf16)
+                low = first // 2
+                if each == 1:
+                    blocks[0][first : first + half, :] = value
+                else:
+                    blocks[0][low : low + half // 2, :] = value[: half // 2]
+                    blocks[1][low : low + half // 2, :] = value[half // 2 :]
 
 
 def matrix_specs():
@@ -331,32 +337,33 @@
     ]
 
 
-def attend(starts, tokens, matrices, narrow, constants, ids, slots, step, direct, experts, capacity):
+def attend(starts, tokens, matrices, narrow, constants, ids, slots, direct, experts, capacity):
     size = experts * capacity // (1 + direct)
-    fixed = lambda h: (0, 0)
     out_shapes = (
-        [((D, TOK_MB), bf16)] * 3
-        + [((HEADS, SEQ_LEN, SEQ_LEN), bf16), ((D, TOK_MB), bf16), ((TOK_MB, D), f32), ((TOK_MB, D), bf16)]
-        + [((TOP, TOK_MB), f32), ((TOK_MB, D), bf16)]
-        + [((size, D), bf16)] * (1 + direct)
+        [((MICRO, D, TOK_MB), bf16)] * 3
+        + [((MICRO, HEADS, SEQ_LEN, SEQ_LEN), bf16), ((MICRO, D, TOK_MB), bf16), ((MICRO, TOK_MB, D), f32)]
+        + [((MICRO, TOP, TOK_MB), f32), ((MICRO, TOK_MB, D), bf16)]
+        + [((size, D), bf16)] * (MICRO * (1 + direct))
     )
+
+    def whole(shape):
+        return resident(shape, lambda h: (0,) * len(shape))
+
     out_specs = [
-        pl.BlockSpec((1, SEQ_LEN, SEQ_LEN), lambda h: (h, 0, 0)) if len(s) == 3 else resident(s, fixed)
+        pl.BlockSpec((MICRO, 1, SEQ_LEN, SEQ_LEN), lambda h: (0, h, 0, 0)) if len(s) == 4 else whole(s)
         for s, _ in out_shapes
     ]
     return pl.pallas_call(
-        functools.partial(attend_kernel, step=step, experts=experts),
+        functools.partial(attend_kernel, experts=experts),
         grid=(HEADS,),
-        in_specs=[pl.BlockSpec(memory_space=pltpu.SMEM), resident((TOK_MB, D), lambda h: (step, 0))]
+        in_specs=[pl.BlockSpec(memory_space=pltpu.SMEM), whole(tokens.shape)]
         + matrix_specs()
-        + [resident(narrow.shape, fixed)]
-        + [resident(c.shape, fixed) for c in constants]
-        + [resident((TOP, TOK_MB), lambda h: (0, step)), resident((TOP, TOK_MB), fixed)],
+        + [whole(a.shape) for a in (narrow, *constants, ids, slots)],
         out_specs=out_specs,
         out_shape=[jax.ShapeDtypeStruct(*s) for s in out_shapes],
-        scratch_shapes=[pltpu.VMEM((SEQ_LEN, SEQ_LEN), f32), pltpu.VMEM((16, 1024), f32)],
-        compiler_params=pltpu.CompilerParams(vmem_limit_bytes=48 * MIB),
-        cost_estimate=lasting(23),
+        scratch_shapes=[pltpu.VMEM((MICRO, SEQ_LEN, SEQ_LEN), f32), pltpu.VMEM((16, 1024), f32)],
+        compiler_params=pltpu.CompilerParams(vmem_limit_bytes=58 * MIB),
+        cost_estimate=lasting(42),
         name="attend",
     )(starts, tokens, *[matrices] * 4, narrow, *constants, ids, slots)
 
@@ -630,13 +637,15 @@
     query_grad[span, :] = (dot_nn(key_ref[span, :], score_grad) * HEAD_DIM**-0.5).astype(bf16)
     key_grad[span, :] = dot_nt(query_ref[span, :], score_grad).astype(bf16)
     wide = score_grad.astype(f32)
-    pieces = []
-    for a in range(4):
-        piece = wide[a * 128 : a * 128 + 128, :]
-        left, right = 384 - a * 128, 128 + a * 128
-        ends = [jnp.zeros((128, left), f32)] if left else []
-        pieces.append(jnp.concatenate(ends + [piece, jnp.zeros((128, right), f32)], axis=1))
-    folded = pieces[0] + pieces[1] + pieces[2] + pieces[3]
+    chunks = []
+    for place in range(-3, 4):
+        parts = [
+            wide[a * 128 : a * 128 + 128, (a + place) * 128 : (a + place) * 128 + 128]
+            for a in range(4)
+            if 0 <= a + place < 4
+        ]
+        chunks.append(sum(parts[1:], parts[0]))
+    folded = jnp.concatenate([*chunks, jnp.zeros((128, 128), f32)], axis=1)
     for half in (64, 32, 16, 8):
         folded = folded[:half] + pltpu.roll(folded[half:], 1024 - half, 1)
     low_row = iota((8, 1024), 0)
@@ -678,7 +687,7 @@
     size = slot_count // blocks // (1 + passes)
     fixed = lambda h: (0, 0)
     block = lambda h: (step, 0)
-    head_block = pl.BlockSpec((1, SEQ_LEN, SEQ_LEN), lambda h: (h, 0, 0))
+    head_block = pl.BlockSpec((None, 1, SEQ_LEN, SEQ_LEN), lambda h: (step, h, 0, 0))
     wide = 4 * D + 128
     dense_shapes = [(D // (1 + passes), wide)] * (1 + passes)
     dense_specs = [resident(s, fixed) for s in dense_shapes]
@@ -694,7 +703,7 @@
         + [resident(narrow.shape, fixed)]
         + [resident(c.shape, fixed) for c in constants]
         + [resident((TOP, TOK_MB), fixed)]
-        + [head_block if s.ndim == 3 else resident(s.shape, fixed) for s in saved]
+        + [head_block if s.ndim == 4 else resident((None, *s.shape[1:]), lambda h: (step, 0, 0)) for s in saved]
         + (dense_specs + [resident((experts, D), fixed)] if prior else []),
         out_specs=[resident((TOK_MB, D), fixed)] + dense_specs,
         out_shape=[jax.ShapeDtypeStruct((TOK_MB, D), bf16)] + [jax.ShapeDtypeStruct(s, bf16) for s in dense_shapes],
@@ -732,7 +741,7 @@
     mixed_ref[...] = output.astype(bf16)
 
 
-def combine(received, hidden, slots, gates, blocks, slot_count):
+def combine(received, hidden, slots, gates, step, blocks, slot_count):
     passes = len(received) - blocks
     size = slot_count // blocks // (1 + passes)
     fixed = lambda i: (0, 0)
@@ -740,7 +749,7 @@
         functools.partial(combine_kernel, blocks=blocks, passes=passes),
         grid=(1,),
         in_specs=received_specs(received, blocks, size)
-        + [resident(a.shape, fixed) for a in (hidden, slots, gates)],
+        + [resident((None, *a.shape[1:]), lambda i: (step, 0, 0)) for a in (hidden, slots, gates)],
         out_specs=resident((TOK_MB, D), fixed),
         out_shape=jax.ShapeDtypeStruct((TOK_MB, D), bf16),
         scratch_shapes=[pltpu.VMEM((slot_count, D), bf16)],
@@ -794,14 +803,17 @@
 
 
 def reduce_group(total, groups, *after):
-    mask = 1
-    while mask < groups:
-        low = total.astype(bf16)
-        if mask > 1:
-            (low,) = tie([low], *after)
-        total = low.astype(f32) + lax.ppermute(low, "group", swap(groups, mask)).astype(f32)
-        mask *= 2
-    return total
+    parts, masks = [total[:, : 2 * D], total[:, 2 * D :]], [1, 2]
+    for turn in range(2):
+        low = [part.astype(bf16) for part in parts]
+        if turn:
+            low = tie(low, *after)
+        parts = [
+            here.astype(f32) + lax.ppermute(here, "group", swap(groups, mask)).astype(f32)
+            for here, mask in zip(low, masks)
+        ]
+        masks = masks[::-1]
+    return parts
 
 
 def shards(
@@ -834,18 +846,14 @@
     if not direct:
         other = other.reshape(MICRO, 1, slot_count)
     (narrow,) = tie([narrow], *cots[0][1:], other)
-    saved, sent = [], []
-    for step in range(MICRO):
-        out = attend(
-            span_starts, tokens, matrices, narrow, constants, ids, slots[step], step, direct, experts, capacity
-        )
-        saved.append(out[:9])
-        sent.append(out[9:])
-    cots[1] = tie(cots[1], saved[0][0], saved[1][0])
+    *saved, = attend(span_starts, tokens, matrices, narrow, constants, ids, slots, direct, experts, capacity)
+    saved, sent = saved[:8], saved[8:]
+    sent = [sent[step * (1 + direct) : (step + 1) * (1 + direct)] for step in range(MICRO)]
+    cots[1] = tie(cots[1], saved[0])
     if direct:
         sent = [pair_up(*tie(s, *cots[1][1:]), devices) for s in sent]
     sent[0] = send(tie(sent[0], *cots[1][1:]), devices)
-    cots = [pass_on(tie(c, saved[1][0]), devices) for c in cots]
+    cots = [pass_on(tie(c, saved[0]), devices) for c in cots]
     sent[1] = send(tie(sent[1], *sent[0][1:]), devices)
 
     grads, first = run_expert(
@@ -864,7 +872,7 @@
     backs[1] = send(tie(backs[1], *backs[0]), devices)
 
     def run_back(step, prior):
-        query, key, value, probs, attended, hidden, _, _, normed = saved[step]
+        query, key, value, probs, attended, hidden, _, normed = saved
         return backward(
             order, backs[step], tokens, cotangent, matrices, narrow, constants, slots[step],
             (query, key, value, probs, attended, hidden, normed), prior, step, blocks, experts, devices, slot_count,
@@ -902,22 +910,23 @@
     fars = [trade(fars[0], groups, 1), trade(fars[1], groups, 2)]
     inward, outward = [(own[None], beside[None], far) for own, beside, far in zip(owns, besides, fars)]
     mixed = [
-        combine(results[step], saved[step][5], slots[step], saved[step][7], blocks, slot_count)
+        combine(results[step], saved[5], slots, saved[6], step, blocks, slot_count)
         for step in range(MICRO)
     ]
     (total,) = tie([total], mixed[0])
     grad_in = spread_pieces(place, inward, 1).reshape(expert_in.shape)
     grad_out = spread_pieces(place, outward, 2).reshape(expert_out.shape)
     total = reduce_group(total, groups, grad_in, grad_out)
-    thin = total[:, 4 * D :]
+    first, second = total
+    thin = second[:, 2 * D :]
     return (
         jnp.concatenate(mixed, axis=0),
         jnp.concatenate(token_grads, axis=0),
         thin[:, experts],
-        total[:, :D],
-        total[:, D : 2 * D],
-        total[:, 2 * D : 3 * D],
-        total[:, 3 * D : 4 * D],
+        first[:, :D],
+        first[:, D:],
+        second[:, :D],
+        second[:, D : 2 * D],
         thin[:share, experts + 2],
         thin[:, experts + 1],
         thin[:, :experts],

time: 606 us -> 602 us (level)
  Pallas kernels: 256 us -> 249 us
    ppermute x3, waiting for transfers between devices: 24.5 us -> 15.8 us  [sum_chips(): lax.ppermute(low[j * rows:(j + 1) * rows], 'expert', swap(devices, 2 * j))]
    pallas_call x2 -> x1, Pallas kernels: 46.6 us -> 39 us  [attend(): pl.pallas_call(functools.partial(attend_kernel, experts=experts), grid=(H...]
    ppermute x2 -> x4, waiting for transfers between devices: 10.2 us -> 16.5 us  [reduce_group(): lax.ppermute(here, 'group', swap(groups, mask)).astype(f32)]
    ppermute x1, waiting for transfers between devices: 1.3 us -> 7.36 us  [gather_weights(): near = lax.ppermute(mine, 'group', swap(groups, 1))]
    unnamed x145 -> x113, local copies, waits for them, and re-layouts: 20.3 us -> 15.4 us
  transfers between devices with their start and end apart: 55 -> 57, of which waited for: 24 -> 29; matrix products, arithmetic and copies ran while one was open for 3% -> 4% of each run, Pallas kernels for 43% -> 42%
where the time goes in v3:
time: 602 us; the launch traced here: 592 us
  Pallas kernels  249 us (41%)
  waiting for transfers between devices  239 us (40%)
  starting transfers between devices  50.7 us (8%)
  local copies, waits for them, and re-layouts  32.2 us (5%)
  other arithmetic  19.3 us (3%)
    ppermute x24, waiting for transfers between devices, send(): lax.ppermute(blocks[j], 'expert', swap(devices, 2 * j))  154 us
    pallas_call x2, Pallas kernels, run_expert(): pl.pallas_call(functools.partial(expert_kernel, blocks=blocks, passes=pas...  121 us
    pallas_call x2, Pallas kernels, backward(): pl.pallas_call(functools.partial(back_kernel, blocks=blocks, passes=passe...  67.4 us
    pallas_call x1, Pallas kernels, attend(): pl.pallas_call(functools.partial(attend_kernel, experts=experts), grid=(H...  39 us
    ppermute x24, starting transfers between devices, send(): lax.ppermute(blocks[j], 'expert', swap(devices, 2 * j))  30.4 us
    ppermute x8, waiting for transfers between devices, trade(): return lax.ppermute(value, 'group', swap(groups, mask))  23.2 us
    ppermute x4, waiting for transfers between devices, reduce_group(): lax.ppermute(here, 'group', swap(groups, mask)).astype(f32)  16.5 us
    ppermute x3, waiting for transfers between devices, sum_chips(): lax.ppermute(low[j * rows:(j + 1) * rows], 'expert', swap(devices, 2 * j))  15.8 us
  transfers between devices with their start and end apart: 57, of which 29 were waited for; matrix products, arithmetic and copies ran while one was open for 4% of the time, Pallas kernels for 42%

profile of v3, /device:TPU:8, one launch (start us, length us, event | category | flops | bytes accessed | tf_op | source)
XLA Modules:
  0.0 592.3 jit_solution(8851842145864996662)
XLA Ops:
  4.6 3.0 collective-permute-start.1
  10.1 3.8 route.1
  14.7 5.0 collective-permute-done.1
  30.3 7.4 %collective-permute-done.3.refs_1_ = bf16[384,768]{1,0:T(8,128)(2,1)S(1)} collective-permute-done((bf16[384,768]{1,0:T(8,128)(2,1)S(1)}, bf16[384,768]{1,0:T(8,128)(2,1)S(1)}, u32[]{:S(2)}, u32[]{:S(2)}) %collective-permute-start.3) | collective-permute-done | bytes 589856 | tf_op jit(solution)/shard_map/ppermute | solution.py:215
  38.9 16.6 %collective-permute-done.5.refs_6_ = bf16[384,768]{1,0:T(8,128)(2,1)S(1)} collective-permute-done((bf16[384,768]{1,0:T(8,128)(2,1)S(1)}, bf16[384,768]{1,0:T(8,128)(2,1)S(1)}, u32[]{:S(2)}, u32[]{:S(2)}) %collective-permute-start.5) | collective-permute-done | bytes 589856 | tf_op jit(solution)/shard_map/ppermute | solution.py:774
  58.4 3.9 collective-permute-done.6
  63.8 14.2 %collective-permute-done.9.refs_7_ = bf16[384,768]{1,0:T(8,128)(2,1)S(1)} collective-permute-done((bf16[384,768]{1,0:T(8,128)(2,1)S(1)}, bf16[384,768]{1,0:T(8,128)(2,1)S(1)}, u32[]{:S(2)}, u32[]{:S(2)}) %collective-permute-start.9) | collective-permute-done | bytes 589856 | tf_op jit(solution)/shard_map/ppermute | solution.py:774
  92.0 39.0 %attend.1 = (bf16[2,768,512]{2,1,0:T(8,128)(2,1)}, bf16[2,768,512]{2,1,0:T(8,128)(2,1)}, bf16[2,768,512]{2,1,0:T(8,128)(2,1)}, bf16[2,12,512,512]{3,2,1,0:T(8,12...) custom-call(s32[2]{0:T(128)} %starts_ref.1, ...), custom_call_target="tpu_custom_call" | custom-call | bytes 151200000 | tf_op jit(solution)/shard_map/attend/pallas_call | solution.py:356
  146.5 15.5 %collective-permute-done.16.refs_1_ = bf16[384,768]{1,0:T(8,128)(2,1)S(1)} collective-permute-done((bf16[384,768]{1,0:T(8,128)(2,1)S(1)}, bf16[384,768]{1,0:T(8,128)(2,1)S(1)}, u32[]{:S(2)}, u32[]{:S(2)}) %collective-permute-start.16) | collective-permute-done | bytes 589856 | tf_op jit(solution)/shard_map/ppermute | solution.py:774
  161.9 16.4 %collective-permute-done.17.refs_2_ = bf16[384,768]{1,0:T(8,128)(2,1)S(1)} collective-permute-done((bf16[384,768]{1,0:T(8,128)(2,1)S(1)}, bf16[384,768]{1,0:T(8,128)(2,1)S(1)}, u32[]{:S(2)}, u32[]{:S(2)}) %collective-permute-start.17) | collective-permute-done | bytes 589856 | tf_op jit(solution)/shard_map/ppermute | solution.py:774
  178.3 13.7 %collective-permute-done.18.refs_3_ = bf16[384,768]{1,0:T(8,128)(2,1)S(1)} collective-permute-done((bf16[384,768]{1,0:T(8,128)(2,1)S(1)}, bf16[384,768]{1,0:T(8,128)(2,1)S(1)}, u32[]{:S(2)}, u32[]{:S(2)}) %collective-permute-start.18) | collective-permute-done | bytes 589856 | tf_op jit(solution)/shard_map/ppermute | solution.py:774
  198.9 59.0 %expert.2 = (bf16[2,192,3072]{2,1,0:T(8,128)(2,1)}, bf16[2,192,3072]{2,1,0:T(8,128)(2,1)}, bf16[2,768,768]{2,1,0:T(8,128)(2,1)}, bf16[2,768,768]{2,1,0:T(8,128)(...) custom-call(s32[3]{0:T(128)} %pad_add_fusion.place_ref, ...), custom_call_target="tpu_custom_call" | custom-call | bytes 223200000 | tf_op jit(solution)/shard_map/expert/pallas_call | solution.py:498
  261.5 61.6 %expert.3 = (bf16[2,192,3072]{2,1,0:T(8,128)(2,1)}, bf16[2,192,3072]{2,1,0:T(8,128)(2,1)}, bf16[2,768,768]{2,1,0:T(8,128)(2,1)}, bf16[2,768,768]{2,1,0:T(8,128)(...) custom-call(s32[3]{0:T(128)} %pad_add_fusion.place_ref, ...), custom_call_target="tpu_custom_call" | custom-call | bytes 223200000 | tf_op jit(solution)/shard_map/expert/pallas_call | solution.py:498
  332.6 32.5 %backward.2 = (bf16[512,768]{1,0:T(8,128)(2,1)}, bf16[384,3200]{1,0:T(8,128)(2,1)}, bf16[384,3200]{1,0:T(8,128)(2,1)}) custom-call(s32[1]{0:T(128)} %bitcast.me_ref.refs_0_, bf16[384,768]{1,0:T(8,128)(2,1)} %get-tuple-element.237.refs_1_, bf16[384,768]{1,0:T(8,128)(2,1)} %copy-done.34, bf16[384,768]{1,0:T(8,128)(2,1)} %collective-permute-done.26.refs_3_, ...), custom_call_target="tpu_custom_call" | custom-call | bytes 122400000 | tf_op jit(solution)/shard_map/backward/pallas_call | solution.py:694
  365.0 4.6 collective-permute-done.30.refs_3_
  369.6 13.6 %collective-permute-done.31.refs_4_ = bf16[384,768]{1,0:T(8,128)(2,1)S(1)} collective-permute-done((bf16[384,768]{1,0:T(8,128)(2,1)}, bf16[384,768]{1,0:T(8,128)(2,1)S(1)}, u32[]{:S(2)}, u32[]{:S(2)}) %collective-permute-start.31) | collective-permute-done | bytes 589856 | tf_op jit(solution)/shard_map/ppermute | solution.py:774
  386.9 3.0 add_convert_fusion.1
  398.7 34.9 %backward.3 = (bf16[512,768]{1,0:T(8,128)(2,1)}, bf16[384,3200]{1,0:T(8,128)(2,1)}, bf16[384,3200]{1,0:T(8,128)(2,1)}) custom-call(s32[1]{0:T(128)} %bitcast.me_ref.refs_0_, bf16[384,768]{1,0:T(8,128)(2,1)} %get-tuple-element.271.refs_1_, bf16[384,768]{1,0:T(8,128)(2,1)} %copy-done.31, bf16[384,768]{1,0:T(8,128)(2,1)} %copy-done.32, ...), custom_call_target="tpu_custom_call" | custom-call | bytes 122400000 | tf_op jit(solution)/shard_map/backward/pallas_call | solution.py:694
  433.7 12.3 %collective-permute-done.35.refs_3_ = bf16[384,768]{1,0:T(8,128)(2,1)S(1)} collective-permute-done((bf16[384,768]{1,0:T(8,128)(2,1)S(1)}, bf16[384,768]{1,0:T(8,128)(2,1)S(1)}, u32[]{:S(2)}, u32[]{:S(2)}) %collective-permute-start.35) | collective-permute-done | bytes 589856 | tf_op jit(solution)/shard_map/ppermute | solution.py:774
  448.2 4.9 collective-permute-done.41
  456.7 2.9 collective-permute-start.42
  459.7 22.0 %collective-permute-done.51 = bf16[192,3072]{1,0:T(8,128)(2,1)S(1)} collective-permute-done((bf16[192,3072]{1,0:T(8,128)(2,1)S(1)}, bf16[192,3072]{1,0:T(8,128)(2,1)S(1)}, u32[]{:S(2)}, u32[]{:S(2)}) %collective-permute-start.51) | collective-permute-done | bytes 1179680 | tf_op jit(solution)/shard_map/ppermute | solution.py:529
  484.0 5.1 collective-permute-done.44
  489.6 10.7 %collective-permute-done.43 = bf16[96,3200]{1,0:T(8,128)(2,1)S(1)} collective-permute-done((bf16[96,3200]{1,0:T(8,128)(2,1)S(1)}, bf16[96,3200]{1,0:T(8,128)(2,1)S(1)}, u32[]{:S(2)}, u32[]{:S(2)}) %collective-permute-start.43) | collective-permute-done | bytes 614432 | tf_op jit(solution)/shard_map/ppermute | solution.py:801
  500.6 3.4 collective-permute-start.45
  509.4 8.7 %collective-permute-done.45.refs_1_ = bf16[384,768]{1,0:T(8,128)(2,1)S(1)} collective-permute-done((bf16[384,768]{1,0:T(8,128)(2,1)S(1)}, bf16[384,768]{1,0:T(8,128)(2,1)S(1)}, u32[]{:S(2)}, u32[]{:S(2)}) %collective-permute-start.45) | collective-permute-done | bytes 589856 | tf_op jit(solution)/shard_map/ppermute | solution.py:774
  519.2 26.4 %collective-permute-done.47.refs_3_ = bf16[384,768]{1,0:T(8,128)(2,1)S(1)} collective-permute-done((bf16[384,768]{1,0:T(8,128)(2,1)S(1)}, bf16[384,768]{1,0:T(8,128)(2,1)S(1)}, u32[]{:S(2)}, u32[]{:S(2)}) %collective-permute-start.47) | collective-permute-done | bytes 589856 | tf_op jit(solution)/shard_map/ppermute | solution.py:774
  545.6 9.5 %collective-permute-done.46.refs_2_ = bf16[384,768]{1,0:T(8,128)(2,1)S(1)} collective-permute-done((bf16[384,768]{1,0:T(8,128)(2,1)S(1)}, bf16[384,768]{1,0:T(8,128)(2,1)S(1)}, u32[]{:S(2)}, u32[]{:S(2)}) %collective-permute-start.46) | collective-permute-done | bytes 589856 | tf_op jit(solution)/shard_map/ppermute | solution.py:774
  555.9 9.4 %collective-permute-done.50 = bf16[96,1664]{1,0:T(8,128)(2,1)S(1)} collective-permute-done((bf16[96,1664]{1,0:T(8,128)(2,1)S(1)}, bf16[96,1664]{1,0:T(8,128)(2,1)S(1)}, u32[]{:S(2)}, u32[]{:S(2)}) %collective-permute-start.50) | collective-permute-done | bytes 319520 | tf_op jit(solution)/shard_map/ppermute | solution.py:812
  565.4 4.5 spread.2
  569.8 4.5 spread.3
  583.9 5.2 collective-permute-done.55
  (296 shorter events, 113.3 us)
Async XLA Ops:
  27.7 36.2 %collective-permute-start.8 = (bf16[384,768]{1,0:T(8,128)(2,1)S(1)}, bf16[384,768]{1,0:T(8,128)(2,1)S(1)}, u32[]{:S(2)}, u32[]{:S(2)}) collective-permute-start(bf16[384,768]{1,0:T(8,128)(2,1)S(1)} %get-tuple-element.165), channel_id=1, source_target_pairs={{0,2},{1,3},{2,0},{3,1},{4,6},{5,7},{6,4},{7,5},{8,10},{9,11},{10,... | collective-permute-start | bytes 1769480 | tf_op jit(solution)/shard_map/ppermute | solution.py:774
  29.9 48.2 %collective-permute-start.9 = (bf16[384,768]{1,0:T(8,128)(2,1)S(1)}, bf16[384,768]{1,0:T(8,128)(2,1)S(1)}, u32[]{:S(2)}, u32[]{:S(2)}) collective-permute-start(bf16[384,768]{1,0:T(8,128)(2,1)S(1)} %get-tuple-element.166), channel_id=1, source_target_pairs={{0,6},{1,7},{2,4},{3,5},{4,2},{5,3},{6,0},{7,1},{8,14},{9,15},{10,... | collective-permute-start | bytes 1769480 | tf_op jit(solution)/shard_map/ppermute | solution.py:774
  78.1 52.9 %collective-permute-start.12 = (bf16[384,768]{1,0:T(8,128)(2,1)}, bf16[384,768]{1,0:T(8,128)(2,1)}, u32[]{:S(2)}, u32[]{:S(2)}) collective-permute-start(bf16[384,768]{1,0:T(8,128)(2,1)} %get-tuple-element.180), channel_id=1, source_target_pairs={{0,2},{1,3},{2,0},{3,1},{4,6},{5,7},{6,4},{7,5},{8,10},{9,11},{10,... | collective-permute-start | bytes 1769480 | tf_op jit(solution)/shard_map/ppermute | solution.py:774
  78.1 52.9 %collective-permute-start.13 = (bf16[384,768]{1,0:T(8,128)(2,1)}, bf16[384,768]{1,0:T(8,128)(2,1)}, u32[]{:S(2)}, u32[]{:S(2)}) collective-permute-start(bf16[384,768]{1,0:T(8,128)(2,1)} %get-tuple-element.181), channel_id=1, source_target_pairs={{0,4},{1,5},{2,6},{3,7},{4,0},{5,1},{6,2},{7,3},{8,12},{9,13},{10,... | collective-permute-start | bytes 1769480 | tf_op jit(solution)/shard_map/ppermute | solution.py:774
  79.9 53.4 %collective-permute-start.14 = (bf16[384,768]{1,0:T(8,128)(2,1)}, bf16[384,768]{1,0:T(8,128)(2,1)}, u32[]{:S(2)}, u32[]{:S(2)}) collective-permute-start(bf16[384,768]{1,0:T(8,128)(2,1)} %get-tuple-element.182), channel_id=1, source_target_pairs={{0,6},{1,7},{2,4},{3,5},{4,2},{5,3},{6,0},{7,1},{8,14},{9,15},{10,... | collective-permute-start | bytes 1769480 | tf_op jit(solution)/shard_map/ppermute | solution.py:774
  137.5 40.8 %collective-permute-start.17 = (bf16[384,768]{1,0:T(8,128)(2,1)S(1)}, bf16[384,768]{1,0:T(8,128)(2,1)S(1)}, u32[]{:S(2)}, u32[]{:S(2)}) collective-permute-start(bf16[384,768]{1,0:T(8,128)(2,1)S(1)} %get-tuple-element.191), channel_id=1, source_target_pairs={{0,4},{1,5},{2,6},{3,7},{4,0},{5,1},{6,2},{7,3},{8,12},{9,13},{10,... | collective-permute-start | bytes 1769480 | tf_op jit(solution)/shard_map/ppermute | solution.py:774
  139.3 52.7 %collective-permute-start.18 = (bf16[384,768]{1,0:T(8,128)(2,1)S(1)}, bf16[384,768]{1,0:T(8,128)(2,1)S(1)}, u32[]{:S(2)}, u32[]{:S(2)}) collective-permute-start(bf16[384,768]{1,0:T(8,128)(2,1)S(1)} %get-tuple-element.192), channel_id=1, source_target_pairs={{0,6},{1,7},{2,4},{3,5},{4,2},{5,3},{6,0},{7,1},{8,14},{9,15},{10,... | collective-permute-start | bytes 1769480 | tf_op jit(solution)/shard_map/ppermute | solution.py:774
  141.1 56.7 %collective-permute-start.19 = (bf16[768,768]{1,0:T(8,128)(2,1)S(1)}, bf16[768,768]{1,0:T(8,128)(2,1)S(1)}, u32[]{:S(2)}, u32[]{:S(2)}) collective-permute-start(bf16[768,768]{1,0:T(8,128)(2,1)S(1)} %pad_maximum_fusion.4), channel_id=1, source_target_pairs={{0,1},{1,0},{2,3},{3,2},{4,5},{5,4},{6,7},{7,6},{8,9},{9,8},{10,11... | collective-permute-start | bytes 3538952 | tf_op jit(solution)/shard_map/ppermute | solution.py:789
  192.0 65.9 %collective-permute-start.21 = (bf16[384,768]{1,0:T(8,128)(2,1)}, bf16[384,768]{1,0:T(8,128)(2,1)S(1)}, u32[]{:S(2)}, u32[]{:S(2)}) collective-permute-start(bf16[384,768]{1,0:T(8,128)(2,1)} %get-tuple-element.207), channel_id=1, source_target_pairs={{0,2},{1,3},{2,0},{3,1},{4,6},{5,7},{6,4},{7,5},{8,10},{9,11},{10,... | collective-permute-start | bytes 1769480 | tf_op jit(solution)/shard_map/ppermute | solution.py:774
  192.0 65.9 %collective-permute-start.22 = (bf16[384,768]{1,0:T(8,128)(2,1)}, bf16[384,768]{1,0:T(8,128)(2,1)}, u32[]{:S(2)}, u32[]{:S(2)}) collective-permute-start(bf16[384,768]{1,0:T(8,128)(2,1)} %get-tuple-element.208), channel_id=1, source_target_pairs={{0,4},{1,5},{2,6},{3,7},{4,0},{5,1},{6,2},{7,3},{8,12},{9,13},{10,... | collective-permute-start | bytes 1769480 | tf_op jit(solution)/shard_map/ppermute | solution.py:774
  193.8 64.2 %collective-permute-start.23 = (bf16[384,768]{1,0:T(8,128)(2,1)}, bf16[384,768]{1,0:T(8,128)(2,1)}, u32[]{:S(2)}, u32[]{:S(2)}) collective-permute-start(bf16[384,768]{1,0:T(8,128)(2,1)} %get-tuple-element.209), channel_id=1, source_target_pairs={{0,6},{1,7},{2,4},{3,5},{4,2},{5,3},{6,0},{7,1},{8,14},{9,15},{10,... | collective-permute-start | bytes 1769480 | tf_op jit(solution)/shard_map/ppermute | solution.py:774
  196.6 64.9 %collective-permute-start.24 = (bf16[768,768]{1,0:T(8,128)(2,1)}, bf16[768,768]{1,0:T(8,128)(2,1)}, u32[]{:S(2)}, u32[]{:S(2)}) collective-permute-start(bf16[768,768]{1,0:T(8,128)(2,1)} %pad_maximum_fusion.5), channel_id=1, source_target_pairs={{0,1},{1,0},{2,3},{3,2},{4,5},{5,4},{6,7},{7,6},{8,9},{9,8},{10,11... | collective-permute-start | bytes 3538952 | tf_op jit(solution)/shard_map/ppermute | solution.py:789
  258.0 65.2 %collective-permute-start.25 = (bf16[384,768]{1,0:T(8,128)(2,1)}, bf16[384,768]{1,0:T(8,128)(2,1)S(1)}, u32[]{:S(2)}, u32[]{:S(2)}) collective-permute-start(bf16[384,768]{1,0:T(8,128)(2,1)} %get-tuple-element.233), channel_id=1, source_target_pairs={{0,2},{1,3},{2,0},{3,1},{4,6},{5,7},{6,4},{7,5},{8,10},{9,11},{10,... | collective-permute-start | bytes 1769480 | tf_op jit(solution)/shard_map/ppermute | solution.py:774
  258.9 64.2 %collective-permute-start.26 = (bf16[384,768]{1,0:T(8,128)(2,1)}, bf16[384,768]{1,0:T(8,128)(2,1)}, u32[]{:S(2)}, u32[]{:S(2)}) collective-permute-start(bf16[384,768]{1,0:T(8,128)(2,1)} %get-tuple-element.234), channel_id=1, source_target_pairs={{0,4},{1,5},{2,6},{3,7},{4,0},{5,1},{6,2},{7,3},{8,12},{9,13},{10,... | collective-permute-start | bytes 1769480 | tf_op jit(solution)/shard_map/ppermute | solution.py:774
  259.8 63.4 %collective-permute-start.27 = (bf16[384,768]{1,0:T(8,128)(2,1)}, bf16[384,768]{1,0:T(8,128)(2,1)}, u32[]{:S(2)}, u32[]{:S(2)}) collective-permute-start(bf16[384,768]{1,0:T(8,128)(2,1)} %get-tuple-element.235), channel_id=1, source_target_pairs={{0,6},{1,7},{2,4},{3,5},{4,2},{5,3},{6,0},{7,1},{8,14},{9,15},{10,... | collective-permute-start | bytes 1769480 | tf_op jit(solution)/shard_map/ppermute | solution.py:774
  325.6 58.5 %collective-permute-start.36 = (bf16[2,192,3072]{2,1,0:T(8,128)(2,1)}, bf16[2,192,3072]{2,1,0:T(8,128)(2,1)}, u32[]{:S(2)}, u32[]{:S(2)}) collective-permute-start(bf16[2,192,3072]{2,1,0:T(8,128)(2,1)} %get-tuple-element.266), channel_id=1, source_target_pairs={{0,8},{8,0},{16,24},{24,16},{1,9},{9,1},{17,25},{25,17},{2,10},{10... | collective-permute-start | bytes 7077896 | tf_op jit(solution)/shard_map/ppermute | solution.py:529
  326.2 57.9 %collective-permute-start.37 = (bf16[2,768,768]{2,1,0:T(8,128)(2,1)}, bf16[2,768,768]{2,1,0:T(8,128)(2,1)S(1)}, u32[]{:S(2)}, u32[]{:S(2)}) collective-permute-start(bf16[2,768,768]{2,1,0:T(8,128)(2,1)} %get-tuple-element.267), channel_id=1, source_target_pairs={{0,16},{8,24},{16,0},{24,8},{1,17},{9,25},{17,1},{25,9},{2,18},{10... | collective-permute-start | bytes 7077896 | tf_op jit(solution)/shard_map/ppermute | solution.py:529
  328.5 36.6 %collective-permute-start.29 = (bf16[384,768]{1,0:T(8,128)(2,1)}, bf16[384,768]{1,0:T(8,128)(2,1)S(1)}, u32[]{:S(2)}, u32[]{:S(2)}) collective-permute-start(bf16[384,768]{1,0:T(8,128)(2,1)} %get-tuple-element.242), channel_id=1, source_target_pairs={{0,2},{1,3},{2,0},{3,1},{4,6},{5,7},{6,4},{7,5},{8,10},{9,11},{10,... | collective-permute-start | bytes 1769480 | tf_op jit(solution)/shard_map/ppermute | solution.py:774
  330.2 39.3 %collective-permute-start.30 = (bf16[384,768]{1,0:T(8,128)(2,1)}, bf16[384,768]{1,0:T(8,128)(2,1)S(1)}, u32[]{:S(2)}, u32[]{:S(2)}) collective-permute-start(bf16[384,768]{1,0:T(8,128)(2,1)} %get-tuple-element.243), channel_id=1, source_target_pairs={{0,4},{1,5},{2,6},{3,7},{4,0},{5,1},{6,2},{7,3},{8,12},{9,13},{10,... | collective-permute-start | bytes 1769480 | tf_op jit(solution)/shard_map/ppermute | solution.py:774
  330.3 53.0 %collective-permute-start.31 = (bf16[384,768]{1,0:T(8,128)(2,1)}, bf16[384,768]{1,0:T(8,128)(2,1)S(1)}, u32[]{:S(2)}, u32[]{:S(2)}) collective-permute-start(bf16[384,768]{1,0:T(8,128)(2,1)} %get-tuple-element.244), channel_id=1, source_target_pairs={{0,6},{1,7},{2,4},{3,5},{4,2},{5,3},{6,0},{7,1},{8,14},{9,15},{10,... | collective-permute-start | bytes 1769480 | tf_op jit(solution)/shard_map/ppermute | solution.py:774
  391.1 54.9 %collective-permute-start.39 = (bf16[192,3072]{1,0:T(8,128)(2,1)}, bf16[192,3072]{1,0:T(8,128)(2,1)S(1)}, u32[]{:S(2)}, u32[]{:S(2)}) collective-permute-start(bf16[192,3072]{1,0:T(8,128)(2,1)} %slice_bitcast_fusion.2), channel_id=1, source_target_pairs={{0,16},{8,24},{16,0},{24,8},{1,17},{9,25},{17,1},{25,9},{2,18},{10... | collective-permute-start | bytes 3538952 | tf_op jit(solution)/shard_map/ppermute | solution.py:529
  391.5 42.1 %collective-permute-start.33 = (bf16[384,768]{1,0:T(8,128)(2,1)}, bf16[384,768]{1,0:T(8,128)(2,1)S(1)}, u32[]{:S(2)}, u32[]{:S(2)}) collective-permute-start(bf16[384,768]{1,0:T(8,128)(2,1)} %get-tuple-element.257), channel_id=1, source_target_pairs={{0,2},{1,3},{2,0},{3,1},{4,6},{5,7},{6,4},{7,5},{8,10},{9,11},{10,... | collective-permute-start | bytes 1769480 | tf_op jit(solution)/shard_map/ppermute | solution.py:774
  391.5 42.1 %collective-permute-start.34 = (bf16[384,768]{1,0:T(8,128)(2,1)}, bf16[384,768]{1,0:T(8,128)(2,1)S(1)}, u32[]{:S(2)}, u32[]{:S(2)}) collective-permute-start(bf16[384,768]{1,0:T(8,128)(2,1)} %get-tuple-element.258), channel_id=1, source_target_pairs={{0,4},{1,5},{2,6},{3,7},{4,0},{5,1},{6,2},{7,3},{8,12},{9,13},{10,... | collective-permute-start | bytes 1769480 | tf_op jit(solution)/shard_map/ppermute | solution.py:774
  393.6 52.4 %collective-permute-start.35 = (bf16[384,768]{1,0:T(8,128)(2,1)S(1)}, bf16[384,768]{1,0:T(8,128)(2,1)S(1)}, u32[]{:S(2)}, u32[]{:S(2)}) collective-permute-start(bf16[384,768]{1,0:T(8,128)(2,1)S(1)} %copy-done.52), channel_id=1, source_target_pairs={{0,6},{1,7},{2,4},{3,5},{4,2},{5,3},{6,0},{7,1},{8,14},{9,15},{10,... | collective-permute-start | bytes 1769480 | tf_op jit(solution)/shard_map/ppermute | solution.py:774
  398.1 48.4 %collective-permute-start.40 = (bf16[768,768]{1,0:T(8,128)(2,1)}, bf16[768,768]{1,0:T(8,128)(2,1)}, u32[]{:S(2)}, u32[]{:S(2)}) collective-permute-start(bf16[768,768]{1,0:T(8,128)(2,1)} %slice_bitcast_fusion), channel_id=1, source_target_pairs={{0,8},{8,0},{16,24},{24,16},{1,9},{9,1},{17,25},{25,17},{2,10},{10... | collective-permute-start | bytes 3538952 | tf_op jit(solution)/shard_map/ppermute | solution.py:529
  456.7 43.6 %collective-permute-start.43 = (bf16[96,3200]{1,0:T(8,128)(2,1)S(1)}, bf16[96,3200]{1,0:T(8,128)(2,1)S(1)}, u32[]{:S(2)}, u32[]{:S(2)}) collective-permute-start(bf16[96,3200]{1,0:T(8,128)(2,1)S(1)} %get-tuple-element.336), channel_id=1, source_target_pairs={{0,4},{1,5},{2,6},{3,7},{4,0},{5,1},{6,2},{7,3},{8,12},{9,13},{10,... | collective-permute-start | bytes 1843208 | tf_op jit(solution)/shard_map/ppermute | solution.py:801
  456.7 43.6 %collective-permute-start.42 = (bf16[96,3200]{1,0:T(8,128)(2,1)S(1)}, bf16[96,3200]{1,0:T(8,128)(2,1)S(1)}, u32[]{:S(2)}, u32[]{:S(2)}) collective-permute-start(bf16[96,3200]{1,0:T(8,128)(2,1)S(1)} %get-tuple-element.334), channel_id=1, source_target_pairs={{0,2},{1,3},{2,0},{3,1},{4,6},{5,7},{6,4},{7,5},{8,10},{9,11},{10,... | collective-permute-start | bytes 1843208 | tf_op jit(solution)/shard_map/ppermute | solution.py:801
  483.2 82.2 %collective-permute-start.52 = (bf16[2,192,3072]{2,1,0:T(8,128)(2,1)S(1)}, bf16[2,192,3072]{2,1,0:T(8,128)(2,1)S(1)}, u32[]{:S(2)}, u32[]{:S(2)}) collective-permute-start(bf16[2,192,3072]{2,1,0:T(8,128)(2,1)S(1)} %pad_maximum_fusion), channel_id=1, source_target_pairs={{0,8},{8,0},{16,24},{24,16},{1,9},{9,1},{17,25},{25,17},{2,10},{10... | collective-permute-start | bytes 7077896 | tf_op jit(solution)/shard_map/ppermute | solution.py:529
  489.1 80.7 %collective-permute-start.54 = (bf16[2,768,768]{2,1,0:T(8,128)(2,1)S(1)}, bf16[2,768,768]{2,1,0:T(8,128)(2,1)S(1)}, u32[]{:S(2)}, u32[]{:S(2)}) collective-permute-start(bf16[2,768,768]{2,1,0:T(8,128)(2,1)S(1)} %pad_maximum_fusion.1), channel_id=1, source_target_pairs={{0,16},{8,24},{16,0},{24,8},{1,17},{9,25},{17,1},{25,9},{2,18},{10... | collective-permute-start | bytes 7077896 | tf_op jit(solution)/shard_map/ppermute | solution.py:529
  504.0 41.5 %collective-permute-start.47 = (bf16[384,768]{1,0:T(8,128)(2,1)S(1)}, bf16[384,768]{1,0:T(8,128)(2,1)S(1)}, u32[]{:S(2)}, u32[]{:S(2)}) collective-permute-start(bf16[384,768]{1,0:T(8,128)(2,1)S(1)} %copy-done.50), channel_id=1, source_target_pairs={{0,6},{1,7},{2,4},{3,5},{4,2},{5,3},{6,0},{7,1},{8,14},{9,15},{10,... | collective-permute-start | bytes 1769480 | tf_op jit(solution)/shard_map/ppermute | solution.py:774
  504.6 50.4 %collective-permute-start.46 = (bf16[384,768]{1,0:T(8,128)(2,1)S(1)}, bf16[384,768]{1,0:T(8,128)(2,1)S(1)}, u32[]{:S(2)}, u32[]{:S(2)}) collective-permute-start(bf16[384,768]{1,0:T(8,128)(2,1)S(1)} %copy-done.49), channel_id=1, source_target_pairs={{0,4},{1,5},{2,6},{3,7},{4,0},{5,1},{6,2},{7,3},{8,12},{9,13},{10,... | collective-permute-start | bytes 1769480 | tf_op jit(solution)/shard_map/ppermute | solution.py:774
  518.2 37.6 %collective-permute-start.49 = (bf16[96,1536]{1,0:T(8,128)(2,1)S(1)}, bf16[96,1536]{1,0:T(8,128)(2,1)S(1)}, u32[]{:S(2)}, u32[]{:S(2)}) collective-permute-start(bf16[96,1536]{1,0:T(8,128)(2,1)S(1)} %slice.314), channel_id=1, source_target_pairs={{0,8},{8,0},{16,24},{24,16},{1,9},{9,1},{17,25},{25,17},{2,10},{10... | collective-permute-start | bytes 884744 | tf_op jit(solution)/shard_map/ppermute | solution.py:812
  (84 other events, 1337.8 us)

commit v4 on v3

--- a/solution.py
+++ b/solution.py
@@ -868,8 +868,9 @@
     backs.append(last[blocks:])
     *flat, router_grad = tie(grads, *backs[0][1:])
     away = [trade(flat[1], groups, 1), trade(flat[3], groups, 2)]
-    backs[0] = pass_on(tie(backs[0], last[0]), devices)
-    backs[1] = send(tie(backs[1], *backs[0]), devices)
+    backs[0] = tie(backs[0], last[0])
+    backs[1] = send(tie(backs[1], *backs[0][1:]), devices)
+    backs[0] = pass_on(backs[0], devices)
 
     def run_back(step, prior):
         query, key, value, probs, attended, hidden, _, normed = saved

time: 602 us -> 604 us (level)
  starting transfers between devices: 50.7 us -> 58.1 us
    unnamed x113 -> x111, local copies, waits for them, and re-layouts: 15.4 us -> 15.4 us
  transfers between devices with their start and end apart: 57 -> 57, of which waited for: 29 -> 28; matrix products, arithmetic and copies ran while one was open for 4% -> 5% of each run, Pallas kernels for 42% -> 42%
where the time goes in v4:
time: 604 us; the launch traced here: 594 us
  Pallas kernels  249 us (41%)
  waiting for transfers between devices  233 us (39%)
  starting transfers between devices  58.1 us (10%)
  local copies, waits for them, and re-layouts  32.2 us (5%)
  other arithmetic  20.6 us (3%)
    ppermute x24, waiting for transfers between devices, send(): lax.ppermute(blocks[j], 'expert', swap(devices, 2 * j))  150 us
    pallas_call x2, Pallas kernels, run_expert(): pl.pallas_call(functools.partial(expert_kernel, blocks=blocks, passes=pas...  121 us
    pallas_call x2, Pallas kernels, backward(): pl.pallas_call(functools.partial(back_kernel, blocks=blocks, passes=passe...  67.3 us
    pallas_call x1, Pallas kernels, attend(): pl.pallas_call(functools.partial(attend_kernel, experts=experts), grid=(H...  39 us
    ppermute x24, starting transfers between devices, send(): lax.ppermute(blocks[j], 'expert', swap(devices, 2 * j))  30.4 us
    ppermute x8, waiting for transfers between devices, trade(): return lax.ppermute(value, 'group', swap(groups, mask))  22.2 us
    ppermute x3, waiting for transfers between devices, sum_chips(): lax.ppermute(low[j * rows:(j + 1) * rows], 'expert', swap(devices, 2 * j))  15.6 us
    unnamed x111, local copies, waits for them, and re-layouts  15.4 us
  transfers between devices with their start and end apart: 57, of which 28 were waited for; matrix products, arithmetic and copies ran while one was open for 5% of the time, Pallas kernels for 42%

profile of v4, /device:TPU:8, one launch (start us, length us, event | category | flops | bytes accessed | tf_op | source)
XLA Modules:
  0.0 594.2 jit_solution(2120700502645777019)
XLA Ops:
  4.6 3.0 collective-permute-start.1
  10.1 3.8 route.1
  14.7 5.0 collective-permute-done.1
  30.3 7.4 %collective-permute-done.3.refs_1_ = bf16[384,768]{1,0:T(8,128)(2,1)S(1)} collective-permute-done((bf16[384,768]{1,0:T(8,128)(2,1)S(1)}, bf16[384,768]{1,0:T(8,128)(2,1)S(1)}, u32[]{:S(2)}, u32[]{:S(2)}) %collective-permute-start.3) | collective-permute-done | bytes 589856 | tf_op jit(solution)/shard_map/ppermute | solution.py:215
  38.9 16.6 %collective-permute-done.5.refs_6_ = bf16[384,768]{1,0:T(8,128)(2,1)S(1)} collective-permute-done((bf16[384,768]{1,0:T(8,128)(2,1)S(1)}, bf16[384,768]{1,0:T(8,128)(2,1)S(1)}, u32[]{:S(2)}, u32[]{:S(2)}) %collective-permute-start.5) | collective-permute-done | bytes 589856 | tf_op jit(solution)/shard_map/ppermute | solution.py:774
  58.4 3.9 collective-permute-done.6
  63.8 14.2 %collective-permute-done.9.refs_7_ = bf16[384,768]{1,0:T(8,128)(2,1)S(1)} collective-permute-done((bf16[384,768]{1,0:T(8,128)(2,1)S(1)}, bf16[384,768]{1,0:T(8,128)(2,1)S(1)}, u32[]{:S(2)}, u32[]{:S(2)}) %collective-permute-start.9) | collective-permute-done | bytes 589856 | tf_op jit(solution)/shard_map/ppermute | solution.py:774
  92.0 39.0 %attend.1 = (bf16[2,768,512]{2,1,0:T(8,128)(2,1)}, bf16[2,768,512]{2,1,0:T(8,128)(2,1)}, bf16[2,768,512]{2,1,0:T(8,128)(2,1)}, bf16[2,12,512,512]{3,2,1,0:T(8,12...) custom-call(s32[2]{0:T(128)} %starts_ref.1, ...), custom_call_target="tpu_custom_call" | custom-call | bytes 151200000 | tf_op jit(solution)/shard_map/attend/pallas_call | solution.py:356
  146.5 15.5 %collective-permute-done.16.refs_1_ = bf16[384,768]{1,0:T(8,128)(2,1)S(1)} collective-permute-done((bf16[384,768]{1,0:T(8,128)(2,1)S(1)}, bf16[384,768]{1,0:T(8,128)(2,1)S(1)}, u32[]{:S(2)}, u32[]{:S(2)}) %collective-permute-start.16) | collective-permute-done | bytes 589856 | tf_op jit(solution)/shard_map/ppermute | solution.py:774
  161.9 16.4 %collective-permute-done.17.refs_2_ = bf16[384,768]{1,0:T(8,128)(2,1)S(1)} collective-permute-done((bf16[384,768]{1,0:T(8,128)(2,1)S(1)}, bf16[384,768]{1,0:T(8,128)(2,1)S(1)}, u32[]{:S(2)}, u32[]{:S(2)}) %collective-permute-start.17) | collective-permute-done | bytes 589856 | tf_op jit(solution)/shard_map/ppermute | solution.py:774
  178.3 13.7 %collective-permute-done.18.refs_3_ = bf16[384,768]{1,0:T(8,128)(2,1)S(1)} collective-permute-done((bf16[384,768]{1,0:T(8,128)(2,1)S(1)}, bf16[384,768]{1,0:T(8,128)(2,1)S(1)}, u32[]{:S(2)}, u32[]{:S(2)}) %collective-permute-start.18) | collective-permute-done | bytes 589856 | tf_op jit(solution)/shard_map/ppermute | solution.py:774
  199.0 59.0 %expert.2 = (bf16[2,192,3072]{2,1,0:T(8,128)(2,1)}, bf16[2,192,3072]{2,1,0:T(8,128)(2,1)}, bf16[2,768,768]{2,1,0:T(8,128)(2,1)}, bf16[2,768,768]{2,1,0:T(8,128)(...) custom-call(s32[3]{0:T(128)} %pad_add_fusion.place_ref, ...), custom_call_target="tpu_custom_call" | custom-call | bytes 223200000 | tf_op jit(solution)/shard_map/expert/pallas_call | solution.py:498
  261.6 61.6 %expert.3 = (bf16[2,192,3072]{2,1,0:T(8,128)(2,1)}, bf16[2,192,3072]{2,1,0:T(8,128)(2,1)}, bf16[2,768,768]{2,1,0:T(8,128)(2,1)}, bf16[2,768,768]{2,1,0:T(8,128)(...) custom-call(s32[3]{0:T(128)} %pad_add_fusion.place_ref, ...), custom_call_target="tpu_custom_call" | custom-call | bytes 223200000 | tf_op jit(solution)/shard_map/expert/pallas_call | solution.py:498
  330.8 32.5 %backward.2 = (bf16[512,768]{1,0:T(8,128)(2,1)}, bf16[384,3200]{1,0:T(8,128)(2,1)}, bf16[384,3200]{1,0:T(8,128)(2,1)}) custom-call(s32[1]{0:T(128)} %bitcast.me_ref.refs_0_, bf16[384,768]{1,0:T(8,128)(2,1)} %get-tuple-element.244.refs_1_, bf16[384,768]{1,0:T(8,128)(2,1)} %copy-done.33, bf16[384,768]{1,0:T(8,128)(2,1)} %collective-permute-done.26.refs_3_, ...), custom_call_target="tpu_custom_call" | custom-call | bytes 122400000 | tf_op jit(solution)/shard_map/backward/pallas_call | solution.py:694
  363.3 4.5 collective-permute-done.29.refs_3_
  367.9 13.4 %collective-permute-done.30.refs_4_ = bf16[384,768]{1,0:T(8,128)(2,1)S(1)} collective-permute-done((bf16[384,768]{1,0:T(8,128)(2,1)}, bf16[384,768]{1,0:T(8,128)(2,1)S(1)}, u32[]{:S(2)}, u32[]{:S(2)}) %collective-permute-start.30) | collective-permute-done | bytes 589856 | tf_op jit(solution)/shard_map/ppermute | solution.py:774
  401.3 34.8 %backward.3 = (bf16[512,768]{1,0:T(8,128)(2,1)}, bf16[384,3200]{1,0:T(8,128)(2,1)}, bf16[384,3200]{1,0:T(8,128)(2,1)}) custom-call(s32[1]{0:T(128)} %bitcast.me_ref.refs_0_, bf16[384,768]{1,0:T(8,128)(2,1)} %get-tuple-element.271.refs_1_, bf16[384,768]{1,0:T(8,128)(2,1)} %copy-done.30, bf16[384,768]{1,0:T(8,128)(2,1)} %copy-done.31, ...), custom_call_target="tpu_custom_call" | custom-call | bytes 122400000 | tf_op jit(solution)/shard_map/backward/pallas_call | solution.py:694
  436.2 9.9 %collective-permute-done.35.refs_3_ = bf16[384,768]{1,0:T(8,128)(2,1)S(1)} collective-permute-done((bf16[384,768]{1,0:T(8,128)(2,1)S(1)}, bf16[384,768]{1,0:T(8,128)(2,1)S(1)}, u32[]{:S(2)}, u32[]{:S(2)}) %collective-permute-start.35) | collective-permute-done | bytes 589856 | tf_op jit(solution)/shard_map/ppermute | solution.py:774
  448.4 4.9 collective-permute-done.41
  456.8 2.9 collective-permute-start.42
  459.8 22.1 %collective-permute-done.51 = bf16[192,3072]{1,0:T(8,128)(2,1)S(1)} collective-permute-done((bf16[192,3072]{1,0:T(8,128)(2,1)S(1)}, bf16[192,3072]{1,0:T(8,128)(2,1)S(1)}, u32[]{:S(2)}, u32[]{:S(2)}) %collective-permute-start.51) | collective-permute-done | bytes 1179680 | tf_op jit(solution)/shard_map/ppermute | solution.py:529
  484.0 6.0 %collective-permute-done.44 = bf16[96,3200]{1,0:T(8,128)(2,1)S(1)} collective-permute-done((bf16[96,3200]{1,0:T(8,128)(2,1)S(1)}, bf16[96,3200]{1,0:T(8,128)(2,1)S(1)}, u32[]{:S(2)}, u32[]{:S(2)}) %collective-permute-start.44) | collective-permute-done | bytes 614432 | tf_op jit(solution)/shard_map/ppermute | solution.py:801
  491.5 9.6 %collective-permute-done.43 = bf16[96,3200]{1,0:T(8,128)(2,1)S(1)} collective-permute-done((bf16[96,3200]{1,0:T(8,128)(2,1)S(1)}, bf16[96,3200]{1,0:T(8,128)(2,1)S(1)}, u32[]{:S(2)}, u32[]{:S(2)}) %collective-permute-start.43) | collective-permute-done | bytes 614432 | tf_op jit(solution)/shard_map/ppermute | solution.py:801
  501.4 3.4 collective-permute-start.45
  510.3 8.8 %collective-permute-done.45.refs_1_ = bf16[384,768]{1,0:T(8,128)(2,1)S(1)} collective-permute-done((bf16[384,768]{1,0:T(8,128)(2,1)S(1)}, bf16[384,768]{1,0:T(8,128)(2,1)S(1)}, u32[]{:S(2)}, u32[]{:S(2)}) %collective-permute-start.45) | collective-permute-done | bytes 589856 | tf_op jit(solution)/shard_map/ppermute | solution.py:774
  520.7 25.7 %collective-permute-done.47.refs_3_ = bf16[384,768]{1,0:T(8,128)(2,1)S(1)} collective-permute-done((bf16[384,768]{1,0:T(8,128)(2,1)S(1)}, bf16[384,768]{1,0:T(8,128)(2,1)S(1)}, u32[]{:S(2)}, u32[]{:S(2)}) %collective-permute-start.47) | collective-permute-done | bytes 589856 | tf_op jit(solution)/shard_map/ppermute | solution.py:774
  546.4 9.4 %collective-permute-done.46.refs_2_ = bf16[384,768]{1,0:T(8,128)(2,1)S(1)} collective-permute-done((bf16[384,768]{1,0:T(8,128)(2,1)S(1)}, bf16[384,768]{1,0:T(8,128)(2,1)S(1)}, u32[]{:S(2)}, u32[]{:S(2)}) %collective-permute-start.46) | collective-permute-done | bytes 589856 | tf_op jit(solution)/shard_map/ppermute | solution.py:774
  557.8 8.3 %collective-permute-done.50 = bf16[96,1664]{1,0:T(8,128)(2,1)S(1)} collective-permute-done((bf16[96,1664]{1,0:T(8,128)(2,1)S(1)}, bf16[96,1664]{1,0:T(8,128)(2,1)S(1)}, u32[]{:S(2)}, u32[]{:S(2)}) %collective-permute-start.50) | collective-permute-done | bytes 319520 | tf_op jit(solution)/shard_map/ppermute | solution.py:812
  566.2 4.5 spread.2
  570.7 4.5 spread.3
  578.0 2.9 combine.3
  584.7 6.3 %collective-permute-done.55 = bf16[96,1664]{1,0:T(8,128)(2,1)S(1)} collective-permute-done((bf16[96,1664]{1,0:T(8,128)(2,1)S(1)}, bf16[96,1664]{1,0:T(8,128)(2,1)S(1)}, u32[]{:S(2)}, u32[]{:S(2)}) %collective-permute-start.55) | collective-permute-done | bytes 319520 | tf_op jit(solution)/shard_map/ppermute | solution.py:812
  (294 shorter events, 119.0 us)
Async XLA Ops:
  27.7 36.2 %collective-permute-start.8 = (bf16[384,768]{1,0:T(8,128)(2,1)S(1)}, bf16[384,768]{1,0:T(8,128)(2,1)S(1)}, u32[]{:S(2)}, u32[]{:S(2)}) collective-permute-start(bf16[384,768]{1,0:T(8,128)(2,1)S(1)} %get-tuple-element.165), channel_id=1, source_target_pairs={{0,2},{1,3},{2,0},{3,1},{4,6},{5,7},{6,4},{7,5},{8,10},{9,11},{10,... | collective-permute-start | bytes 1769480 | tf_op jit(solution)/shard_map/ppermute | solution.py:774
  29.9 48.2 %collective-permute-start.9 = (bf16[384,768]{1,0:T(8,128)(2,1)S(1)}, bf16[384,768]{1,0:T(8,128)(2,1)S(1)}, u32[]{:S(2)}, u32[]{:S(2)}) collective-permute-start(bf16[384,768]{1,0:T(8,128)(2,1)S(1)} %get-tuple-element.166), channel_id=1, source_target_pairs={{0,6},{1,7},{2,4},{3,5},{4,2},{5,3},{6,0},{7,1},{8,14},{9,15},{10,... | collective-permute-start | bytes 1769480 | tf_op jit(solution)/shard_map/ppermute | solution.py:774
  78.1 52.9 %collective-permute-start.12 = (bf16[384,768]{1,0:T(8,128)(2,1)}, bf16[384,768]{1,0:T(8,128)(2,1)}, u32[]{:S(2)}, u32[]{:S(2)}) collective-permute-start(bf16[384,768]{1,0:T(8,128)(2,1)} %get-tuple-element.180), channel_id=1, source_target_pairs={{0,2},{1,3},{2,0},{3,1},{4,6},{5,7},{6,4},{7,5},{8,10},{9,11},{10,... | collective-permute-start | bytes 1769480 | tf_op jit(solution)/shard_map/ppermute | solution.py:774
  78.1 52.9 %collective-permute-start.13 = (bf16[384,768]{1,0:T(8,128)(2,1)}, bf16[384,768]{1,0:T(8,128)(2,1)}, u32[]{:S(2)}, u32[]{:S(2)}) collective-permute-start(bf16[384,768]{1,0:T(8,128)(2,1)} %get-tuple-element.181), channel_id=1, source_target_pairs={{0,4},{1,5},{2,6},{3,7},{4,0},{5,1},{6,2},{7,3},{8,12},{9,13},{10,... | collective-permute-start | bytes 1769480 | tf_op jit(solution)/shard_map/ppermute | solution.py:774
  79.9 53.4 %collective-permute-start.14 = (bf16[384,768]{1,0:T(8,128)(2,1)}, bf16[384,768]{1,0:T(8,128)(2,1)}, u32[]{:S(2)}, u32[]{:S(2)}) collective-permute-start(bf16[384,768]{1,0:T(8,128)(2,1)} %get-tuple-element.182), channel_id=1, source_target_pairs={{0,6},{1,7},{2,4},{3,5},{4,2},{5,3},{6,0},{7,1},{8,14},{9,15},{10,... | collective-permute-start | bytes 1769480 | tf_op jit(solution)/shard_map/ppermute | solution.py:774
  137.5 40.8 %collective-permute-start.17 = (bf16[384,768]{1,0:T(8,128)(2,1)S(1)}, bf16[384,768]{1,0:T(8,128)(2,1)S(1)}, u32[]{:S(2)}, u32[]{:S(2)}) collective-permute-start(bf16[384,768]{1,0:T(8,128)(2,1)S(1)} %get-tuple-element.191), channel_id=1, source_target_pairs={{0,4},{1,5},{2,6},{3,7},{4,0},{5,1},{6,2},{7,3},{8,12},{9,13},{10,... | collective-permute-start | bytes 1769480 | tf_op jit(solution)/shard_map/ppermute | solution.py:774
  139.3 52.7 %collective-permute-start.18 = (bf16[384,768]{1,0:T(8,128)(2,1)S(1)}, bf16[384,768]{1,0:T(8,128)(2,1)S(1)}, u32[]{:S(2)}, u32[]{:S(2)}) collective-permute-start(bf16[384,768]{1,0:T(8,128)(2,1)S(1)} %get-tuple-element.192), channel_id=1, source_target_pairs={{0,6},{1,7},{2,4},{3,5},{4,2},{5,3},{6,0},{7,1},{8,14},{9,15},{10,... | collective-permute-start | bytes 1769480 | tf_op jit(solution)/shard_map/ppermute | solution.py:774
  141.1 56.8 %collective-permute-start.19 = (bf16[768,768]{1,0:T(8,128)(2,1)S(1)}, bf16[768,768]{1,0:T(8,128)(2,1)S(1)}, u32[]{:S(2)}, u32[]{:S(2)}) collective-permute-start(bf16[768,768]{1,0:T(8,128)(2,1)S(1)} %pad_maximum_fusion.4), channel_id=1, source_target_pairs={{0,1},{1,0},{2,3},{3,2},{4,5},{5,4},{6,7},{7,6},{8,9},{9,8},{10,11... | collective-permute-start | bytes 3538952 | tf_op jit(solution)/shard_map/ppermute | solution.py:789
  192.0 66.0 %collective-permute-start.21 = (bf16[384,768]{1,0:T(8,128)(2,1)}, bf16[384,768]{1,0:T(8,128)(2,1)S(1)}, u32[]{:S(2)}, u32[]{:S(2)}) collective-permute-start(bf16[384,768]{1,0:T(8,128)(2,1)} %get-tuple-element.207), channel_id=1, source_target_pairs={{0,2},{1,3},{2,0},{3,1},{4,6},{5,7},{6,4},{7,5},{8,10},{9,11},{10,... | collective-permute-start | bytes 1769480 | tf_op jit(solution)/shard_map/ppermute | solution.py:774
  192.0 66.0 %collective-permute-start.22 = (bf16[384,768]{1,0:T(8,128)(2,1)}, bf16[384,768]{1,0:T(8,128)(2,1)}, u32[]{:S(2)}, u32[]{:S(2)}) collective-permute-start(bf16[384,768]{1,0:T(8,128)(2,1)} %get-tuple-element.208), channel_id=1, source_target_pairs={{0,4},{1,5},{2,6},{3,7},{4,0},{5,1},{6,2},{7,3},{8,12},{9,13},{10,... | collective-permute-start | bytes 1769480 | tf_op jit(solution)/shard_map/ppermute | solution.py:774
  193.8 64.2 %collective-permute-start.23 = (bf16[384,768]{1,0:T(8,128)(2,1)}, bf16[384,768]{1,0:T(8,128)(2,1)}, u32[]{:S(2)}, u32[]{:S(2)}) collective-permute-start(bf16[384,768]{1,0:T(8,128)(2,1)} %get-tuple-element.209), channel_id=1, source_target_pairs={{0,6},{1,7},{2,4},{3,5},{4,2},{5,3},{6,0},{7,1},{8,14},{9,15},{10,... | collective-permute-start | bytes 1769480 | tf_op jit(solution)/shard_map/ppermute | solution.py:774
  196.7 64.9 %collective-permute-start.24 = (bf16[768,768]{1,0:T(8,128)(2,1)}, bf16[768,768]{1,0:T(8,128)(2,1)}, u32[]{:S(2)}, u32[]{:S(2)}) collective-permute-start(bf16[768,768]{1,0:T(8,128)(2,1)} %pad_maximum_fusion.5), channel_id=1, source_target_pairs={{0,1},{1,0},{2,3},{3,2},{4,5},{5,4},{6,7},{7,6},{8,9},{9,8},{10,11... | collective-permute-start | bytes 3538952 | tf_op jit(solution)/shard_map/ppermute | solution.py:789
  258.0 65.2 %collective-permute-start.25 = (bf16[384,768]{1,0:T(8,128)(2,1)}, bf16[384,768]{1,0:T(8,128)(2,1)S(1)}, u32[]{:S(2)}, u32[]{:S(2)}) collective-permute-start(bf16[384,768]{1,0:T(8,128)(2,1)} %get-tuple-element.233), channel_id=1, source_target_pairs={{0,2},{1,3},{2,0},{3,1},{4,6},{5,7},{6,4},{7,5},{8,10},{9,11},{10,... | collective-permute-start | bytes 1769480 | tf_op jit(solution)/shard_map/ppermute | solution.py:774
  259.0 64.2 %collective-permute-start.26 = (bf16[384,768]{1,0:T(8,128)(2,1)}, bf16[384,768]{1,0:T(8,128)(2,1)}, u32[]{:S(2)}, u32[]{:S(2)}) collective-permute-start(bf16[384,768]{1,0:T(8,128)(2,1)} %get-tuple-element.234), channel_id=1, source_target_pairs={{0,4},{1,5},{2,6},{3,7},{4,0},{5,1},{6,2},{7,3},{8,12},{9,13},{10,... | collective-permute-start | bytes 1769480 | tf_op jit(solution)/shard_map/ppermute | solution.py:774
  259.9 63.3 %collective-permute-start.27 = (bf16[384,768]{1,0:T(8,128)(2,1)}, bf16[384,768]{1,0:T(8,128)(2,1)}, u32[]{:S(2)}, u32[]{:S(2)}) collective-permute-start(bf16[384,768]{1,0:T(8,128)(2,1)} %get-tuple-element.235), channel_id=1, source_target_pairs={{0,6},{1,7},{2,4},{3,5},{4,2},{5,3},{6,0},{7,1},{8,14},{9,15},{10,... | collective-permute-start | bytes 1769480 | tf_op jit(solution)/shard_map/ppermute | solution.py:774
  325.6 59.3 %collective-permute-start.36 = (bf16[2,192,3072]{2,1,0:T(8,128)(2,1)}, bf16[2,192,3072]{2,1,0:T(8,128)(2,1)S(1)}, u32[]{:S(2)}, u32[]{:S(2)}) collective-permute-start(bf16[2,192,3072]{2,1,0:T(8,128)(2,1)} %get-tuple-element.266), channel_id=1, source_target_pairs={{0,8},{8,0},{16,24},{24,16},{1,9},{9,1},{17,25},{25,17},{2,10},{10... | collective-permute-start | bytes 7077896 | tf_op jit(solution)/shard_map/ppermute | solution.py:529
  326.2 60.1 %collective-permute-start.37 = (bf16[2,768,768]{2,1,0:T(8,128)(2,1)}, bf16[2,768,768]{2,1,0:T(8,128)(2,1)}, u32[]{:S(2)}, u32[]{:S(2)}) collective-permute-start(bf16[2,768,768]{2,1,0:T(8,128)(2,1)} %get-tuple-element.267), channel_id=1, source_target_pairs={{0,16},{8,24},{16,0},{24,8},{1,17},{9,25},{17,1},{25,9},{2,18},{10... | collective-permute-start | bytes 7077896 | tf_op jit(solution)/shard_map/ppermute | solution.py:529
  326.7 36.6 %collective-permute-start.28 = (bf16[384,768]{1,0:T(8,128)(2,1)}, bf16[384,768]{1,0:T(8,128)(2,1)S(1)}, u32[]{:S(2)}, u32[]{:S(2)}) collective-permute-start(bf16[384,768]{1,0:T(8,128)(2,1)} %get-tuple-element.241), channel_id=1, source_target_pairs={{0,2},{1,3},{2,0},{3,1},{4,6},{5,7},{6,4},{7,5},{8,10},{9,11},{10,... | collective-permute-start | bytes 1769480 | tf_op jit(solution)/shard_map/ppermute | solution.py:774
  328.5 39.3 %collective-permute-start.29 = (bf16[384,768]{1,0:T(8,128)(2,1)}, bf16[384,768]{1,0:T(8,128)(2,1)S(1)}, u32[]{:S(2)}, u32[]{:S(2)}) collective-permute-start(bf16[384,768]{1,0:T(8,128)(2,1)} %get-tuple-element.242), channel_id=1, source_target_pairs={{0,4},{1,5},{2,6},{3,7},{4,0},{5,1},{6,2},{7,3},{8,12},{9,13},{10,... | collective-permute-start | bytes 1769480 | tf_op jit(solution)/shard_map/ppermute | solution.py:774
  328.5 52.7 %collective-permute-start.30 = (bf16[384,768]{1,0:T(8,128)(2,1)}, bf16[384,768]{1,0:T(8,128)(2,1)S(1)}, u32[]{:S(2)}, u32[]{:S(2)}) collective-permute-start(bf16[384,768]{1,0:T(8,128)(2,1)} %get-tuple-element.243), channel_id=1, source_target_pairs={{0,6},{1,7},{2,4},{3,5},{4,2},{5,3},{6,0},{7,1},{8,14},{9,15},{10,... | collective-permute-start | bytes 1769480 | tf_op jit(solution)/shard_map/ppermute | solution.py:774
  390.1 56.0 %collective-permute-start.39 = (bf16[192,3072]{1,0:T(8,128)(2,1)}, bf16[192,3072]{1,0:T(8,128)(2,1)S(1)}, u32[]{:S(2)}, u32[]{:S(2)}) collective-permute-start(bf16[192,3072]{1,0:T(8,128)(2,1)} %slice_bitcast_fusion.2), channel_id=1, source_target_pairs={{0,16},{8,24},{16,0},{24,8},{1,17},{9,25},{17,1},{25,9},{2,18},{10... | collective-permute-start | bytes 3538952 | tf_op jit(solution)/shard_map/ppermute | solution.py:529
  391.7 44.5 %collective-permute-start.33 = (bf16[384,768]{1,0:T(8,128)(2,1)}, bf16[384,768]{1,0:T(8,128)(2,1)S(1)}, u32[]{:S(2)}, u32[]{:S(2)}) collective-permute-start(bf16[384,768]{1,0:T(8,128)(2,1)} %get-tuple-element.257), channel_id=1, source_target_pairs={{0,2},{1,3},{2,0},{3,1},{4,6},{5,7},{6,4},{7,5},{8,10},{9,11},{10,... | collective-permute-start | bytes 1769480 | tf_op jit(solution)/shard_map/ppermute | solution.py:774
  391.7 44.5 %collective-permute-start.34 = (bf16[384,768]{1,0:T(8,128)(2,1)}, bf16[384,768]{1,0:T(8,128)(2,1)S(1)}, u32[]{:S(2)}, u32[]{:S(2)}) collective-permute-start(bf16[384,768]{1,0:T(8,128)(2,1)} %get-tuple-element.258), channel_id=1, source_target_pairs={{0,4},{1,5},{2,6},{3,7},{4,0},{5,1},{6,2},{7,3},{8,12},{9,13},{10,... | collective-permute-start | bytes 1769480 | tf_op jit(solution)/shard_map/ppermute | solution.py:774
  393.7 52.4 %collective-permute-start.35 = (bf16[384,768]{1,0:T(8,128)(2,1)S(1)}, bf16[384,768]{1,0:T(8,128)(2,1)S(1)}, u32[]{:S(2)}, u32[]{:S(2)}) collective-permute-start(bf16[384,768]{1,0:T(8,128)(2,1)S(1)} %copy-done.51), channel_id=1, source_target_pairs={{0,6},{1,7},{2,4},{3,5},{4,2},{5,3},{6,0},{7,1},{8,14},{9,15},{10,... | collective-permute-start | bytes 1769480 | tf_op jit(solution)/shard_map/ppermute | solution.py:774
  399.9 46.7 %collective-permute-start.40 = (bf16[768,768]{1,0:T(8,128)(2,1)}, bf16[768,768]{1,0:T(8,128)(2,1)}, u32[]{:S(2)}, u32[]{:S(2)}) collective-permute-start(bf16[768,768]{1,0:T(8,128)(2,1)} %slice_bitcast_fusion), channel_id=1, source_target_pairs={{0,8},{8,0},{16,24},{24,16},{1,9},{9,1},{17,25},{25,17},{2,10},{10... | collective-permute-start | bytes 3538952 | tf_op jit(solution)/shard_map/ppermute | solution.py:529
  456.8 44.4 %collective-permute-start.43 = (bf16[96,3200]{1,0:T(8,128)(2,1)S(1)}, bf16[96,3200]{1,0:T(8,128)(2,1)S(1)}, u32[]{:S(2)}, u32[]{:S(2)}) collective-permute-start(bf16[96,3200]{1,0:T(8,128)(2,1)S(1)} %get-tuple-element.336), channel_id=1, source_target_pairs={{0,4},{1,5},{2,6},{3,7},{4,0},{5,1},{6,2},{7,3},{8,12},{9,13},{10,... | collective-permute-start | bytes 1843208 | tf_op jit(solution)/shard_map/ppermute | solution.py:801
  456.8 44.4 %collective-permute-start.42 = (bf16[96,3200]{1,0:T(8,128)(2,1)S(1)}, bf16[96,3200]{1,0:T(8,128)(2,1)S(1)}, u32[]{:S(2)}, u32[]{:S(2)}) collective-permute-start(bf16[96,3200]{1,0:T(8,128)(2,1)S(1)} %get-tuple-element.334), channel_id=1, source_target_pairs={{0,2},{1,3},{2,0},{3,1},{4,6},{5,7},{6,4},{7,5},{8,10},{9,11},{10,... | collective-permute-start | bytes 1843208 | tf_op jit(solution)/shard_map/ppermute | solution.py:801
  482.2 84.0 %collective-permute-start.52 = (bf16[2,192,3072]{2,1,0:T(8,128)(2,1)S(1)}, bf16[2,192,3072]{2,1,0:T(8,128)(2,1)S(1)}, u32[]{:S(2)}, u32[]{:S(2)}) collective-permute-start(bf16[2,192,3072]{2,1,0:T(8,128)(2,1)S(1)} %pad_maximum_fusion), channel_id=1, source_target_pairs={{0,8},{8,0},{16,24},{24,16},{1,9},{9,1},{17,25},{25,17},{2,10},{10... | collective-permute-start | bytes 7077896 | tf_op jit(solution)/shard_map/ppermute | solution.py:529
  490.0 80.7 %collective-permute-start.54 = (bf16[2,768,768]{2,1,0:T(8,128)(2,1)S(1)}, bf16[2,768,768]{2,1,0:T(8,128)(2,1)S(1)}, u32[]{:S(2)}, u32[]{:S(2)}) collective-permute-start(bf16[2,768,768]{2,1,0:T(8,128)(2,1)S(1)} %pad_maximum_fusion.1), channel_id=1, source_target_pairs={{0,16},{8,24},{16,0},{24,8},{1,17},{9,25},{17,1},{25,9},{2,18},{10... | collective-permute-start | bytes 7077896 | tf_op jit(solution)/shard_map/ppermute | solution.py:529
  504.9 41.5 %collective-permute-start.47 = (bf16[384,768]{1,0:T(8,128)(2,1)S(1)}, bf16[384,768]{1,0:T(8,128)(2,1)S(1)}, u32[]{:S(2)}, u32[]{:S(2)}) collective-permute-start(bf16[384,768]{1,0:T(8,128)(2,1)S(1)} %copy-done.49), channel_id=1, source_target_pairs={{0,6},{1,7},{2,4},{3,5},{4,2},{5,3},{6,0},{7,1},{8,14},{9,15},{10,... | collective-permute-start | bytes 1769480 | tf_op jit(solution)/shard_map/ppermute | solution.py:774
  505.5 50.4 %collective-permute-start.46 = (bf16[384,768]{1,0:T(8,128)(2,1)S(1)}, bf16[384,768]{1,0:T(8,128)(2,1)S(1)}, u32[]{:S(2)}, u32[]{:S(2)}) collective-permute-start(bf16[384,768]{1,0:T(8,128)(2,1)S(1)} %copy-done.48), channel_id=1, source_target_pairs={{0,4},{1,5},{2,6},{3,7},{4,0},{5,1},{6,2},{7,3},{8,12},{9,13},{10,... | collective-permute-start | bytes 1769480 | tf_op jit(solution)/shard_map/ppermute | solution.py:774
  519.1 38.7 %collective-permute-start.49 = (bf16[96,1536]{1,0:T(8,128)(2,1)S(1)}, bf16[96,1536]{1,0:T(8,128)(2,1)S(1)}, u32[]{:S(2)}, u32[]{:S(2)}) collective-permute-start(bf16[96,1536]{1,0:T(8,128)(2,1)S(1)} %slice.314), channel_id=1, source_target_pairs={{0,8},{8,0},{16,24},{24,16},{1,9},{9,1},{17,25},{25,17},{2,10},{10... | collective-permute-start | bytes 884744 | tf_op jit(solution)/shard_map/ppermute | solution.py:812
  (83 other events, 1336.0 us)
